TPU v7x, 512 devices: a whole 4x4x16 slice. The times are simulated.
512 devices in a mesh: pool: 2 (over z_hi), grp: 32 (over x, y, core), tp: 8 (over z_lo).
Axes of the slice: x: 4, y: 4, z: 16 (z_hi: 2, z_lo: 8; z = z_hi * 8 + z_lo), core: 2. Of those that a mesh axis runs over, the one named last changes fastest.
Arguments:
- prompt_states: bfloat16 [32768, 5120], P(('pool', 'grp'), 'tp'), may hold values from -6 to 6
- prompt_lengths: int32 [64, 32], replicated, may hold values from 1 to 16
- prompt_target: int32 [64, 32, 1], replicated, may hold values from 0 to 31; in each aligned block of 32 rows (0 to 31, 32 to 63, ..., all dimensions but the last counted through in order) at most 2 rows name the same one
- prompt_query: bfloat16 [2048, 4, 8192], P(('pool', 'grp'), None, 'tp'), may hold values from -360 to 360
- prompt_next: bfloat16 [2048, 4, 5120], P(('pool', 'grp'), None, 'tp'), may hold values from -6 to 6
- key_weight: bfloat16 [5120, 1024], P(None, 'tp'), may hold values from -0.078125 to 0.078125
- value_weight: bfloat16 [5120, 1024], P(None, 'tp'), may hold values from -0.078125 to 0.078125
- key_gain: float32 [128], replicated, may hold values from 0.1 to 1.9
- seq_query: bfloat16 [256, 4, 8192], P(('pool', 'grp'), None, 'tp'), may hold values from -360 to 360
- seq_next: bfloat16 [256, 4, 5120], P(('pool', 'grp'), None, 'tp'), may hold values from -6 to 6
- cache_kv: bfloat16 [256, 2, 256, 1024], P(('pool', 'grp'), None, None, 'tp'), may hold values from -6 to 6
- context_lengths: int32 [256], P(('pool', 'grp')), may hold values from 1 to 256
Outputs:
- seq_output: bfloat16 [256, 4, 8192], P(('pool', 'grp'), None, 'tp')
- joined_output: bfloat16 [64, 64, 4, 8192], P(('pool', 'grp'), None, None, 'tp')
Inputs may be any that keep to these rules, and one draw needn't show every extreme that they name: `prompt_target`: at most 2 prompts of one instance join the same decode instance.
All inputs are finite; a program needn't handle non-finite values.
Results may differ from a plain program's by a relative error of at most 0.011.
Values may be sent and summed in bfloat16 or wider, within the bound.
No kernel may reach another device: no remote copies, remote signals or barrier semaphores. Data moves between devices by JAX's collectives and lax.ppermute only.
A program may use at most 64 MiB of HBM per device.

v0:
```python
import jax
import jax.numpy as jnp
from jax import lax
from jax.sharding import PartitionSpec as P

HD = 128
QPK = 8
MOST = 2


EPS = 1e-06
MASKED_SCORE = -1e30


def partner(shard, axis, apart):
    return lax.ppermute(shard, axis, [(i, i ^ 1 << apart) for i in range(lax.axis_size(axis))])


def head_norm(raw_rows, key_gain):
    return (
        raw_rows * lax.rsqrt(jnp.mean(raw_rows * raw_rows, axis=-1, keepdims=True) + EPS) * key_gain
    )


def finish(raw_key, raw_value, key_gain):
    row_count = raw_key.shape[0]
    head_count = raw_key.shape[1] // HD
    normed_keys = head_norm(raw_key.reshape(row_count, head_count, HD), key_gain).astype(
        jnp.bfloat16
    )
    values = raw_value.reshape(row_count, head_count, HD).astype(jnp.bfloat16)
    return (normed_keys, values)


def rank_within(targets):
    slot_total = targets.shape[1]
    same_target = targets[:, :, None] == targets[:, None, :]
    earlier = jnp.arange(slot_total)[None, :] < jnp.arange(slot_total)[:, None]
    return jnp.sum(same_target & earlier[None], axis=2)


def column_adder(key_weight, value_weight):

    def accumulate(totals, segments, offset):
        return tuple(
            (
                (
                    jnp.dot(segment, key_weight, preferred_element_type=jnp.float32),
                    jnp.dot(segment, value_weight, preferred_element_type=jnp.float32),
                )
                for segment in segments
            )
        )

    return accumulate


def empty_pair(row_count, width):
    blank_sum = jnp.zeros((row_count, width), jnp.float32)
    return (blank_sum, blank_sum)


def attend_batch(queries, old_keys, old_values, old_valid, new_keys, new_values):
    batch_size, step_count = (queries.shape[0], queries.shape[1])
    head_count = old_keys.shape[2]
    grouped = queries.reshape(batch_size, step_count, head_count, QPK, HD)
    scaling = HD ** (-0.5)
    old_scores = (
        jnp.einsum("bskgd,bckd->bskgc", grouped, old_keys, preferred_element_type=jnp.float32)
        * scaling
    )
    new_scores = (
        jnp.einsum("bskgd,btkd->bskgt", grouped, new_keys, preferred_element_type=jnp.float32)
        * scaling
    )
    old_scores = jnp.where(old_valid[:, None, None, None, :], old_scores, MASKED_SCORE)
    causal = jnp.arange(step_count)[None, :] <= jnp.arange(step_count)[:, None]
    new_scores = jnp.where(causal[None, :, None, None, :], new_scores, MASKED_SCORE)
    highest = jnp.maximum(
        jnp.max(old_scores, axis=-1, keepdims=True), jnp.max(new_scores, axis=-1, keepdims=True)
    )
    old_exp = jnp.exp(old_scores - highest)
    new_exp = jnp.exp(new_scores - highest)
    totals = jnp.sum(old_exp, axis=-1, keepdims=True) + jnp.sum(new_exp, axis=-1, keepdims=True)
    old_prob = (old_exp / totals).astype(jnp.bfloat16)
    new_prob = (new_exp / totals).astype(jnp.bfloat16)
    blended = jnp.einsum(
        "bskgc,bckd->bskgd", old_prob, old_values, preferred_element_type=jnp.float32
    )
    blended = blended + jnp.einsum(
        "bskgt,btkd->bskgd", new_prob, new_values, preferred_element_type=jnp.float32
    )
    return blended.reshape(batch_size, step_count, head_count * QPK * HD).astype(jnp.bfloat16)


def on_device(
    prompt_states,
    prompt_lengths,
    prompt_target,
    prompt_query,
    prompt_next,
    key_weight,
    value_weight,
    key_gain,
    seq_query,
    seq_next,
    cache_kv,
    context_lengths,
):
    groups = lax.axis_size("grp")
    pool_count = lax.axis_size("pool")
    pool_index = lax.axis_index("pool")
    group_index = lax.axis_index("grp")
    tile_rows = prompt_states.shape[0]
    prompt_slots = prompt_query.shape[0]
    prompt_len = tile_rows // prompt_slots
    seq_count = seq_query.shape[0]
    step_count = seq_query.shape[1]
    query_width = seq_query.shape[2]
    kv_width = key_weight.shape[1]
    head_count = kv_width // HD
    feature_width = prompt_next.shape[2]
    accumulate = column_adder(key_weight, value_weight)
    seq_rows = seq_next.reshape(seq_count * step_count, feature_width)
    state_raw, seq_raw = accumulate(
        (empty_pair(tile_rows, kv_width), empty_pair(seq_rows.shape[0], kv_width)),
        (
            lax.all_gather(prompt_states, "tp", axis=1, tiled=True),
            lax.all_gather(seq_rows, "tp", axis=1, tiled=True),
        ),
        jnp.int32(0),
    )
    prompt_keys, prompt_values = finish(state_raw[0], state_raw[1], key_gain)
    prompt_kv = jnp.stack(
        [
            prompt_keys.reshape(prompt_slots, prompt_len, kv_width),
            prompt_values.reshape(prompt_slots, prompt_len, kv_width),
        ],
        axis=1,
    )
    packed_parts = jnp.concatenate(
        [
            prompt_kv.reshape(prompt_slots, -1),
            prompt_query.reshape(prompt_slots, -1),
            prompt_next.reshape(prompt_slots, -1),
        ],
        axis=1,
    )
    targets = prompt_target[:, :, 0]
    rankings = rank_within(targets)
    instance = pool_index * groups + group_index
    my_targets = lax.dynamic_index_in_dim(targets, instance, 0, keepdims=False)
    my_rankings = lax.dynamic_index_in_dim(rankings, instance, 0, keepdims=False)
    chooser = (my_targets[None, None, :] == jnp.arange(groups)[:, None, None]) & (
        my_rankings[None, None, :] == jnp.arange(MOST)[None, :, None]
    )
    chooser = chooser.astype(jnp.bfloat16).reshape(groups * MOST, prompt_slots)
    outgoing = (
        jnp.dot(chooser, packed_parts, preferred_element_type=jnp.float32)
        .astype(jnp.bfloat16)
        .reshape(groups, MOST, -1)
    )
    spread = lax.all_to_all(outgoing, "grp", split_axis=0, concat_axis=0, tiled=True)
    arrived = partner(spread, "pool", 0)
    slot_count = groups * MOST
    arrived = arrived.reshape(slot_count, -1)
    source_base = (pool_index + 1) % pool_count * groups
    source_targets = lax.dynamic_slice_in_dim(targets, source_base, groups, 0)
    source_rankings = lax.dynamic_slice_in_dim(rankings, source_base, groups, 0)
    source_lengths = lax.dynamic_slice_in_dim(prompt_lengths, source_base, groups, 0)
    matches = (source_targets[:, None, :] == group_index) & (
        source_rankings[:, None, :] == jnp.arange(MOST)[None, :, None]
    )
    slot_lengths = jnp.sum(jnp.where(matches, source_lengths[:, None, :], 0), axis=2).reshape(
        slot_count
    )
    kv_size = 2 * prompt_len * kv_width
    query_size = step_count * query_width
    arrived_kv = arrived[:, :kv_size].reshape(slot_count, 2, prompt_len, head_count, HD)
    arrived_query = arrived[:, kv_size : kv_size + query_size].reshape(
        slot_count, step_count, query_width
    )
    trailing = arrived[:, kv_size + query_size :]
    joined_rows = trailing.reshape(slot_count * step_count, feature_width)
    (joined_raw,) = accumulate(
        (empty_pair(joined_rows.shape[0], kv_width),),
        (lax.all_gather(joined_rows, "tp", axis=1, tiled=True),),
        jnp.int32(0),
    )
    joined_keys, joined_values = finish(joined_raw[0], joined_raw[1], key_gain)
    joined_keys = joined_keys.reshape(slot_count, step_count, head_count, HD)
    joined_values = joined_values.reshape(slot_count, step_count, head_count, HD)
    prompt_valid = jnp.arange(prompt_len)[None, :] < slot_lengths[:, None]
    joined_output = attend_batch(
        arrived_query, arrived_kv[:, 0], arrived_kv[:, 1], prompt_valid, joined_keys, joined_values
    )
    seq_keys, seq_values = finish(seq_raw[0], seq_raw[1], key_gain)
    seq_keys = seq_keys.reshape(seq_count, step_count, head_count, HD)
    seq_values = seq_values.reshape(seq_count, step_count, head_count, HD)
    cache_len = cache_kv.shape[2]
    cache_view = cache_kv.reshape(seq_count, 2, cache_len, head_count, HD)
    context_valid = jnp.arange(cache_len)[None, :] < context_lengths[:, None]
    seq_output = attend_batch(
        seq_query, cache_view[:, 0], cache_view[:, 1], context_valid, seq_keys, seq_values
    )
    return (seq_output, joined_output[None])


def solution(mesh):
    return jax.shard_map(
        on_device,
        mesh=mesh,
        in_specs=(
            P(("pool", "grp"), "tp"),
            P(),
            P(),
            P(("pool", "grp"), None, "tp"),
            P(("pool", "grp"), None, "tp"),
            P(None, "tp"),
            P(None, "tp"),
            P(),
            P(("pool", "grp"), None, "tp"),
            P(("pool", "grp"), None, "tp"),
            P(("pool", "grp"), None, None, "tp"),
            P(("pool", "grp")),
        ),
        out_specs=(P(("pool", "grp"), None, "tp"), P(("pool", "grp"), None, None, "tp")),
        check_vma=False,
    )
```

profile of v0, /device:TPU:1, one launch (start us, length us, event | category | flops | bytes accessed | tf_op | source)
XLA Modules:
  0.0 393.1 jit_solution(13669225518630355796)
XLA Ops:
  7.2 0.0 copy-start
  7.2 0.0 all-gather.3.cloned.1.call-start
  7.2 0.7 all-gather.3.cloned.1.call-update
  7.9 0.0 all-gather.5.cloned.1.call-start
  8.0 1.0 convert_reduce_fusion
  9.0 0.0 copy-start.8
  9.0 0.6 copy-done.8
  9.6 0.2 dynamic-slice_reduce_fusion
  9.8 1.5 dynamic-slice_reduce_fusion.1
  11.3 1.0 copy.58
  12.4 0.0 copy-start.9
  12.4 0.0 copy-start.2
  12.4 127.0 %all-gather.3.cloned.1.call-done = bf16[512,5120]{1,0:T(8,128)(2,1)} async-done(((bf16[512,640]{1,0:T(8,128)(2,1)}), bf16[512,5120]{1,0:T(8,128)(2,1)}) %all-gather.3.cloned.1.call-update) | async-done | bytes 5242896 | tf_op jit(solution)/shard_map/all_gather | solution.py:128
  139.5 4.2 %multiply_reduce_fusion = (f32[512]{0:T(512)S(1)}, f32[512,128]{1,0:T(8,128)S(1)}) fusion(bf16[512,5120]{1,0:T(8,128)(2,1)} %all-gather.3.cloned.1.call-done, bf16[5120,128]{1,0:T(8,128)(2,1)S(1)} %copy-done), kind=kOutput, calls=%fused_computation.52 | convolution fusion | flops 671219200 | bytes 6817792 | tf_op jit(solution)/shard_map/dot_general | solution.py:48
  143.7 0.1 multiply_convert_fusion
  143.9 1.5 convolution_convert_fusion.1
  145.4 0.1 copy.65
  145.5 0.5 convolution_convert_fusion
  146.0 1.4 reshape.419
  147.4 28.7 %all_to_all.5 = bf16[32,2,10752]{2,1,0:T(2,128)(2,1)S(1)} all-to-all(bf16[32,2,10752]{2,1,0:T(2,128)(2,1)} %reshape.419), channel_id=1, replica_groups=mesh['pool'=2,'grp'=32,'tp'=8] {'grp'}, dimensions={0} | all-to-all | bytes 2752512 | tf_op jit(solution)/shard_map/all_to_all | solution.py:163
  176.1 5.1 %collective-permute-start = (bf16[32,2,10752]{2,1,0:T(2,128)(2,1)S(1)}, bf16[32,2,10752]{2,1,0:T(2,128)(2,1)}, u32[]{:S(2)}, u32[]{:S(2)}) collective-permute-start(bf16[32,2,10752]{2,1,0:T(2,128)(2,1)S(1)} %all_to_all.5), channel_id=1, source_target_pairs={{0,256},{256,0},{1,257},{257,1},{2,258},{258,2},{3,259},{259,3},{4... | collective-permute-start | bytes 4128776 | tf_op jit(solution)/shard_map/ppermute | solution.py:16
  181.2 123.2 %collective-permute-done = bf16[32,2,10752]{2,1,0:T(2,128)(2,1)} collective-permute-done((bf16[32,2,10752]{2,1,0:T(2,128)(2,1)S(1)}, bf16[32,2,10752]{2,1,0:T(2,128)(2,1)}, u32[]{:S(2)}, u32[]{:S(2)}) %collective-permute-start) | collective-permute-done | bytes 1376288 | tf_op jit(solution)/shard_map/ppermute | solution.py:16
  304.4 1.6 reshape.420
  306.1 0.0 copy-start.6
  306.1 0.9 reshape.425
  307.1 0.0 all-gather.5.cloned.1.call-update
  307.1 0.8 constant_dynamic-slice_fusion
  307.9 0.1 copy.42
  308.0 0.1 copy.43
  308.1 0.1 dynamic-slice_compare_fusion
  308.2 0.1 copy.54
  308.3 0.1 select_reduce_fusion
  308.4 0.1 copy.44
  308.5 0.1 lt.79
  308.6 0.7 reshape.410
  309.4 0.8 reshape.409
  310.1 0.0 copy-start.12
  310.2 42.6 %all_gather.9 = bf16[16,5120]{1,0:T(8,128)(2,1)S(1)} all-gather(bf16[16,640]{1,0:T(8,128)(2,1)S(1)} %reshape.410), channel_id=1, replica_groups=mesh['pool'=2,'grp'=32,'tp'=8] {'tp'}, dimensions={1}, use_global_device_ids=true | all-gather | bytes 184320 | tf_op jit(solution)/shard_map/all_gather | solution.py:129
  352.8 0.4 multiply_reduce_fusion.2
  353.2 0.1 iota_compare_fusion.4
  353.3 0.1 multiply_convert_fusion.2
  353.4 0.3 fusion.35
  353.6 0.3 fusion.34
  354.0 0.2 fusion.26
  354.2 0.2 convolution_bitcast_fusion
  354.4 0.3 convolution_convert_fusion.3
  354.7 0.2 fusion.10
  354.9 0.6 convert_element_type.81
  355.6 0.1 iota_compare_fusion.1
  355.6 0.1 slice_bitcast_fusion.1
  355.7 0.1 copy.60
  355.8 0.1 copy.61
  355.9 0.6 fusion.36
  356.5 19.6 %all-gather.5.cloned.1.call-done = bf16[256,5120]{1,0:T(8,128)(2,1)} async-done(((bf16[256,640]{1,0:T(8,128)(2,1)}), bf16[256,5120]{1,0:T(8,128)(2,1)}) %all-gather.5.cloned.1.call-update) | async-done | bytes 2621456 | tf_op jit(solution)/shard_map/all_gather | solution.py:187
  376.1 2.6 multiply_reduce_fusion.1
  378.7 0.1 multiply_convert_fusion.1
  378.8 2.4 fusion.37
  381.3 0.5 fusion.22
  381.8 0.8 fusion.14
  382.6 0.4 copy-done.1
  383.0 0.8 convolution_convert_fusion.2
  383.9 0.5 fusion.23
  384.3 1.0 fusion.4
  385.3 0.9 convert_element_type.93
  (36 shorter events, 0.4 us)
Async XLA Ops:
  7.2 132.3 %copy-start = (bf16[5120,128]{1,0:T(8,128)(2,1)S(1)}, bf16[5120,128]{1,0:T(8,128)(2,1)}, u32[]{:S(2)}) copy-start(bf16[5120,128]{1,0:T(8,128)(2,1)} %param.17) | copy-start | bytes 3932164
  7.2 5.2 %copy-start.7 = (bf16[32,4,640]{2,1,0:T(4,128)(2,1)S(1)}, bf16[32,4,640]{2,1,0:T(4,128)(2,1)}, u32[]{:S(2)}) copy-start(bf16[32,4,640]{2,1,0:T(4,128)(2,1)} %param.16) | copy-start | bytes 491524
  7.2 132.3 %all-gather.3.cloned.1.call-start = ((), (), s32[]{:S(2)}) async-start(), calls=%async_computation.1 | async-start | bytes 5898240 | tf_op jit(solution)/shard_map/all_gather | solution.py:128
  7.9 368.1 %all-gather.5.cloned.1.call-start = ((), (), s32[]{:S(2)}) async-start(), calls=%async_computation.2 | async-start | bytes 2949120 | tf_op jit(solution)/shard_map/all_gather | solution.py:187
  9.0 0.6 copy-start.8
  12.4 131.3 %copy-start.9 = (f32[128]{0:T(128)S(1)}, f32[128]{0:T(128)}, u32[]{:S(2)}) copy-start(f32[128]{0:T(128)} %param.19) | copy-start | bytes 1540
  12.4 131.4 %copy-start.2 = (bf16[5120,128]{1,0:T(8,128)(2,1)S(1)}, bf16[5120,128]{1,0:T(8,128)(2,1)}, u32[]{:S(2)}) copy-start(bf16[5120,128]{1,0:T(8,128)(2,1)} %param.18) | copy-start | bytes 3932164
  139.5 4.4 %copy-start.11 = (bf16[512,5120]{1,0:T(8,128)(2,1)S(1)}, bf16[512,5120]{1,0:T(8,128)(2,1)}, u32[]{:S(2)}) copy-start(bf16[512,5120]{1,0:T(8,128)(2,1)} %all-gather.3.cloned.1.call-done) | copy-start | bytes 15728644
  176.1 128.3 %collective-permute-start = (bf16[32,2,10752]{2,1,0:T(2,128)(2,1)S(1)}, bf16[32,2,10752]{2,1,0:T(2,128)(2,1)}, u32[]{:S(2)}, u32[]{:S(2)}) collective-permute-start(bf16[32,2,10752]{2,1,0:T(2,128)(2,1)S(1)} %all_to_all.5), channel_id=1, source_target_pairs={{0,256},{256,0},{1,257},{257,1},{2,258},{258,2},{3,259},{259,3},{4... | collective-permute-start | bytes 4128776 | tf_op jit(solution)/shard_map/ppermute | solution.py:16
  306.1 2.0 copy-start.6
  306.1 4.0 %copy-start.5 = (bf16[4,2,256,128]{3,2,1,0:T(8,128)(2,1)S(1)}, bf16[4,2,256,128]{3,2,1,0:T(8,128)(2,1)}, u32[]{:S(2)}) copy-start(bf16[4,2,256,128]{3,2,1,0:T(8,128)(2,1)} %param.22) | copy-start | bytes 1572868
  310.1 43.0 %copy-start.12 = (s32[4]{0:T(128)S(1)}, s32[4]{0:T(128)}, u32[]{:S(2)}) copy-start(s32[4]{0:T(128)} %param.23) | copy-start | bytes 52
  310.2 43.1 %copy-start.10 = (f32[128]{0:T(128)S(1)}, f32[128]{0:T(128)}, u32[]{:S(2)}) copy-start(f32[128]{0:T(128)} %param.19) | copy-start | bytes 1540
  352.8 1.6 copy-start.3
  378.8 3.8 copy-start.4
  381.3 1.7 copy-start.1
Sparse Core Ops, SparseCore 0:
  10.1 129.2 all-gather.2
  307.2 68.7 all-gather.4
where the time goes:
time: 394 us; the launch traced here: 393 us
  waiting for transfers between devices  271 us (69%)
  blocking collectives  71.2 us (18%)
  matrix products  15.8 us (4%)
  between operations  14.5 us (4%)
  local copies, waits for them, and re-layouts  12.5 us (3%)
  starting transfers between devices  5.15 us (1%)
    all_gather x1, waiting for transfers between devices, on_device(): lax.all_gather(prompt_states, 'tp', axis=1, tiled=True)  127 us
    ppermute x1, waiting for transfers between devices, partner(): lax.ppermute(shard, axis, [(i, i ^ 1 << apart) for i in range(lax.axis_si...  123 us
    all_gather x1, blocking collectives, on_device(): lax.all_gather(seq_rows, 'tp', axis=1, tiled=True)  42.6 us
    all_to_all x1, blocking collectives, on_device(): lax.all_to_all(outgoing, 'grp', split_axis=0, concat_axis=0, tiled=True)  28.7 us
    all_gather x1, waiting for transfers between devices, on_device(): lax.all_gather(joined_rows, 'tp', axis=1, tiled=True)  19.6 us
  transfers between devices with their start and end apart: 3, of which 3 were waited for; matrix products, arithmetic and copies ran while one was open for 3% of the time, Pallas kernels for 0%

commit v1 on v0

v1 whole, which is shorter than its diff:
```python
import functools

import jax
import jax.numpy as jnp
from jax import lax
from jax.experimental import pallas as pl
from jax.experimental.pallas import tpu as pltpu
from jax.sharding import PartitionSpec as P

HD = 128
QPK = 8
MOST = 2
EPS = 1e-06
MASKED_SCORE = -1e30
GROUP = 8
ORDER = (0, 2, 1, 3)
CHUNKS = 1


def exchange(block, axis, apart):
    size = lax.axis_size(axis)
    return lax.ppermute(block, axis, [(i, i ^ apart) for i in range(size)])


def finish(own, received, gain):
    raw = own + received.astype(jnp.float32)
    raw_key = raw[:, :HD]
    scale = lax.rsqrt(jnp.mean(raw_key * raw_key, axis=-1, keepdims=True) + EPS)
    return (raw_key * scale * gain).astype(jnp.bfloat16), raw[:, HD:].astype(jnp.bfloat16)


def contract_last(left, right):
    return lax.dot_general(left, right, (((1,), (1,)), ((), ())), preferred_element_type=jnp.float32)


def attend(query_rows, old_keys, old_values, new_keys, new_values, old_seen, new_seen, out):
    rows = query_rows.shape[0]
    queries = jnp.concatenate([query_rows[:, h * HD : (h + 1) * HD] for h in range(QPK)], axis=0)
    scaling = HD ** (-0.5)
    old_scores = jnp.where(old_seen, contract_last(queries, old_keys) * scaling, MASKED_SCORE)
    new_scores = jnp.where(new_seen, contract_last(queries, new_keys) * scaling, MASKED_SCORE)
    highest = jnp.maximum(
        jnp.max(old_scores, axis=-1, keepdims=True), jnp.max(new_scores, axis=-1, keepdims=True)
    )
    old_exp = jnp.exp(old_scores - highest)
    new_exp = jnp.exp(new_scores - highest)
    totals = jnp.sum(old_exp, axis=-1, keepdims=True) + jnp.sum(new_exp, axis=-1, keepdims=True)
    old_prob = (old_exp / totals).astype(jnp.bfloat16)
    new_prob = (new_exp / totals).astype(jnp.bfloat16)
    blended = jnp.dot(old_prob, old_values, preferred_element_type=jnp.float32) + jnp.dot(
        new_prob, new_values, preferred_element_type=jnp.float32
    )
    blended = blended.astype(jnp.bfloat16)
    for h in range(QPK):
        out[:, h * HD : (h + 1) * HD] = blended[h * rows : (h + 1) * rows, :]


def seen_masks(rows, steps, old_len, old_count, new_count, old_live):
    old_shape, new_shape = (rows * QPK, old_count), (rows * QPK, new_count)
    old_row = lax.broadcasted_iota(jnp.int32, old_shape, 0) & (rows - 1)
    old_col = lax.broadcasted_iota(jnp.int32, old_shape, 1)
    step_bits = steps.bit_length() - 1
    len_bits = old_len.bit_length() - 1
    old_seen = ((old_row >> step_bits) == (old_col >> len_bits)) & (old_live > 0)
    new_row = lax.broadcasted_iota(jnp.int32, new_shape, 0) & (rows - 1)
    new_col = lax.broadcasted_iota(jnp.int32, new_shape, 1)
    new_seen = ((new_row >> step_bits) == (new_col >> step_bits)) & (new_col <= new_row)
    return old_seen, new_seen


def prompt_kernel(
    steps, prompt_len, own_old, got_old, own_new, got_new, gain, live, query, out
):
    old_keys, old_values = finish(own_old[...], got_old[...], gain[...])
    new_keys, new_values = finish(own_new[...], got_new[...], gain[...])
    rows = query.shape[0]
    old_seen, new_seen = seen_masks(
        rows, steps, prompt_len, old_keys.shape[0], new_keys.shape[0], live[0]
    )
    attend(query[...], old_keys, old_values, new_keys, new_values, old_seen, new_seen, out)


def prompt_attention(own_old, got_old, own_new, got_new, gain, live, query, steps, prompt_len):
    new_rows, old_rows = GROUP * steps, GROUP * prompt_len
    groups = query.shape[0] // new_rows
    row_block = lambda count, width: pl.BlockSpec((count, width), lambda g: (g, 0))
    return pl.pallas_call(
        functools.partial(prompt_kernel, steps, prompt_len),
        grid=(groups,),
        in_specs=[
            row_block(old_rows, 2 * HD),
            row_block(old_rows, 2 * HD),
            row_block(new_rows, 2 * HD),
            row_block(new_rows, 2 * HD),
            pl.BlockSpec((1, HD), lambda g: (0, 0)),
            pl.BlockSpec((1, 1, old_rows), lambda g: (g, 0, 0)),
            row_block(new_rows, QPK * HD),
        ],
        out_specs=row_block(new_rows, QPK * HD),
        out_shape=jax.ShapeDtypeStruct(query.shape, jnp.bfloat16),
        compiler_params=pltpu.CompilerParams(vmem_limit_bytes=24 * 2**20),
        cost_estimate=pl.CostEstimate(flops=10**9, bytes_accessed=2 * 10**6, transcendentals=10**5),
        name="prompt_attention",
    )(own_old, got_old, own_new, got_new, gain, live, query)


def cached_kernel(steps, own_new, got_new, gain, live, query, cache, out):
    new_keys, new_values = finish(own_new[...], got_new[...], gain[...])
    sequences, _, context, _ = cache.shape
    old_keys = cache[:, 0].reshape(sequences * context, HD)
    old_values = cache[:, 1].reshape(sequences * context, HD)
    old_seen, new_seen = seen_masks(
        query.shape[0], steps, context, sequences * context, new_keys.shape[0], live[...]
    )
    attend(query[...], old_keys, old_values, new_keys, new_values, old_seen, new_seen, out)


def cached_attention(own_new, got_new, gain, live, query, cache, steps):
    whole = pl.BlockSpec(memory_space=pltpu.VMEM)
    return pl.pallas_call(
        functools.partial(cached_kernel, steps),
        in_specs=[whole] * 6,
        out_specs=whole,
        out_shape=jax.ShapeDtypeStruct(query.shape, jnp.bfloat16),
        compiler_params=pltpu.CompilerParams(vmem_limit_bytes=24 * 2**20),
        cost_estimate=pl.CostEstimate(flops=10**9, bytes_accessed=2 * 10**6, transcendentals=10**5),
        name="cached_attention",
    )(own_new, got_new, gain, live, query, cache)


def rank_within(targets):
    slot_total = targets.shape[0]
    same_target = targets[:, None] == targets[None, :]
    earlier = jnp.arange(slot_total)[None, :] < jnp.arange(slot_total)[:, None]
    return jnp.sum(same_target & earlier, axis=1)


def on_device(
    prompt_states,
    prompt_lengths,
    prompt_target,
    prompt_query,
    prompt_next,
    key_weight,
    value_weight,
    key_gain,
    seq_query,
    seq_next,
    cache_kv,
    context_lengths,
):
    groups = lax.axis_size("grp")
    pool_index = lax.axis_index("pool")
    group_index = lax.axis_index("grp")
    lane = lax.axis_index("tp")
    prompts = prompt_query.shape[0]
    prompt_len = prompt_states.shape[0] // prompts
    seq_count, steps, query_width = seq_query.shape
    width = prompt_next.shape[2]
    quad = len(ORDER)

    share = quad * width // groups
    per_block = groups // quad
    block_number = jnp.asarray(ORDER, jnp.int32)[group_index // per_block]
    start = ((lane ^ 4) ^ block_number) * width + (group_index % per_block) * share
    weight_share = jnp.concatenate(
        [
            lax.dynamic_slice_in_dim(key_weight, start, share, 0),
            lax.dynamic_slice_in_dim(value_weight, start, share, 0),
        ],
        axis=1,
    )
    partner_weight = lax.all_gather(exchange(weight_share, "tp", 4), "grp", axis=0, tiled=True)
    own_weight = jnp.concatenate(
        [
            jnp.concatenate(
                [
                    lax.dynamic_slice_in_dim(weight, (lane ^ k) * width, width, 0)
                    for weight in (key_weight, value_weight)
                ],
                axis=1,
            )
            for k in ORDER
        ],
        axis=0,
    )

    gain = key_gain.reshape(1, HD)
    instance = pool_index * groups + group_index
    lengths = lax.dynamic_index_in_dim(prompt_lengths, instance, 0, keepdims=False)
    prompt_live = (jnp.arange(prompt_len)[None, :] < lengths[:, None]).astype(jnp.int32)
    prompt_live = prompt_live.reshape(prompts // GROUP, 1, GROUP * prompt_len)
    context = cache_kv.shape[2]
    seq_live = (jnp.arange(context)[None, :] < context_lengths[:, None]).astype(jnp.int32)
    seq_live = seq_live.reshape(1, seq_count * context)

    query_rows = prompt_query.reshape(prompts * steps, query_width)
    next_rows = prompt_next.reshape(prompts * steps, width)
    seq_rows = seq_next.reshape(seq_count * steps, width)

    part = prompts // CHUNKS
    old_rows, new_rows = part * prompt_len, part * steps
    outputs = []
    seq_output = None
    for c in range(CHUNKS):
        blocks = [
            prompt_states[c * old_rows : (c + 1) * old_rows],
            next_rows[c * new_rows : (c + 1) * new_rows],
        ]
        if c == CHUNKS - 1:
            blocks.append(seq_rows)
        mine = jnp.concatenate(blocks, axis=0)
        second = exchange(mine, "tp", 2)
        first = exchange(mine, "tp", 1)
        third = exchange(second, "tp", 1)
        features = (mine, second, first, third)

        def partial_sum(weight):
            return sum(
                jnp.dot(
                    block,
                    weight[k * width : (k + 1) * width],
                    preferred_element_type=jnp.float32,
                )
                for k, block in enumerate(features)
            )

        sent = partial_sum(partner_weight).astype(jnp.bfloat16)
        got = exchange(sent, "tp", 4)
        own = partial_sum(own_weight)
        outputs.append(
            prompt_attention(
                own[:old_rows],
                got[:old_rows],
                own[old_rows : old_rows + new_rows],
                got[old_rows : old_rows + new_rows],
                gain,
                prompt_live[c * part // GROUP : (c + 1) * part // GROUP],
                query_rows[c * new_rows : (c + 1) * new_rows],
                steps,
                prompt_len,
            )
        )
        if c == CHUNKS - 1:
            seq_output = cached_attention(
                own[old_rows + new_rows :],
                got[old_rows + new_rows :],
                gain,
                seq_live,
                seq_query.reshape(seq_count * steps, query_width),
                cache_kv,
                steps,
            ).reshape(seq_count, steps, query_width)

    crossed = [exchange(block, "pool", 1) for block in outputs]
    source = (pool_index ^ 1) * groups + group_index
    targets = lax.dynamic_index_in_dim(prompt_target[:, :, 0], source, 0, keepdims=False)
    places = targets * MOST + rank_within(targets)
    place_rows = (places[:, None] * steps + jnp.arange(steps)[None, :]).reshape(-1)
    chooser = (jnp.arange(groups * MOST * steps)[:, None] == place_rows[None, :]).astype(
        jnp.bfloat16
    )
    outgoing = sum(
        jnp.dot(
            chooser[:, c * new_rows : (c + 1) * new_rows],
            crossed[c],
            preferred_element_type=jnp.float32,
        )
        for c in range(CHUNKS)
    ).astype(jnp.bfloat16)
    arrived = lax.all_to_all(outgoing, "grp", split_axis=0, concat_axis=0, tiled=True)
    return seq_output, arrived.reshape(1, groups * MOST, steps, query_width)


def solution(mesh):
    return jax.shard_map(
        on_device,
        mesh=mesh,
        in_specs=(
            P(("pool", "grp"), "tp"),
            P(),
            P(),
            P(("pool", "grp"), None, "tp"),
            P(("pool", "grp"), None, "tp"),
            P(None, "tp"),
            P(None, "tp"),
            P(),
            P(("pool", "grp"), None, "tp"),
            P(("pool", "grp"), None, "tp"),
            P(("pool", "grp"), None, None, "tp"),
            P(("pool", "grp")),
        ),
        out_specs=(P(("pool", "grp"), None, "tp"), P(("pool", "grp"), None, None, "tp")),
        check_vma=False,
    )
```

time: 394 us -> 189 us (0.48)
  waiting for transfers between devices: 271 us -> 90.7 us
  blocking collectives: 71.2 us -> 0 us
  starting transfers between devices: 5.15 us -> 59.5 us
  matrix products: 15.8 us -> 8 us
    all_gather x2 -> x1, waiting for transfers between devices: 147 us -> 17.2 us  [on_device(): lax.all_gather(exchange(weight_share, 'tp', 4), 'grp', axis=0, tiled=True)]
    ppermute x1 -> x6, waiting for transfers between devices: 123 us -> 63.3 us  [exchange(): return lax.ppermute(block, axis, [(i, i ^ apart) for i in range(size)])]
    ppermute x1 -> x6, starting transfers between devices: 5.07 us -> 50.5 us  [exchange(): return lax.ppermute(block, axis, [(i, i ^ apart) for i in range(size)])]
    all_gather x1 -> x0, blocking collectives: 42.6 us -> none  [on_device(): lax.all_gather(seq_rows, 'tp', axis=1, tiled=True)]
    all_to_all x1 -> x0, blocking collectives: 28.7 us -> none  [on_device(): lax.all_to_all(outgoing, 'grp', split_axis=0, concat_axis=0, tiled=True)]
    all_to_all x0 -> x1, waiting for transfers between devices: none -> 10.1 us  [on_device(): lax.all_to_all(outgoing, 'grp', split_axis=0, concat_axis=0, tiled=True)]
    all_to_all x0 -> x1, starting transfers between devices: none -> 8.93 us  [on_device(): lax.all_to_all(outgoing, 'grp', split_axis=0, concat_axis=0, tiled=True)]
    dot_general x15 -> x9, matrix products: 15.8 us -> 8 us  [the longest x8 6.91 us: partial_sum(): jnp.dot(block, weight[k * width:(k + 1) * width], preferred_element_type=...]
  transfers between devices with their start and end apart: 3 -> 8, of which waited for: 3 -> 6; matrix products, arithmetic and copies ran while one was open for 3% -> 7% of each run, Pallas kernels for 0% -> 0%
where the time goes in v1:
time: 189 us; the launch traced here: 188 us
  waiting for transfers between devices  90.7 us (48%)
  starting transfers between devices  59.5 us (31%)
  between operations  15.2 us (8%)
  local copies, waits for them, and re-layouts  11.1 us (6%)
  matrix products  8 us (4%)
  Pallas kernels  3.38 us (2%)
    ppermute x6, waiting for transfers between devices, exchange(): return lax.ppermute(block, axis, [(i, i ^ apart) for i in range(size)])  63.3 us
    ppermute x6, starting transfers between devices, exchange(): return lax.ppermute(block, axis, [(i, i ^ apart) for i in range(size)])  50.5 us
    all_gather x1, waiting for transfers between devices, on_device(): lax.all_gather(exchange(weight_share, 'tp', 4), 'grp', axis=0, tiled=True)  17.2 us
    all_to_all x1, waiting for transfers between devices, on_device(): lax.all_to_all(outgoing, 'grp', split_axis=0, concat_axis=0, tiled=True)  10.1 us
    all_to_all x1, starting transfers between devices, on_device(): lax.all_to_all(outgoing, 'grp', split_axis=0, concat_axis=0, tiled=True)  8.93 us
    dot_general x8, matrix products, partial_sum(): jnp.dot(block, weight[k * width:(k + 1) * width], preferred_element_type=...  6.91 us
  transfers between devices with their start and end apart: 8, of which 6 were waited for; matrix products, arithmetic and copies ran while one was open for 7% of the time, Pallas kernels for 0%

profile of v1, /device:TPU:1, one launch (start us, length us, event | category | flops | bytes accessed | tf_op | source)
XLA Modules:
  0.0 188.1 jit_solution(2037053073454897971)
XLA Ops:
  7.2 0.0 copy-start
  7.2 0.0 copy-start.13
  7.2 0.0 all-gather.2.cloned.1.call-start
  7.3 1.2 dynamic_slice.48
  9.2 0.8 constant_dynamic-slice_fusion
  9.9 9.6 %collective-permute-start.3 = (bf16[80,256]{1,0:T(8,128)(2,1)S(1)}, bf16[80,256]{1,0:T(8,128)(2,1)S(1)}, u32[]{:S(2)}, u32[]{:S(2)}) collective-permute-start(bf16[80,256]{1,0:T(8,128)(2,1)S(1)} %pad_maximum_fusion), channel_id=1, source_target_pairs={{0,4},{1,5},{2,6},{3,7},{4,0},{5,1},{6,2},{7,3},{8,12},{9,13},{10,... | collective-permute-start | bytes 122888 | tf_op jit(solution)/shard_map/ppermute | solution.py:22
  19.6 1.4 collective-permute-done.3
  21.0 0.6 copy-done.11
  21.6 0.0 all-gather.2.cloned.1.call-update
  21.6 0.7 reshape.132
  22.3 1.0 reshape.131
  23.3 1.1 constant_dynamic-update-slice_fusion.2
  24.5 4.9 %collective-permute-start = (bf16[656,640]{1,0:T(8,128)(2,1)S(1)}, bf16[656,640]{1,0:T(8,128)(2,1)S(1)}, u32[]{:S(2)}, u32[]{:S(2)}) collective-permute-start(bf16[656,640]{1,0:T(8,128)(2,1)S(1)} %constant_dynamic-update-slice_fusion), channel_id=1, source_target_pairs={{0,2},{1,3},{2,0},{3,1},{4,6},{5,7},{6,4},{7,5},{8,10},{9,11},{10,... | collective-permute-start | bytes 2519048 | tf_op jit(solution)/shard_map/ppermute | solution.py:22
  29.4 4.6 %collective-permute-start.1 = (bf16[656,640]{1,0:T(8,128)(2,1)S(1)}, bf16[656,640]{1,0:T(8,128)(2,1)S(1)}, u32[]{:S(2)}, u32[]{:S(2)}) collective-permute-start(bf16[656,640]{1,0:T(8,128)(2,1)S(1)} %constant_dynamic-update-slice_fusion), channel_id=1, source_target_pairs={{0,1},{1,0},{2,3},{3,2},{4,5},{5,4},{6,7},{7,6},{8,9},{9,8},{10,11... | collective-permute-start | bytes 2519048 | tf_op jit(solution)/shard_map/ppermute | solution.py:22
  34.0 0.0 copy-done
  34.0 0.2 dynamic-slice_reduce_fusion
  34.2 0.1 lt.116
  34.3 0.1 lt.113
  34.4 0.1 lt.117
  34.5 0.1 lt.118
  34.6 0.0 copy-done.13
  34.6 0.7 dynamic-slice_reduce_fusion.1
  35.3 0.0 copy-start.10
  35.3 2.4 %constant_dynamic-slice_fusion.2 = (bf16[640,128]{1,0:T(8,128)(2,1)}, bf16[640,128]{1,0:T(8,128)(2,1)}, bf16[640,128]{1,0:T(8,128)(2,1)}, bf16[640,128]{1,0:T(8,...) fusion(bf16[5120,128]{1,0:T(8,128)(2,1)} %param.19, ...), kind=kLoop, calls=%fused_computation.45 | loop fusion | bytes 2621456 | tf_op jit(solution)/shard_map/dynamic_slice | solution.py:178
  37.7 0.2 convert_reduce_fusion
  37.9 0.0 copy-done.10
  37.9 0.1 reshape.136.query
  38.0 0.0 copy-start.8
  38.0 0.0 copy-start.9
  38.0 0.4 fusion.9
  38.4 25.7 %collective-permute-done = bf16[656,640]{1,0:T(8,128)(2,1)S(1)} collective-permute-done((bf16[656,640]{1,0:T(8,128)(2,1)S(1)}, bf16[656,640]{1,0:T(8,128)(2,1)S(1)}, u32[]{:S(2)}, u32[]{:S(2)}) %collective-permute-start) | collective-permute-done | bytes 839712 | tf_op jit(solution)/shard_map/ppermute | solution.py:22
  64.1 4.8 %collective-permute-start.2 = (bf16[656,640]{1,0:T(8,128)(2,1)S(1)}, bf16[656,640]{1,0:T(8,128)(2,1)}, u32[]{:S(2)}, u32[]{:S(2)}) collective-permute-start(bf16[656,640]{1,0:T(8,128)(2,1)S(1)} %collective-permute-done), channel_id=1, source_target_pairs={{0,1},{1,0},{2,3},{3,2},{4,5},{5,4},{6,7},{7,6},{8,9},{9,8},{10,11... | collective-permute-start | bytes 2519048 | tf_op jit(solution)/shard_map/ppermute | solution.py:22
  68.9 0.4 convolution_add_fusion.4
  69.4 17.2 %all-gather.2.cloned.1.call-done = bf16[2560,256]{1,0:T(8,128)(2,1)} async-done(((bf16[80,256]{1,0:T(8,128)(2,1)}), bf16[2560,256]{1,0:T(8,128)(2,1)}) %all-gather.2.cloned.1.call-update) | async-done | bytes 1310736 | tf_op jit(solution)/shard_map/all_gather | solution.py:173
  86.6 1.5 fusion.6
  88.1 0.0 collective-permute-done.1
  88.1 0.4 fusion.4
  88.5 0.4 fusion
  89.0 0.0 collective-permute-done.2
  89.0 1.6 fusion.2
  90.7 0.0 copy-start.4
  90.7 7.5 %collective-permute-start.4 = (bf16[656,256]{1,0:T(8,128)(2,1)S(1)}, bf16[656,256]{1,0:T(8,128)(2,1)S(1)}, u32[]{:S(2)}, u32[]{:S(2)}) collective-permute-start(bf16[656,256]{1,0:T(8,128)(2,1)S(1)} %fusion.2), channel_id=1, source_target_pairs={{0,4},{1,5},{2,6},{3,7},{4,0},{5,1},{6,2},{7,3},{8,12},{9,13},{10,... | collective-permute-start | bytes 1007624 | tf_op jit(solution)/shard_map/ppermute | solution.py:22
  98.2 0.4 convolution_add_fusion.3
  98.7 1.6 convolution_add_fusion.2
  100.3 0.0 copy-start.2
  100.3 26.8 %collective-permute-done.4 = bf16[656,256]{1,0:T(8,128)(2,1)S(1)} collective-permute-done((bf16[656,256]{1,0:T(8,128)(2,1)S(1)}, bf16[656,256]{1,0:T(8,128)(2,1)S(1)}, u32[]{:S(2)}, u32[]{:S(2)}) %collective-permute-start.4) | collective-permute-done | bytes 335904 | tf_op jit(solution)/shard_map/ppermute | solution.py:22
  127.2 0.0 copy-done.2
  127.2 2.7 %prompt_attention.1 = bf16[128,1024]{1,0:T(8,128)(2,1)S(1)} custom-call(f32[512,256]{1,0:T(8,128)S(1)} %slice.46.own_old, bf16[512,256]{1,0:T(8,128)(2,1)S(1)} %slice.47.got_old, f32[128,256]{1,0:T(8,128)S(1)} %slice.48.own_new, bf16[128,256]{1,0:T(8,128)(2,1)S(1)} %slice.49.got_new, f32[1,128]{1,0:T(1,128)S(1)} %bitcast.18, ...), custom_call_target="tpu_custom_call" | custom-call | flops 1000000000 | bytes 2000000 | tf_op jit(solution)/shard_map/prompt_attention/pallas_call | solution.py:87
  129.9 0.0 copy-start.14
  129.9 0.0 copy-start.12
  129.9 0.0 copy-start.1
  129.9 19.1 %collective-permute-start.5 = (bf16[128,1024]{1,0:T(8,128)(2,1)S(1)}, bf16[128,1024]{1,0:T(8,128)(2,1)S(1)}, u32[]{:S(2)}, u32[]{:S(2)}) collective-permute-start(bf16[128,1024]{1,0:T(8,128)(2,1)S(1)} %prompt_attention.1), channel_id=1, source_target_pairs={{0,256},{256,0},{1,257},{257,1},{2,258},{258,2},{3,259},{259,3},{4... | collective-permute-start | bytes 786440 | tf_op jit(solution)/shard_map/ppermute | solution.py:22
  149.0 0.1 iota_add_fusion
  149.0 0.1 add.109
  149.2 9.5 %collective-permute-done.5 = bf16[128,1024]{1,0:T(8,128)(2,1)S(1)} collective-permute-done((bf16[128,1024]{1,0:T(8,128)(2,1)S(1)}, bf16[128,1024]{1,0:T(8,128)(2,1)S(1)}, u32[]{:S(2)}, u32[]{:S(2)}) %collective-permute-start.5) | collective-permute-done | bytes 262176 | tf_op jit(solution)/shard_map/ppermute | solution.py:22
  158.6 1.1 fusion.1
  159.7 8.9 %all-to-all-start = ((bf16[32,8,1024]{2,1,0:T(8,128)(2,1)}), bf16[32,8,1024]{2,1,0:T(8,128)(2,1)S(1)}, u32[]{:S(2)}, u32[]{:S(2)}) async-start(bf16[32,8,1024]{2,1,0:T(8,128)(2,1)} %fusion.1), calls=%async_computation | async-start | bytes 1048576 | tf_op jit(solution)/shard_map/all_to_all | solution.py:271
  168.6 0.0 copy-done.14
  168.7 0.1 convert_bitcast_fusion
  168.8 0.0 copy-done.1
  168.8 0.7 cached_attention.1
  169.5 0.6 reshape.135
  170.1 10.1 %all-to-all-done = bf16[32,8,1024]{2,1,0:T(8,128)(2,1)S(1)} async-done(((bf16[32,8,1024]{2,1,0:T(8,128)(2,1)}), bf16[32,8,1024]{2,1,0:T(8,128)(2,1)S(1)}, u32[]{:S(2)}, u32[]{:S(2)}) %all-to-all-start) | async-done | bytes 524320 | tf_op jit(solution)/shard_map/all_to_all | solution.py:271
  180.3 1.0 reshape.137
  (27 shorter events, 0.2 us)
Async XLA Ops:
  7.2 26.9 %copy-start = (s32[64,32]{0,1:T(8,128)S(1)}, s32[64,32]{0,1:T(8,128)}, u32[]{:S(2)}) copy-start(s32[64,32]{0,1:T(8,128)} %param.14) | copy-start | bytes 24580
  7.2 27.4 %copy-start.13 = (s32[64,32,1]{0,2,1:T(1,128)S(1)}, s32[64,32,1]{0,2,1:T(1,128)}, u32[]{:S(2)}) copy-start(s32[64,32,1]{0,2,1:T(1,128)} %param.15) | copy-start | bytes 24580
  7.2 79.4 %all-gather.2.cloned.1.call-start = ((), (), s32[]{:S(2)}) async-start(), calls=%async_computation.1 | async-start | bytes 1351680 | tf_op jit(solution)/shard_map/all_gather | solution.py:173
  9.9 11.0 %collective-permute-start.3 = (bf16[80,256]{1,0:T(8,128)(2,1)S(1)}, bf16[80,256]{1,0:T(8,128)(2,1)S(1)}, u32[]{:S(2)}, u32[]{:S(2)}) collective-permute-start(bf16[80,256]{1,0:T(8,128)(2,1)S(1)} %pad_maximum_fusion), channel_id=1, source_target_pairs={{0,4},{1,5},{2,6},{3,7},{4,0},{5,1},{6,2},{7,3},{8,12},{9,13},{10,... | collective-permute-start | bytes 122888 | tf_op jit(solution)/shard_map/ppermute | solution.py:22
  21.0 0.6 copy-start.11
  24.5 39.6 %collective-permute-start = (bf16[656,640]{1,0:T(8,128)(2,1)S(1)}, bf16[656,640]{1,0:T(8,128)(2,1)S(1)}, u32[]{:S(2)}, u32[]{:S(2)}) collective-permute-start(bf16[656,640]{1,0:T(8,128)(2,1)S(1)} %constant_dynamic-update-slice_fusion), channel_id=1, source_target_pairs={{0,2},{1,3},{2,0},{3,1},{4,6},{5,7},{6,4},{7,5},{8,10},{9,11},{10,... | collective-permute-start | bytes 2519048 | tf_op jit(solution)/shard_map/ppermute | solution.py:22
  29.4 58.7 %collective-permute-start.1 = (bf16[656,640]{1,0:T(8,128)(2,1)S(1)}, bf16[656,640]{1,0:T(8,128)(2,1)S(1)}, u32[]{:S(2)}, u32[]{:S(2)}) collective-permute-start(bf16[656,640]{1,0:T(8,128)(2,1)S(1)} %constant_dynamic-update-slice_fusion), channel_id=1, source_target_pairs={{0,1},{1,0},{2,3},{3,2},{4,5},{5,4},{6,7},{7,6},{8,9},{9,8},{10,11... | collective-permute-start | bytes 2519048 | tf_op jit(solution)/shard_map/ppermute | solution.py:22
  35.3 2.6 %copy-start.10 = (bf16[32,4,1024]{2,1,0:T(4,128)(2,1)S(1)}, bf16[32,4,1024]{2,1,0:T(4,128)(2,1)}, u32[]{:S(2)}) copy-start(bf16[32,4,1024]{2,1,0:T(4,128)(2,1)} %param.16) | copy-start | bytes 786436
  38.0 31.0 %copy-start.8 = (bf16[640,128]{1,0:T(8,128)(2,1)S(1)}, bf16[640,128]{1,0:T(8,128)(2,1)}, u32[]{:S(2)}) copy-start(bf16[640,128]{1,0:T(8,128)(2,1)} %get-tuple-element.8) | copy-start | bytes 491524
  38.0 31.0 %copy-start.9 = (bf16[640,128]{1,0:T(8,128)(2,1)S(1)}, bf16[640,128]{1,0:T(8,128)(2,1)}, u32[]{:S(2)}) copy-start(bf16[640,128]{1,0:T(8,128)(2,1)} %get-tuple-element.11) | copy-start | bytes 491524
  64.1 24.9 %collective-permute-start.2 = (bf16[656,640]{1,0:T(8,128)(2,1)S(1)}, bf16[656,640]{1,0:T(8,128)(2,1)}, u32[]{:S(2)}, u32[]{:S(2)}) collective-permute-start(bf16[656,640]{1,0:T(8,128)(2,1)S(1)} %collective-permute-done), channel_id=1, source_target_pairs={{0,1},{1,0},{2,3},{3,2},{4,5},{5,4},{6,7},{7,6},{8,9},{9,8},{10,11... | collective-permute-start | bytes 2519048 | tf_op jit(solution)/shard_map/ppermute | solution.py:22
  86.6 1.5 copy-start.3
  89.0 9.2 %copy-start.6 = (bf16[640,128]{1,0:T(8,128)(2,1)S(1)}, bf16[640,128]{1,0:T(8,128)(2,1)}, u32[]{:S(2)}) copy-start(bf16[640,128]{1,0:T(8,128)(2,1)} %get-tuple-element.7) | copy-start | bytes 491524
  89.0 9.2 %copy-start.7 = (bf16[640,128]{1,0:T(8,128)(2,1)S(1)}, bf16[640,128]{1,0:T(8,128)(2,1)}, u32[]{:S(2)}) copy-start(bf16[640,128]{1,0:T(8,128)(2,1)} %get-tuple-element.12) | copy-start | bytes 491524
  90.7 8.0 %copy-start.4 = (bf16[640,128]{1,0:T(8,128)(2,1)S(1)}, bf16[640,128]{1,0:T(8,128)(2,1)}, u32[]{:S(2)}) copy-start(bf16[640,128]{1,0:T(8,128)(2,1)} %get-tuple-element.6) | copy-start | bytes 491524
  90.7 8.0 %copy-start.5 = (bf16[640,128]{1,0:T(8,128)(2,1)S(1)}, bf16[640,128]{1,0:T(8,128)(2,1)}, u32[]{:S(2)}) copy-start(bf16[640,128]{1,0:T(8,128)(2,1)} %get-tuple-element.13) | copy-start | bytes 491524
  90.7 36.5 %collective-permute-start.4 = (bf16[656,256]{1,0:T(8,128)(2,1)S(1)}, bf16[656,256]{1,0:T(8,128)(2,1)S(1)}, u32[]{:S(2)}, u32[]{:S(2)}) collective-permute-start(bf16[656,256]{1,0:T(8,128)(2,1)S(1)} %fusion.2), channel_id=1, source_target_pairs={{0,4},{1,5},{2,6},{3,7},{4,0},{5,1},{6,2},{7,3},{8,12},{9,13},{10,... | collective-permute-start | bytes 1007624 | tf_op jit(solution)/shard_map/ppermute | solution.py:22
  100.3 26.9 %copy-start.2 = (f32[128]{0:T(128)S(1)}, f32[128]{0:T(128)}, u32[]{:S(2)}) copy-start(f32[128]{0:T(128)} %param.20) | copy-start | bytes 1540
  129.9 38.8 %copy-start.14 = (s32[4]{0:T(128)S(1)}, s32[4]{0:T(128)}, u32[]{:S(2)}) copy-start(s32[4]{0:T(128)} %param.24) | copy-start | bytes 52
  129.9 38.9 %copy-start.12 = (bf16[4,4,1024]{2,1,0:T(4,128)(2,1)S(1)}, bf16[4,4,1024]{2,1,0:T(4,128)(2,1)}, u32[]{:S(2)}) copy-start(bf16[4,4,1024]{2,1,0:T(4,128)(2,1)} %param.21) | copy-start | bytes 98308
  129.9 38.9 %copy-start.1 = (bf16[4,2,256,128]{3,2,1,0:T(8,128)(2,1)S(1)}, bf16[4,2,256,128]{3,2,1,0:T(8,128)(2,1)}, u32[]{:S(2)}) copy-start(bf16[4,2,256,128]{3,2,1,0:T(8,128)(2,1)} %cache.1) | copy-start | bytes 1572868
  129.9 28.7 %collective-permute-start.5 = (bf16[128,1024]{1,0:T(8,128)(2,1)S(1)}, bf16[128,1024]{1,0:T(8,128)(2,1)S(1)}, u32[]{:S(2)}, u32[]{:S(2)}) collective-permute-start(bf16[128,1024]{1,0:T(8,128)(2,1)S(1)} %prompt_attention.1), channel_id=1, source_target_pairs={{0,256},{256,0},{1,257},{257,1},{2,258},{258,2},{3,259},{259,3},{4... | collective-permute-start | bytes 786440 | tf_op jit(solution)/shard_map/ppermute | solution.py:22
  159.7 20.6 %all-to-all-start = ((bf16[32,8,1024]{2,1,0:T(8,128)(2,1)}), bf16[32,8,1024]{2,1,0:T(8,128)(2,1)S(1)}, u32[]{:S(2)}, u32[]{:S(2)}) async-start(bf16[32,8,1024]{2,1,0:T(8,128)(2,1)} %fusion.1), calls=%async_computation | async-start | bytes 1048576 | tf_op jit(solution)/shard_map/all_to_all | solution.py:271
Sparse Core Ops, SparseCore 0:
  21.7 64.8 all-gather.1

commit v2 on v1

v2 whole, which is shorter than its diff:
```python
import functools

import jax
import jax.numpy as jnp
from jax import lax
from jax.experimental import pallas as pl
from jax.experimental.pallas import tpu as pltpu
from jax.sharding import PartitionSpec as P

HD = 128
QPK = 8
MOST = 2
EPS = 1e-06
MASKED_SCORE = -1e30
GROUP = 8
QUAD = 4
BUCKETS = (384,)


def exchange(block, axis, apart):
    size = lax.axis_size(axis)
    return lax.ppermute(block, axis, [(i, i ^ apart) for i in range(size)])


def finish(own, received, gain):
    raw = own + received.astype(jnp.float32)
    raw_key = raw[:, :HD]
    scale = lax.rsqrt(jnp.mean(raw_key * raw_key, axis=-1, keepdims=True) + EPS)
    return (raw_key * scale * gain).astype(jnp.bfloat16), raw[:, HD:].astype(jnp.bfloat16)


def contract_last(left, right):
    return lax.dot_general(left, right, (((1,), (1,)), ((), ())), preferred_element_type=jnp.float32)


def attend(query_rows, old_keys, old_values, new_keys, new_values, old_seen, new_seen, out):
    rows = query_rows.shape[0]
    queries = jnp.concatenate([query_rows[:, h * HD : (h + 1) * HD] for h in range(QPK)], axis=0)
    scaling = HD ** (-0.5)
    old_scores = jnp.where(old_seen, contract_last(queries, old_keys) * scaling, MASKED_SCORE)
    new_scores = jnp.where(new_seen, contract_last(queries, new_keys) * scaling, MASKED_SCORE)
    highest = jnp.maximum(
        jnp.max(old_scores, axis=-1, keepdims=True), jnp.max(new_scores, axis=-1, keepdims=True)
    )
    old_exp = jnp.exp(old_scores - highest)
    new_exp = jnp.exp(new_scores - highest)
    totals = jnp.sum(old_exp, axis=-1, keepdims=True) + jnp.sum(new_exp, axis=-1, keepdims=True)
    old_prob = (old_exp / totals).astype(jnp.bfloat16)
    new_prob = (new_exp / totals).astype(jnp.bfloat16)
    blended = jnp.dot(old_prob, old_values, preferred_element_type=jnp.float32) + jnp.dot(
        new_prob, new_values, preferred_element_type=jnp.float32
    )
    blended = blended.astype(jnp.bfloat16)
    for h in range(QPK):
        out[:, h * HD : (h + 1) * HD] = blended[h * rows : (h + 1) * rows, :]


def new_mask(rows, steps, count, first):
    shape = (rows * QPK, count)
    step_bits = steps.bit_length() - 1
    row = (lax.broadcasted_iota(jnp.int32, shape, 0) & (rows - 1)) + first
    column = lax.broadcasted_iota(jnp.int32, shape, 1)
    return ((row >> step_bits) == (column >> step_bits)) & (column <= row)


def old_mask(rows, steps, owners, first):
    shape = (rows * QPK, owners.shape[1])
    step_bits = steps.bit_length() - 1
    row = (lax.broadcasted_iota(jnp.int32, shape, 0) & (rows - 1)) + first
    return (row >> step_bits) == owners


def pack_kernel(place, states, nexts, sequences, packed):
    kept = packed.shape[0] - nexts.shape[0] - sequences.shape[0]
    row = lax.broadcasted_iota(jnp.int32, (kept, place.shape[1]), 0)
    chooser = (row == place[...]).astype(jnp.float32).astype(jnp.bfloat16)
    live = jnp.dot(chooser, states[...], preferred_element_type=jnp.float32)
    packed[:kept, :] = live.astype(jnp.bfloat16)
    packed[kept : kept + nexts.shape[0], :] = nexts[...]
    packed[kept + nexts.shape[0] :, :] = sequences[...]


def pack(place, states, nexts, sequences, kept):
    whole = pl.BlockSpec(memory_space=pltpu.VMEM)
    rows = kept + nexts.shape[0] + sequences.shape[0]
    return pl.pallas_call(
        pack_kernel,
        in_specs=[whole] * 4,
        out_specs=whole,
        out_shape=jax.ShapeDtypeStruct((rows, states.shape[1]), jnp.bfloat16),
        compiler_params=pltpu.CompilerParams(vmem_limit_bytes=24 * 2**20),
        name="pack",
    )(place, states, nexts, sequences)


def prompt_kernel(steps, own, got, gain, owners, query, out):
    kept = owners.shape[1]
    count = query.shape[0]
    old_keys, old_values = finish(own[:kept], got[:kept], gain[...])
    new_keys, new_values = finish(own[kept : kept + count], got[kept : kept + count], gain[...])
    rows = GROUP * steps
    for first in range(0, count, rows):
        attend(
            query[first : first + rows],
            old_keys,
            old_values,
            new_keys[first : first + rows],
            new_values[first : first + rows],
            old_mask(rows, steps, owners[...], first),
            new_mask(rows, steps, rows, 0),
            out.at[pl.ds(first, rows)],
        )


def prompt_attention(own, got, gain, owners, query, steps):
    whole = pl.BlockSpec(memory_space=pltpu.VMEM)
    return pl.pallas_call(
        functools.partial(prompt_kernel, steps),
        in_specs=[whole] * 5,
        out_specs=whole,
        out_shape=jax.ShapeDtypeStruct(query.shape, jnp.bfloat16),
        compiler_params=pltpu.CompilerParams(vmem_limit_bytes=32 * 2**20),
        cost_estimate=pl.CostEstimate(flops=10**9, bytes_accessed=2 * 10**6, transcendentals=10**5),
        name="prompt_attention",
    )(own, got, gain, owners, query)


def cached_kernel(steps, own_new, got_new, gain, owners, query, cache, out):
    new_keys, new_values = finish(own_new[...], got_new[...], gain[...])
    sequences, _, context, _ = cache.shape
    old_keys = cache[:, 0].reshape(sequences * context, HD)
    old_values = cache[:, 1].reshape(sequences * context, HD)
    rows = query.shape[0]
    attend(
        query[...],
        old_keys,
        old_values,
        new_keys,
        new_values,
        old_mask(rows, steps, owners[...], 0),
        new_mask(rows, steps, rows, 0),
        out,
    )


def cached_attention(own, got, gain, owners, query, cache, steps):
    rows = query.shape[0]
    last = own.shape[0] // rows - 1
    fresh = pl.BlockSpec((rows, 2 * HD), lambda g: (last, 0))
    return pl.pallas_call(
        functools.partial(cached_kernel, steps),
        grid=(1,),
        in_specs=[
            fresh,
            fresh,
            pl.BlockSpec((1, HD), lambda g: (0, 0)),
            pl.BlockSpec(owners.shape, lambda g: (0, 0)),
            pl.BlockSpec(query.shape, lambda g: (0, 0)),
            pl.BlockSpec(cache.shape, lambda g: (0, 0, 0, 0)),
        ],
        out_specs=pl.BlockSpec(query.shape, lambda g: (0, 0)),
        out_shape=jax.ShapeDtypeStruct(query.shape, jnp.bfloat16),
        compiler_params=pltpu.CompilerParams(vmem_limit_bytes=24 * 2**20),
        cost_estimate=pl.CostEstimate(flops=10**9, bytes_accessed=2 * 10**6, transcendentals=10**5),
        name="cached_attention",
    )(own, got, gain, owners, query, cache)


def spread(share):
    copies = jnp.broadcast_to(share[None], (lax.axis_size("grp"),) + share.shape)
    arrived = lax.all_to_all(copies, "grp", split_axis=0, concat_axis=0, tiled=True)
    return arrived.reshape(-1, share.shape[1])


def project_kernel(order, block_number, *refs):
    features, (key_block, value_block, partner_block, own, sent, total) = refs[:-6], refs[-6:]
    k = pl.program_id(0)

    @pl.when(k == 0)
    def _():
        total[...] = jnp.zeros_like(total)

    def add(block):
        weight = jnp.concatenate([key_block[...], value_block[...], partner_block[...]], axis=1)
        total[...] += jnp.dot(block[...], weight, preferred_element_type=jnp.float32)

    for index, block in enumerate(features):
        pl.when(k == index)(functools.partial(add, block))

    @pl.when(k == pl.num_programs(0) - 1)
    def _():
        own[...] = total[:, : 2 * HD]
        sent[...] = total[:, 2 * HD :].astype(jnp.bfloat16)


def project(features, order, block_number, weights):
    rows, width = features[0].shape
    own_spec = pl.BlockSpec((width, HD), lambda k, o, b: (b[k], 0))
    whole = pl.BlockSpec((rows, 2 * HD), lambda k, o, b: (0, 0))
    return pl.pallas_call(
        project_kernel,
        grid_spec=pltpu.PrefetchScalarGridSpec(
            num_scalar_prefetch=2,
            grid=(QUAD,),
            in_specs=[pl.BlockSpec((rows, width), lambda k, o, b: (0, 0))] * QUAD
            + [own_spec, own_spec, pl.BlockSpec((width, 2 * HD), lambda k, o, b: (o[k], 0))],
            out_specs=[whole, whole],
            scratch_shapes=[pltpu.VMEM((rows, 4 * HD), jnp.float32)],
        ),
        out_shape=[
            jax.ShapeDtypeStruct((rows, 2 * HD), jnp.float32),
            jax.ShapeDtypeStruct((rows, 2 * HD), jnp.bfloat16),
        ],
        compiler_params=pltpu.CompilerParams(vmem_limit_bytes=32 * 2**20),
        cost_estimate=pl.CostEstimate(
            flops=2 * rows * width * QUAD * 4 * HD, bytes_accessed=8 * 10**6, transcendentals=0
        ),
        name="project",
    )(order, block_number, *features, *weights)


def pass_on(block, awaited):
    anywhere = pl.BlockSpec(memory_space=pl.ANY)
    return pl.pallas_call(
        lambda block_ref, awaited_ref, out_ref: None,
        in_specs=[anywhere, anywhere],
        out_specs=anywhere,
        out_shape=jax.ShapeDtypeStruct(block.shape, block.dtype),
        input_output_aliases={0: 0},
        name="pass_on",
    )(block, awaited)


def rank_within(targets):
    slot_total = targets.shape[0]
    same_target = targets[:, None] == targets[None, :]
    earlier = jnp.arange(slot_total)[None, :] < jnp.arange(slot_total)[:, None]
    return jnp.sum(same_target & earlier, axis=1)


def run(
    kept,
    prompt_states,
    prompt_lengths,
    prompt_target,
    prompt_query,
    prompt_next,
    key_weight,
    value_weight,
    key_gain,
    seq_query,
    seq_next,
    cache_kv,
    context_lengths,
):
    groups = lax.axis_size("grp")
    pool_index = lax.axis_index("pool")
    group_index = lax.axis_index("grp")
    lane = lax.axis_index("tp")
    prompts = prompt_query.shape[0]
    prompt_len = prompt_states.shape[0] // prompts
    seq_count, steps, query_width = seq_query.shape
    width = prompt_next.shape[2]
    quad = QUAD

    share = quad * width // groups
    start = ((lane ^ 4) // quad * quad) * width + group_index * share
    weight_share = jnp.concatenate(
        [
            lax.dynamic_slice_in_dim(key_weight, start, share, 0),
            lax.dynamic_slice_in_dim(value_weight, start, share, 0),
        ],
        axis=1,
    )
    received_share = exchange(weight_share, "tp", 4)
    partner_weight = spread(received_share)
    gain = key_gain.reshape(1, HD)
    instance = pool_index * groups + group_index
    lengths = lax.dynamic_index_in_dim(prompt_lengths, instance, 0, keepdims=False)
    ends = jnp.cumsum(lengths)
    position = jnp.arange(prompt_len)[None, :]
    place = jnp.where(position < lengths[:, None], (ends - lengths)[:, None] + position, -1)
    place = place.reshape(1, prompts * prompt_len).astype(jnp.int32)
    prompt_owners = jnp.sum(ends[:, None] <= jnp.arange(kept)[None, :], axis=0, dtype=jnp.int32)
    prompt_owners = prompt_owners.reshape(1, kept)
    context = cache_kv.shape[2]
    seq_owners = jnp.where(
        jnp.arange(context)[None, :] < context_lengths[:, None],
        jnp.arange(seq_count, dtype=jnp.int32)[:, None],
        seq_count,
    ).reshape(1, seq_count * context)

    query_rows = prompt_query.reshape(prompts * steps, query_width)
    mine = pack(
        place,
        prompt_states,
        prompt_next.reshape(prompts * steps, width),
        seq_next.reshape(seq_count * steps, width),
        kept,
    )
    mine = pass_on(mine, received_share)
    second = exchange(mine, "tp", 2)
    first = exchange(mine, "tp", 1)
    second = pass_on(second, first)
    third = exchange(second, "tp", 1)
    order = jnp.asarray([0, 1, 2, 3], jnp.int32) ^ (lane % quad)
    own, sent = project(
        [mine, first, second, third],
        order,
        lane // quad * quad + order,
        (key_weight, value_weight, partner_weight),
    )
    got = exchange(sent, "tp", 4)
    result = prompt_attention(own, got, gain, prompt_owners, query_rows, steps)
    crossed = exchange(result, "pool", 1)
    seq_output = cached_attention(
        own,
        got,
        gain,
        seq_owners,
        seq_query.reshape(seq_count * steps, query_width),
        cache_kv,
        steps,
    ).reshape(seq_count, steps, query_width)

    source = (pool_index ^ 1) * groups + group_index
    targets = lax.dynamic_index_in_dim(prompt_target[:, :, 0], source, 0, keepdims=False)
    places = targets * MOST + rank_within(targets)
    place_rows = (places[:, None] * steps + jnp.arange(steps)[None, :]).reshape(-1)
    chooser = (jnp.arange(groups * MOST * steps)[:, None] == place_rows[None, :]).astype(
        jnp.bfloat16
    )
    outgoing = jnp.dot(chooser, crossed, preferred_element_type=jnp.float32).astype(jnp.bfloat16)
    arrived = lax.all_to_all(outgoing, "grp", split_axis=0, concat_axis=0, tiled=True)
    return seq_output, arrived.reshape(1, groups * MOST, steps, query_width)


def on_device(*arrays):
    rows = arrays[0].shape[0]
    most = jnp.max(jnp.sum(arrays[1], axis=1))
    sizes = [size for size in BUCKETS if size < rows] + [rows]
    choice = sum((most > size).astype(jnp.int32) for size in sizes[:-1])
    return lax.switch(choice, [functools.partial(run, size) for size in sizes], *arrays)


def solution(mesh):
    return jax.shard_map(
        on_device,
        mesh=mesh,
        in_specs=(
            P(("pool", "grp"), "tp"),
            P(),
            P(),
            P(("pool", "grp"), None, "tp"),
            P(("pool", "grp"), None, "tp"),
            P(None, "tp"),
            P(None, "tp"),
            P(),
            P(("pool", "grp"), None, "tp"),
            P(("pool", "grp"), None, "tp"),
            P(("pool", "grp"), None, None, "tp"),
            P(("pool", "grp")),
        ),
        out_specs=(P(("pool", "grp"), None, "tp"), P(("pool", "grp"), None, None, "tp")),
        check_vma=False,
    )
```

time: 189 us -> 168 us (0.89)
  between operations: 15.2 us -> 1.29 us
  starting transfers between devices: 59.5 us -> 48.8 us
  matrix products: 8 us -> 1.08 us
  Pallas kernels: 3.38 us -> 8.76 us
    ppermute x6, waiting for transfers between devices: 63.3 us -> 82.1 us  [exchange(): return lax.ppermute(block, axis, [(i, i ^ apart) for i in range(size)])]
    ppermute x6, starting transfers between devices: 50.5 us -> 32.7 us  [exchange(): return lax.ppermute(block, axis, [(i, i ^ apart) for i in range(size)])]
    all_gather x1 -> x0, waiting for transfers between devices: 17.2 us -> none  [on_device(): lax.all_gather(exchange(weight_share, 'tp', 4), 'grp', axis=0, tiled=True)]
    all_to_all x1 -> x2, starting transfers between devices: 8.93 us -> 16.2 us  [the longest x1 8.6 us: spread(): lax.all_to_all(copies, 'grp', split_axis=0, concat_axis=0, tiled=True)]
    dot_general x9 -> x1, matrix products: 8 us -> 1.08 us  [run(): jnp.dot(chooser, crossed, preferred_element_type=jnp.float32)]
    pallas_call x2 -> x6, Pallas kernels: 3.38 us -> 8.76 us  [the longest x1 4.47 us: project(): pl.pallas_call(project_kernel, grid_spec=pltpu.PrefetchScalarGridSpec(num...]
    dynamic_slice x5 -> x1, local copies, waits for them, and re-layouts: 5.3 us -> 0.75 us  [run(): lax.dynamic_slice_in_dim(value_weight, start, share, 0)]
    cond x0 -> x25, local copies, waits for them, and re-layouts: none -> 4.54 us
  transfers between devices with their start and end apart: 8 -> 8, of which waited for: 6 -> 6; matrix products, arithmetic and copies ran while one was open for 7% -> 4% of each run, Pallas kernels for 0% -> 1%
where the time goes in v2:
time: 168 us; the launch traced here: 167 us
  waiting for transfers between devices  92.2 us (55%)
  starting transfers between devices  48.8 us (29%)
  local copies, waits for them, and re-layouts  12.8 us (8%)
  Pallas kernels  8.76 us (5%)
  other arithmetic  2.07 us (1%)
    ppermute x6, waiting for transfers between devices, exchange(): return lax.ppermute(block, axis, [(i, i ^ apart) for i in range(size)])  82.1 us
    ppermute x6, starting transfers between devices, exchange(): return lax.ppermute(block, axis, [(i, i ^ apart) for i in range(size)])  32.7 us
    all_to_all x1, waiting for transfers between devices, run(): lax.all_to_all(outgoing, 'grp', split_axis=0, concat_axis=0, tiled=True)  10.2 us
    all_to_all x1, starting transfers between devices, spread(): lax.all_to_all(copies, 'grp', split_axis=0, concat_axis=0, tiled=True)  8.6 us
    all_to_all x1, starting transfers between devices, run(): lax.all_to_all(outgoing, 'grp', split_axis=0, concat_axis=0, tiled=True)  7.56 us
    cond x25, local copies, waits for them, and re-layouts  4.54 us
    pallas_call x1, Pallas kernels, project(): pl.pallas_call(project_kernel, grid_spec=pltpu.PrefetchScalarGridSpec(num...  4.47 us
  transfers between devices with their start and end apart: 8, of which 6 were waited for; matrix products, arithmetic and copies ran while one was open for 4% of the time, Pallas kernels for 1%

profile of v2, /device:TPU:1, one launch (start us, length us, event | category | flops | bytes accessed | tf_op | source)
XLA Modules:
  0.0 167.3 jit_solution(8321864178505884239)
XLA Ops:
  0.6 0.7 reduce_sum.45
  1.4 0.6 reduce_max.9
  2.7 164.7 %conditional.1 = (bf16[4,4,1024]{2,1,0:T(4,128)(2,1)}, bf16[1,64,4,1024]{3,2,1,0:T(4,128)(2,1)}) conditional(s32[]{:T(128)} %clamp.3, (s32[4]{0:T(128)S(1)}, s32[64,32]{0,1:T(8,128)}, bf16[32,4,640]{2,1,0:T(4,128)(2,1)}, bf16[4,4,640]{2,1,0:T(4,128)(2,1)}, bf16[512,640]{1,0:T(8,128)(2,1)}, /*index=5*/bf16[5120,128]{1,0:T(8,128)(2,1)}, ...), branch_computations={%region_2.6_spmd, %region_6.10_spmd} | conditional | flops 3787208704 | bytes 56855816 | solution.py:343
  2.7 0.8 constant_dynamic-slice_fusion.1
  3.5 9.6 %collective-permute-start = (bf16[80,256]{1,0:T(8,128)(2,1)S(1)}, bf16[80,256]{1,0:T(8,128)(2,1)S(1)}, u32[]{:S(2)}, u32[]{:S(2)}) collective-permute-start(bf16[80,256]{1,0:T(8,128)(2,1)S(1)} %pad_maximum_fusion), channel_id=1, source_target_pairs={{0,4},{1,5},{2,6},{3,7},{4,0},{5,1},{6,2},{7,3},{8,12},{9,13},{10,... | collective-permute-start | bytes 122888 | tf_op jit(solution)/shard_map/cond/branch_0_fun/ppermute | solution.py:22
  13.1 0.8 copy.62
  14.0 0.1 copy.60
  14.0 0.1 reduce-window.12
  14.1 0.1 reduce
  14.2 0.1 add_select_fusion
  14.3 0.1 select_n.83.place
  14.4 1.0 reshape.336.nexts
  15.4 0.7 reshape.337.sequences
  16.1 1.6 pack.2.block_ref
  17.7 0.0 copy-start.2
  17.7 0.8 copy-done.2
  18.5 0.0 collective-permute-done.awaited_ref
  18.5 0.0 copy-start.13
  18.5 0.6 copy-done.13
  19.2 3.5 %collective-permute-start.1 = (bf16[528,640]{1,0:T(8,128)(2,1)}, bf16[528,640]{1,0:T(8,128)(2,1)S(1)}, u32[]{:S(2)}, u32[]{:S(2)}) collective-permute-start(bf16[528,640]{1,0:T(8,128)(2,1)} %pass_on.4.refs_0_), channel_id=1, source_target_pairs={{0,1},{1,0},{2,3},{3,2},{4,5},{5,4},{6,7},{7,6},{8,9},{9,8},{10,11... | collective-permute-start | bytes 2027528 | tf_op jit(solution)/shard_map/cond/branch_0_fun/ppermute | solution.py:22
  22.7 4.9 %collective-permute-start.2 = (bf16[528,640]{1,0:T(8,128)(2,1)}, bf16[528,640]{1,0:T(8,128)(2,1)S(1)}, u32[]{:S(2)}, u32[]{:S(2)}) collective-permute-start(bf16[528,640]{1,0:T(8,128)(2,1)} %pass_on.4.refs_0_), channel_id=1, source_target_pairs={{0,2},{1,3},{2,0},{3,1},{4,6},{5,7},{6,4},{7,5},{8,10},{9,11},{10,... | collective-permute-start | bytes 2027528 | tf_op jit(solution)/shard_map/cond/branch_0_fun/ppermute | solution.py:22
  27.6 1.9 %broadcast_in_dim.24 = bf16[32,80,256]{2,1,0:T(8,128)(2,1)} broadcast(bf16[80,256]{1,0:T(8,128)(2,1)} %copy-done.13), dimensions={1,2} | broadcast | bytes 1351680 | tf_op jit(solution)/shard_map/cond/branch_0_fun/broadcast_in_dim | solution.py:170
  29.5 8.6 %all-to-all-start = ((bf16[32,80,256]{2,1,0:T(8,128)(2,1)}), bf16[32,80,256]{2,1,0:T(8,128)(2,1)S(1)}, u32[]{:S(2)}, u32[]{:S(2)}) async-start(bf16[32,80,256]{2,1,0:T(8,128)(2,1)} %broadcast_in_dim.24), calls=%async_computation | async-start | bytes 2621440 | tf_op jit(solution)/shard_map/cond/branch_0_fun/all_to_all | solution.py:171
  38.2 0.0 copy-start.3
  38.2 10.4 %collective-permute-done.1.awaited_ref.refs_1_ = bf16[528,640]{1,0:T(8,128)(2,1)S(1)} collective-permute-done((bf16[528,640]{1,0:T(8,128)(2,1)}, bf16[528,640]{1,0:T(8,128)(2,1)S(1)}, u32[]{:S(2)}, u32[]{:S(2)}) %collective-permute-start.1) | collective-permute-done | bytes 675872 | tf_op jit(solution)/shard_map/cond/branch_0_fun/ppermute | solution.py:22
  48.6 0.0 copy-start.6
  48.6 8.0 %collective-permute-done.2.block_ref = bf16[528,640]{1,0:T(8,128)(2,1)S(1)} collective-permute-done((bf16[528,640]{1,0:T(8,128)(2,1)}, bf16[528,640]{1,0:T(8,128)(2,1)S(1)}, u32[]{:S(2)}, u32[]{:S(2)}) %collective-permute-start.2) | collective-permute-done | bytes 675872 | tf_op jit(solution)/shard_map/cond/branch_0_fun/ppermute | solution.py:22
  56.6 0.0 copy-done.6
  56.6 0.0 copy-start.8
  56.6 0.8 copy-done.8
  57.5 1.9 %collective-permute-start.3 = (bf16[528,640]{1,0:T(8,128)(2,1)}, bf16[528,640]{1,0:T(8,128)(2,1)S(1)}, u32[]{:S(2)}, u32[]{:S(2)}) collective-permute-start(bf16[528,640]{1,0:T(8,128)(2,1)} %pass_on.5.refs_2_), channel_id=1, source_target_pairs={{0,1},{1,0},{2,3},{3,2},{4,5},{5,4},{6,7},{7,6},{8,9},{9,8},{10,11... | collective-permute-start | bytes 2027528 | tf_op jit(solution)/shard_map/cond/branch_0_fun/ppermute | solution.py:22
  59.4 0.0 all-to-all-done
  59.4 15.0 %collective-permute-done.3.refs_3_ = bf16[528,640]{1,0:T(8,128)(2,1)S(1)} collective-permute-done((bf16[528,640]{1,0:T(8,128)(2,1)}, bf16[528,640]{1,0:T(8,128)(2,1)S(1)}, u32[]{:S(2)}, u32[]{:S(2)}) %collective-permute-start.3) | collective-permute-done | bytes 675872 | tf_op jit(solution)/shard_map/cond/branch_0_fun/ppermute | solution.py:22
  74.4 0.0 copy-done.3
  74.4 0.0 copy-start.7
  74.4 1.1 copy-done.7
  75.5 1.1 copy-done.9
  76.6 4.5 %project.2 = (f32[528,256]{1,0:T(8,128)S(1)}, bf16[528,256]{1,0:T(8,128)(2,1)S(1)}) custom-call(s32[4]{0:T(128)S(1)} %get-tuple-element.215.order, s32[4]{0:T(128)S(1)} %get-tuple-element.214.block_number, bf16[528,640]{1,0:T(8,128)(2,1)S(1)} %copy-done.3, bf16[528,640]{1,0:T(8,128)(2,1)S(1)} %copy-done.7, bf16[528,640]{1,0:T(8,128)(2,1)S(1)} %copy-done.9, ...), custom_call_target="tpu_custom_call" | custom-call | flops 1384120320 | bytes 8000000 | tf_op jit(solution)/shard_map/cond/branch_0_fun/project/pallas_call | solution.py:200
  81.1 6.1 %collective-permute-start.4 = (bf16[528,256]{1,0:T(8,128)(2,1)S(1)}, bf16[528,256]{1,0:T(8,128)(2,1)S(1)}, u32[]{:S(2)}, u32[]{:S(2)}) collective-permute-start(bf16[528,256]{1,0:T(8,128)(2,1)S(1)} %get-tuple-element.60), channel_id=1, source_target_pairs={{0,4},{1,5},{2,6},{3,7},{4,0},{5,1},{6,2},{7,3},{8,12},{9,13},{10,... | collective-permute-start | bytes 811016 | tf_op jit(solution)/shard_map/cond/branch_0_fun/ppermute | solution.py:22
  87.2 0.1 convert_reduce_fusion
  87.4 1.0 reshape.343.query
  88.4 0.0 copy-done.17
  88.4 0.1 copy.63
  88.5 0.2 convert_reduce_fusion.1
  88.6 24.0 %collective-permute-done.4.got_new.got = bf16[528,256]{1,0:T(8,128)(2,1)S(1)} collective-permute-done((bf16[528,256]{1,0:T(8,128)(2,1)S(1)}, bf16[528,256]{1,0:T(8,128)(2,1)S(1)}, u32[]{:S(2)}, u32[]{:S(2)}) %collective-permute-start.4) | collective-permute-done | bytes 270368 | tf_op jit(solution)/shard_map/cond/branch_0_fun/ppermute | solution.py:22
  112.7 0.0 copy-done.25
  112.7 2.0 %prompt_attention.2 = bf16[128,1024]{1,0:T(8,128)(2,1)S(1)} custom-call(f32[528,256]{1,0:T(8,128)S(1)} %get-tuple-element.59.own_new.own, bf16[528,256]{1,0:T(8,128)(2,1)S(1)} %collective-permute-done.4.got_new.got, f32[1,128]{1,0:T(1,128)S(1)} %bitcast.42, s32[1,384]{1,0:T(1,128)S(1)} %reshape.342.owners, bf16[128,1024]{1,0:T(8,128)(2,1)S(1)} %reshape.343.query), custom_call_target="tpu_custom_call" | custom-call | flops 1000000000 | bytes 2000000 | tf_op jit(solution)/shard_map/cond/branch_0_fun/prompt_attention/pallas_call | solution.py:117
  114.7 0.0 copy-start.15
  114.7 0.0 copy-start.19
  114.7 0.0 copy-start.23
  114.7 6.5 %collective-permute-start.5 = (bf16[128,1024]{1,0:T(8,128)(2,1)S(1)}, bf16[128,1024]{1,0:T(8,128)(2,1)S(1)}, u32[]{:S(2)}, u32[]{:S(2)}) collective-permute-start(bf16[128,1024]{1,0:T(8,128)(2,1)S(1)} %prompt_attention.2), channel_id=1, source_target_pairs={{0,256},{256,0},{1,257},{257,1},{2,258},{258,2},{3,259},{259,3},{4... | collective-permute-start | bytes 786440 | tf_op jit(solution)/shard_map/cond/branch_0_fun/ppermute | solution.py:22
  121.3 0.1 iota_add_fusion
  121.4 0.1 add.137
  121.5 24.6 %collective-permute-done.5 = bf16[128,1024]{1,0:T(8,128)(2,1)S(1)} collective-permute-done((bf16[128,1024]{1,0:T(8,128)(2,1)S(1)}, bf16[128,1024]{1,0:T(8,128)(2,1)S(1)}, u32[]{:S(2)}, u32[]{:S(2)}) %collective-permute-start.5) | collective-permute-done | bytes 262176 | tf_op jit(solution)/shard_map/cond/branch_0_fun/ppermute | solution.py:22
  146.1 1.1 fusion
  147.2 7.6 %all-to-all-start.1 = ((bf16[32,8,1024]{2,1,0:T(8,128)(2,1)}), bf16[32,8,1024]{2,1,0:T(8,128)(2,1)S(1)}, u32[]{:S(2)}, u32[]{:S(2)}) async-start(bf16[32,8,1024]{2,1,0:T(8,128)(2,1)} %fusion), calls=%async_computation.1 | async-start | bytes 1048576 | tf_op jit(solution)/shard_map/cond/branch_0_fun/all_to_all | solution.py:334
  154.7 0.0 copy-done.15
  154.8 0.0 copy-done.19
  154.8 0.1 select_bitcast_fusion
  154.9 0.0 copy-done.23
  154.9 0.7 cached_attention.2
  155.6 0.6 reshape.341
  156.2 10.2 %all-to-all-done.1 = bf16[32,8,1024]{2,1,0:T(8,128)(2,1)S(1)} async-done(((bf16[32,8,1024]{2,1,0:T(8,128)(2,1)}), bf16[32,8,1024]{2,1,0:T(8,128)(2,1)S(1)}, u32[]{:S(2)}, u32[]{:S(2)}) %all-to-all-start.1) | async-done | bytes 524320 | tf_op jit(solution)/shard_map/cond/branch_0_fun/all_to_all | solution.py:334
  166.4 1.0 reshape.344
  (15 shorter events, 0.1 us)
Async XLA Ops:
  3.5 15.1 %collective-permute-start = (bf16[80,256]{1,0:T(8,128)(2,1)S(1)}, bf16[80,256]{1,0:T(8,128)(2,1)S(1)}, u32[]{:S(2)}, u32[]{:S(2)}) collective-permute-start(bf16[80,256]{1,0:T(8,128)(2,1)S(1)} %pad_maximum_fusion), channel_id=1, source_target_pairs={{0,4},{1,5},{2,6},{3,7},{4,0},{5,1},{6,2},{7,3},{8,12},{9,13},{10,... | collective-permute-start | bytes 122888 | tf_op jit(solution)/shard_map/cond/branch_0_fun/ppermute | solution.py:22
  17.7 0.9 copy-start.2
  18.5 0.6 copy-start.13
  19.2 29.4 %collective-permute-start.1 = (bf16[528,640]{1,0:T(8,128)(2,1)}, bf16[528,640]{1,0:T(8,128)(2,1)S(1)}, u32[]{:S(2)}, u32[]{:S(2)}) collective-permute-start(bf16[528,640]{1,0:T(8,128)(2,1)} %pass_on.4.refs_0_), channel_id=1, source_target_pairs={{0,1},{1,0},{2,3},{3,2},{4,5},{5,4},{6,7},{7,6},{8,9},{9,8},{10,11... | collective-permute-start | bytes 2027528 | tf_op jit(solution)/shard_map/cond/branch_0_fun/ppermute | solution.py:22
  22.7 33.9 %collective-permute-start.2 = (bf16[528,640]{1,0:T(8,128)(2,1)}, bf16[528,640]{1,0:T(8,128)(2,1)S(1)}, u32[]{:S(2)}, u32[]{:S(2)}) collective-permute-start(bf16[528,640]{1,0:T(8,128)(2,1)} %pass_on.4.refs_0_), channel_id=1, source_target_pairs={{0,2},{1,3},{2,0},{3,1},{4,6},{5,7},{6,4},{7,5},{8,10},{9,11},{10,... | collective-permute-start | bytes 2027528 | tf_op jit(solution)/shard_map/cond/branch_0_fun/ppermute | solution.py:22
  29.5 29.9 %all-to-all-start = ((bf16[32,80,256]{2,1,0:T(8,128)(2,1)}), bf16[32,80,256]{2,1,0:T(8,128)(2,1)S(1)}, u32[]{:S(2)}, u32[]{:S(2)}) async-start(bf16[32,80,256]{2,1,0:T(8,128)(2,1)} %broadcast_in_dim.24), calls=%async_computation | async-start | bytes 2621440 | tf_op jit(solution)/shard_map/cond/branch_0_fun/all_to_all | solution.py:171
  38.2 36.3 %copy-start.3 = (bf16[528,640]{1,0:T(8,128)(2,1)S(1)}, bf16[528,640]{1,0:T(8,128)(2,1)}, u32[]{:S(2)}) copy-start(bf16[528,640]{1,0:T(8,128)(2,1)} %pass_on.4.refs_0_) | copy-start | bytes 2027524 | tf_op jit(solution)/shard_map/cond
  48.6 8.0 %copy-start.6 = (bf16[528,640]{1,0:T(8,128)(2,1)}, bf16[528,640]{1,0:T(8,128)(2,1)S(1)}, u32[]{:S(2)}) copy-start(bf16[528,640]{1,0:T(8,128)(2,1)S(1)} %collective-permute-done.1.awaited_ref.refs_1_) | copy-start | bytes 2027524 | tf_op jit(solution)/shard_map/cond
  56.6 0.8 copy-start.8
  57.5 16.9 %collective-permute-start.3 = (bf16[528,640]{1,0:T(8,128)(2,1)}, bf16[528,640]{1,0:T(8,128)(2,1)S(1)}, u32[]{:S(2)}, u32[]{:S(2)}) collective-permute-start(bf16[528,640]{1,0:T(8,128)(2,1)} %pass_on.5.refs_2_), channel_id=1, source_target_pairs={{0,1},{1,0},{2,3},{3,2},{4,5},{5,4},{6,7},{7,6},{8,9},{9,8},{10,11... | collective-permute-start | bytes 2027528 | tf_op jit(solution)/shard_map/cond/branch_0_fun/ppermute | solution.py:22
  74.4 1.1 copy-start.7
  75.5 1.1 copy-start.9
  76.6 11.8 %copy-start.17 = (s32[64,32,1]{0,2,1:T(1,128)S(1)}, s32[64,32,1]{0,2,1:T(1,128)}, u32[]{:S(2)}) copy-start(s32[64,32,1]{0,2,1:T(1,128)} %get-tuple-element.197) | copy-start | bytes 24580 | tf_op jit(solution)/shard_map/cond
  76.6 36.1 %copy-start.25 = (f32[128]{0:T(128)S(1)}, f32[128]{0:T(128)}, u32[]{:S(2)}) copy-start(f32[128]{0:T(128)} %get-tuple-element.122) | copy-start | bytes 1540 | tf_op jit(solution)/shard_map/cond
  81.1 31.6 %collective-permute-start.4 = (bf16[528,256]{1,0:T(8,128)(2,1)S(1)}, bf16[528,256]{1,0:T(8,128)(2,1)S(1)}, u32[]{:S(2)}, u32[]{:S(2)}) collective-permute-start(bf16[528,256]{1,0:T(8,128)(2,1)S(1)} %get-tuple-element.60), channel_id=1, source_target_pairs={{0,4},{1,5},{2,6},{3,7},{4,0},{5,1},{6,2},{7,3},{8,12},{9,13},{10,... | collective-permute-start | bytes 811016 | tf_op jit(solution)/shard_map/cond/branch_0_fun/ppermute | solution.py:22
  114.7 40.0 %copy-start.15 = (bf16[4,4,1024]{2,1,0:T(4,128)(2,1)S(1)}, bf16[4,4,1024]{2,1,0:T(4,128)(2,1)}, u32[]{:S(2)}) copy-start(bf16[4,4,1024]{2,1,0:T(4,128)(2,1)} %get-tuple-element.126) | copy-start | bytes 98308 | tf_op jit(solution)/shard_map/cond
  114.7 40.0 %copy-start.19 = (s32[4]{0:T(128)S(1)}, s32[4]{0:T(128)}, u32[]{:S(2)}) copy-start(s32[4]{0:T(128)} %get-tuple-element.124) | copy-start | bytes 52 | tf_op jit(solution)/shard_map/cond
  114.7 40.1 %copy-start.23 = (bf16[4,2,256,128]{3,2,1,0:T(8,128)(2,1)S(1)}, bf16[4,2,256,128]{3,2,1,0:T(8,128)(2,1)}, u32[]{:S(2)}) copy-start(bf16[4,2,256,128]{3,2,1,0:T(8,128)(2,1)} %get-tuple-element.128.cache) | copy-start | bytes 1572868 | tf_op jit(solution)/shard_map/cond
  114.7 31.3 %collective-permute-start.5 = (bf16[128,1024]{1,0:T(8,128)(2,1)S(1)}, bf16[128,1024]{1,0:T(8,128)(2,1)S(1)}, u32[]{:S(2)}, u32[]{:S(2)}) collective-permute-start(bf16[128,1024]{1,0:T(8,128)(2,1)S(1)} %prompt_attention.2), channel_id=1, source_target_pairs={{0,256},{256,0},{1,257},{257,1},{2,258},{258,2},{3,259},{259,3},{4... | collective-permute-start | bytes 786440 | tf_op jit(solution)/shard_map/cond/branch_0_fun/ppermute | solution.py:22
  147.2 19.2 %all-to-all-start.1 = ((bf16[32,8,1024]{2,1,0:T(8,128)(2,1)}), bf16[32,8,1024]{2,1,0:T(8,128)(2,1)S(1)}, u32[]{:S(2)}, u32[]{:S(2)}) async-start(bf16[32,8,1024]{2,1,0:T(8,128)(2,1)} %fusion), calls=%async_computation.1 | async-start | bytes 1048576 | tf_op jit(solution)/shard_map/cond/branch_0_fun/all_to_all | solution.py:334

commit v3 on v2

--- a/solution.py
+++ b/solution.py
@@ -14,7 +14,7 @@
 MASKED_SCORE = -1e30
 GROUP = 8
 QUAD = 4
-BUCKETS = (384,)
+BUCKETS = (336, 352, 368, 384)
 
 
 def exchange(block, axis, apart):
@@ -71,18 +71,20 @@
 
 
 def pack_kernel(place, states, nexts, sequences, packed):
-    kept = packed.shape[0] - nexts.shape[0] - sequences.shape[0]
+    next_rows = nexts[...].reshape(-1, packed.shape[1])
+    sequence_rows = sequences[...].reshape(-1, packed.shape[1])
+    kept = packed.shape[0] - next_rows.shape[0] - sequence_rows.shape[0]
     row = lax.broadcasted_iota(jnp.int32, (kept, place.shape[1]), 0)
     chooser = (row == place[...]).astype(jnp.float32).astype(jnp.bfloat16)
     live = jnp.dot(chooser, states[...], preferred_element_type=jnp.float32)
     packed[:kept, :] = live.astype(jnp.bfloat16)
-    packed[kept : kept + nexts.shape[0], :] = nexts[...]
-    packed[kept + nexts.shape[0] :, :] = sequences[...]
+    packed[kept : kept + next_rows.shape[0], :] = next_rows
+    packed[kept + next_rows.shape[0] :, :] = sequence_rows
 
 
 def pack(place, states, nexts, sequences, kept):
     whole = pl.BlockSpec(memory_space=pltpu.VMEM)
-    rows = kept + nexts.shape[0] + sequences.shape[0]
+    rows = kept + nexts.shape[0] * nexts.shape[1] + sequences.shape[0] * sequences.shape[1]
     return pl.pallas_call(
         pack_kernel,
         in_specs=[whole] * 4,
@@ -96,8 +98,9 @@
 def prompt_kernel(steps, own, got, gain, owners, query, out):
     kept = owners.shape[1]
     count = query.shape[0]
-    old_keys, old_values = finish(own[:kept], got[:kept], gain[...])
-    new_keys, new_values = finish(own[kept : kept + count], got[kept : kept + count], gain[...])
+    keys, values = finish(own[: kept + count], got[: kept + count], gain[...])
+    old_keys, old_values = keys[:kept], values[:kept]
+    new_keys, new_values = keys[kept:], values[kept:]
     rows = GROUP * steps
     for first in range(0, count, rows):
         attend(
@@ -172,16 +175,16 @@
     return arrived.reshape(-1, share.shape[1])
 
 
-def project_kernel(order, block_number, *refs):
-    features, (key_block, value_block, partner_block, own, sent, total) = refs[:-6], refs[-6:]
+def multiply_kernel(count, order, block_number, *refs):
+    features, weights, (begun, result, total) = refs[:count], refs[count:-3], refs[-3:]
     k = pl.program_id(0)
 
     @pl.when(k == 0)
     def _():
-        total[...] = jnp.zeros_like(total)
+        total[...] = jnp.broadcast_to(begun[...], total.shape)
 
     def add(block):
-        weight = jnp.concatenate([key_block[...], value_block[...], partner_block[...]], axis=1)
+        weight = jnp.concatenate([block_ref[...] for block_ref in weights], axis=1)
         total[...] += jnp.dot(block[...], weight, preferred_element_type=jnp.float32)
 
     for index, block in enumerate(features):
@@ -189,37 +192,40 @@
 
     @pl.when(k == pl.num_programs(0) - 1)
     def _():
-        own[...] = total[:, : 2 * HD]
-        sent[...] = total[:, 2 * HD :].astype(jnp.bfloat16)
-
-
-def project(features, order, block_number, weights):
+        result[...] = total[...].astype(result.dtype)
+
+
+def multiply(begun, features, order, block_number, weights, by_block, dtype):
     rows, width = features[0].shape
-    own_spec = pl.BlockSpec((width, HD), lambda k, o, b: (b[k], 0))
-    whole = pl.BlockSpec((rows, 2 * HD), lambda k, o, b: (0, 0))
-    return pl.pallas_call(
-        project_kernel,
+    columns = begun.shape[1]
+    number = lambda o, b, k: b[k] if by_block else o[k]
+    whole = lambda *shape: pl.BlockSpec(shape, lambda k, o, b: (0, 0))
+    return pl.pallas_call(
+        functools.partial(multiply_kernel, len(features)),
         grid_spec=pltpu.PrefetchScalarGridSpec(
             num_scalar_prefetch=2,
-            grid=(QUAD,),
-            in_specs=[pl.BlockSpec((rows, width), lambda k, o, b: (0, 0))] * QUAD
-            + [own_spec, own_spec, pl.BlockSpec((width, 2 * HD), lambda k, o, b: (o[k], 0))],
-            out_specs=[whole, whole],
-            scratch_shapes=[pltpu.VMEM((rows, 4 * HD), jnp.float32)],
+            grid=(len(features),),
+            in_specs=[whole(rows, width)] * len(features)
+            + [
+                pl.BlockSpec((width, weight.shape[1]), lambda k, o, b: (number(o, b, k), 0))
+                for weight in weights
+            ]
+            + [whole(rows if begun.shape[0] == rows else 1, columns)],
+            out_specs=whole(rows, columns),
+            scratch_shapes=[pltpu.VMEM((rows, columns), jnp.float32)],
         ),
-        out_shape=[
-            jax.ShapeDtypeStruct((rows, 2 * HD), jnp.float32),
-            jax.ShapeDtypeStruct((rows, 2 * HD), jnp.bfloat16),
-        ],
-        compiler_params=pltpu.CompilerParams(vmem_limit_bytes=32 * 2**20),
+        out_shape=jax.ShapeDtypeStruct((rows, columns), dtype),
+        compiler_params=pltpu.CompilerParams(vmem_limit_bytes=24 * 2**20),
         cost_estimate=pl.CostEstimate(
-            flops=2 * rows * width * QUAD * 4 * HD, bytes_accessed=8 * 10**6, transcendentals=0
+            flops=2 * len(features) * rows * width * columns,
+            bytes_accessed=2 * 10**6,
+            transcendentals=0,
         ),
-        name="project",
-    )(order, block_number, *features, *weights)
-
-
-def pass_on(block, awaited):
+        name="multiply",
+    )(order, block_number, *features, *weights, begun)
+
+
+def pass_on(block, awaited, flops=0):
     anywhere = pl.BlockSpec(memory_space=pl.ANY)
     return pl.pallas_call(
         lambda block_ref, awaited_ref, out_ref: None,
@@ -227,6 +233,7 @@
         out_specs=anywhere,
         out_shape=jax.ShapeDtypeStruct(block.shape, block.dtype),
         input_output_aliases={0: 0},
+        cost_estimate=pl.CostEstimate(flops=flops, bytes_accessed=flops // 300, transcendentals=0),
         name="pass_on",
     )(block, awaited)
 
@@ -272,8 +279,6 @@
         ],
         axis=1,
     )
-    received_share = exchange(weight_share, "tp", 4)
-    partner_weight = spread(received_share)
     gain = key_gain.reshape(1, HD)
     instance = pool_index * groups + group_index
     lengths = lax.dynamic_index_in_dim(prompt_lengths, instance, 0, keepdims=False)
@@ -294,23 +299,38 @@
     mine = pack(
         place,
         prompt_states,
-        prompt_next.reshape(prompts * steps, width),
-        seq_next.reshape(seq_count * steps, width),
+        prompt_next,
+        seq_next,
         kept,
     )
+    received_share = exchange(pass_on(weight_share, mine), "tp", 4)
+    partner_weight = spread(received_share)
+
+    order = jnp.asarray([0, 1, 2, 3], jnp.int32) ^ (lane % quad)
+    block_number = lane // quad * quad + order
     mine = pass_on(mine, received_share)
     second = exchange(mine, "tp", 2)
     first = exchange(mine, "tp", 1)
-    second = pass_on(second, first)
+    second = pass_on(second, first, 8000000000)
     third = exchange(second, "tp", 1)
-    order = jnp.asarray([0, 1, 2, 3], jnp.int32) ^ (lane % quad)
-    own, sent = project(
-        [mine, first, second, third],
+    blank = jnp.zeros((1, 2 * HD), jnp.float32)
+    near = (mine, first, second)
+    begun = multiply(
+        blank, near, order[:3], block_number[:3], [partner_weight], False, jnp.float32
+    )
+    sent = multiply(
+        begun, [third], order[3:], block_number[3:], [partner_weight], False, jnp.bfloat16
+    )
+    got = exchange(sent, "tp", 4)
+    own = multiply(
+        blank,
+        near + (third,),
         order,
-        lane // quad * quad + order,
-        (key_weight, value_weight, partner_weight),
-    )
-    got = exchange(sent, "tp", 4)
+        block_number,
+        [key_weight, value_weight],
+        True,
+        jnp.float32,
+    )
     result = prompt_attention(own, got, gain, prompt_owners, query_rows, steps)
     crossed = exchange(result, "pool", 1)
     seq_output = cached_attention(

time: 168 us -> 161 us (0.958)
  waiting for transfers between devices: 92.2 us -> 64.1 us
  starting transfers between devices: 48.8 us -> 67.3 us
  between operations: 1.29 us -> 3.24 us
    ppermute x6, waiting for transfers between devices: 82.1 us -> 53.2 us  [exchange(): return lax.ppermute(block, axis, [(i, i ^ apart) for i in range(size)])]
    ppermute x6, starting transfers between devices: 32.7 us -> 45.3 us  [exchange(): return lax.ppermute(block, axis, [(i, i ^ apart) for i in range(size)])]
    all_to_all x1, starting transfers between devices: 7.56 us -> 13.7 us  [run(): lax.all_to_all(outgoing, 'grp', split_axis=0, concat_axis=0, tiled=True)]
    reshape x2 -> x0, local copies, waits for them, and re-layouts: 1.71 us -> none  [the longest x1 0.97 us: run(): prompt_next.reshape(prompts * steps, width)]
    pallas_call x1 -> x3, Pallas kernels: 4.47 us -> 5.47 us  [multiply(): pl.pallas_call(functools.partial(multiply_kernel, len(features)), grid_sp...]
    cond x25 -> x35, local copies, waits for them, and re-layouts: 4.54 us -> 4.48 us
  transfers between devices with their start and end apart: 8 -> 8, of which waited for: 6 -> 8; matrix products, arithmetic and copies ran while one was open for 4% -> 3% of each run, Pallas kernels for 1% -> 3%
where the time goes in v3:
time: 161 us; the launch traced here: 160 us
  starting transfers between devices  67.3 us (42%)
  waiting for transfers between devices  64.1 us (40%)
  local copies, waits for them, and re-layouts  11.2 us (7%)
  Pallas kernels  9.78 us (6%)
  between operations  3.24 us (2%)
  other arithmetic  2.68 us (2%)
    ppermute x6, waiting for transfers between devices, exchange(): return lax.ppermute(block, axis, [(i, i ^ apart) for i in range(size)])  53.2 us
    ppermute x6, starting transfers between devices, exchange(): return lax.ppermute(block, axis, [(i, i ^ apart) for i in range(size)])  45.3 us
    all_to_all x1, starting transfers between devices, run(): lax.all_to_all(outgoing, 'grp', split_axis=0, concat_axis=0, tiled=True)  13.7 us
    all_to_all x1, waiting for transfers between devices, run(): lax.all_to_all(outgoing, 'grp', split_axis=0, concat_axis=0, tiled=True)  10.2 us
    all_to_all x1, starting transfers between devices, spread(): lax.all_to_all(copies, 'grp', split_axis=0, concat_axis=0, tiled=True)  8.31 us
    pallas_call x3, Pallas kernels, multiply(): pl.pallas_call(functools.partial(multiply_kernel, len(features)), grid_sp...  5.47 us
    cond x35, local copies, waits for them, and re-layouts  4.48 us
  transfers between devices with their start and end apart: 8, of which 8 were waited for; matrix products, arithmetic and copies ran while one was open for 3% of the time, Pallas kernels for 3%

profile of v3, /device:TPU:1, one launch (start us, length us, event | category | flops | bytes accessed | tf_op | source)
XLA Modules:
  0.0 159.8 jit_solution(1727100562268135427)
XLA Ops:
  0.6 0.7 reduce_sum.99
  1.4 0.6 reduce_max.9
  4.6 155.2 %conditional.1 = (bf16[4,4,1024]{2,1,0:T(4,128)(2,1)}, bf16[1,64,4,1024]{3,2,1,0:T(4,128)(2,1)}) conditional(s32[]{:T(128)} %clamp.3, (s32[4]{0:T(128)S(1)}, s32[64,32]{0,1:T(8,128)}, bf16[512,640]{1,0:T(8,128)(2,1)}, bf16[32,4,640]{2,1,0:T(4,128)(2,1)}, bf16[4,4,640]{2,1,0:T(4,128)(2,1)}, ...), branch_computations={%region_2.6_spmd, %region_6.10_spmd, %region_10.14_spmd, %region_1... | conditional | flops 11787207680 | bytes 90364992 | solution.py:363
  4.7 0.8 copy.139
  5.5 0.1 copy.134
  5.6 0.1 reduce-window.30
  5.6 0.1 reduce
  5.8 0.1 add_select_fusion
  5.8 0.1 select_n.191.place
  5.9 0.8 constant_dynamic-slice_fusion.1
  6.7 0.6 pad_maximum_fusion.block_ref
  7.3 1.6 %pack.5.awaited_ref.block_ref = bf16[480,640]{1,0:T(8,128)(2,1)S(1)} custom-call(s32[1,512]{1,0:T(1,128)S(1)} %select_n.191.place, bf16[512,640]{1,0:T(8,128)(2,1)} %get-tuple-element.264.states, bf16[32,4,640]{2,1,0:T(4,128)(2,1)} %get-tuple-element.269.nexts, bf16[4,4,640]{2,1,0:T(4,128)(2,1)} %get-tuple-element.274.sequences), custom_call_target="tpu_custom_call" | custom-call | tf_op jit(solution)/shard_map/cond/branch_0_fun/pack/pallas_call | solution.py:88
  8.9 0.8 copy-done.8
  9.8 9.6 %collective-permute-start = (bf16[80,256]{1,0:T(8,128)(2,1)}, bf16[80,256]{1,0:T(8,128)(2,1)S(1)}, u32[]{:S(2)}, u32[]{:S(2)}) collective-permute-start(bf16[80,256]{1,0:T(8,128)(2,1)} %pass_on.15), channel_id=1, source_target_pairs={{0,4},{1,5},{2,6},{3,7},{4,0},{5,1},{6,2},{7,3},{8,12},{9,13},{10,... | collective-permute-start | bytes 122888 | tf_op jit(solution)/shard_map/cond/branch_0_fun/ppermute | solution.py:22
  19.4 1.6 collective-permute-done.awaited_ref
  21.0 0.6 copy-done.56
  21.6 3.5 %collective-permute-start.1 = (bf16[480,640]{1,0:T(8,128)(2,1)}, bf16[480,640]{1,0:T(8,128)(2,1)S(1)}, u32[]{:S(2)}, u32[]{:S(2)}) collective-permute-start(bf16[480,640]{1,0:T(8,128)(2,1)} %pass_on.16.refs_0_), channel_id=1, source_target_pairs={{0,1},{1,0},{2,3},{3,2},{4,5},{5,4},{6,7},{7,6},{8,9},{9,8},{10,11... | collective-permute-start | bytes 1843208 | tf_op jit(solution)/shard_map/cond/branch_0_fun/ppermute | solution.py:22
  25.2 6.1 %collective-permute-start.2 = (bf16[480,640]{1,0:T(8,128)(2,1)}, bf16[480,640]{1,0:T(8,128)(2,1)S(1)}, u32[]{:S(2)}, u32[]{:S(2)}) collective-permute-start(bf16[480,640]{1,0:T(8,128)(2,1)} %pass_on.16.refs_0_), channel_id=1, source_target_pairs={{0,2},{1,3},{2,0},{3,1},{4,6},{5,7},{6,4},{7,5},{8,10},{9,11},{10,... | collective-permute-start | bytes 1843208 | tf_op jit(solution)/shard_map/cond/branch_0_fun/ppermute | solution.py:22
  31.2 2.0 %broadcast_in_dim.89 = bf16[32,80,256]{2,1,0:T(8,128)(2,1)} broadcast(bf16[80,256]{1,0:T(8,128)(2,1)} %copy-done.56), dimensions={1,2} | broadcast | bytes 1351680 | tf_op jit(solution)/shard_map/cond/branch_0_fun/broadcast_in_dim | solution.py:173
  33.2 8.3 %all-to-all-start = ((bf16[32,80,256]{2,1,0:T(8,128)(2,1)}), bf16[32,80,256]{2,1,0:T(8,128)(2,1)S(1)}, u32[]{:S(2)}, u32[]{:S(2)}) async-start(bf16[32,80,256]{2,1,0:T(8,128)(2,1)} %broadcast_in_dim.89), calls=%async_computation | async-start | bytes 2621440 | tf_op jit(solution)/shard_map/cond/branch_0_fun/all_to_all | solution.py:174
  41.5 0.0 copy-start.43
  41.5 0.0 copy-start.51
  41.5 0.0 copy-start.9
  41.5 3.1 %collective-permute-done.1.awaited_ref.refs_1_ = bf16[480,640]{1,0:T(8,128)(2,1)S(1)} collective-permute-done((bf16[480,640]{1,0:T(8,128)(2,1)}, bf16[480,640]{1,0:T(8,128)(2,1)S(1)}, u32[]{:S(2)}, u32[]{:S(2)}) %collective-permute-start.1) | collective-permute-done | bytes 614432 | tf_op jit(solution)/shard_map/cond/branch_0_fun/ppermute | solution.py:22
  44.7 3.0 %collective-permute-done.2.block_ref = bf16[480,640]{1,0:T(8,128)(2,1)S(1)} collective-permute-done((bf16[480,640]{1,0:T(8,128)(2,1)}, bf16[480,640]{1,0:T(8,128)(2,1)S(1)}, u32[]{:S(2)}, u32[]{:S(2)}) %collective-permute-start.2) | collective-permute-done | bytes 614432 | tf_op jit(solution)/shard_map/cond/branch_0_fun/ppermute | solution.py:22
  47.7 0.8 copy-done.32
  48.5 10.5 %collective-permute-start.3 = (bf16[480,640]{1,0:T(8,128)(2,1)}, bf16[480,640]{1,0:T(8,128)(2,1)S(1)}, u32[]{:S(2)}, u32[]{:S(2)}) collective-permute-start(bf16[480,640]{1,0:T(8,128)(2,1)} %pass_on.17.refs_2_), channel_id=1, source_target_pairs={{0,1},{1,0},{2,3},{3,2},{4,5},{5,4},{6,7},{7,6},{8,9},{9,8},{10,11... | collective-permute-start | bytes 1843208 | tf_op jit(solution)/shard_map/cond/branch_0_fun/ppermute | solution.py:22
  59.1 0.6 slice.40.order
  59.7 0.6 slice.41.block_number
  60.2 0.1 convert_reduce_fusion
  60.3 0.1 reshape.816.query
  60.4 0.0 copy-done.51
  60.4 0.1 copy.140
  60.5 0.8 all-to-all-done
  61.3 0.0 copy-done.9
  61.3 1.1 copy-done.30
  62.4 1.1 copy-done.33
  63.4 1.7 %multiply.26.refs_2_ = f32[480,256]{1,0:T(8,128)S(1)} custom-call(s32[3]{0:T(128)S(1)} %bitcast.112, s32[3]{0:T(128)S(1)} %bitcast.111, bf16[480,640]{1,0:T(8,128)(2,1)S(1)} %copy-done.9, bf16[480,640]{1,0:T(8,128)(2,1)S(1)} %copy-done.30, bf16[480,640]{1,0:T(8,128)(2,1)S(1)} %copy-done.33, bf16[2560,256]{1,0:T(8,128)(2,1)S(1)} %bitcast.101, ...), custom_call_target="tpu_custom_call" | custom-call | flops 471859200 | bytes 2000000 | tf_op jit(solution)/shard_map/cond/branch_0_fun/multiply/pallas_call | solution.py:203
  65.2 0.0 copy-start.31
  65.2 0.0 copy-start.34
  65.2 0.0 copy-start.35
  65.2 4.4 %collective-permute-done.3.refs_3_.refs_0_ = bf16[480,640]{1,0:T(8,128)(2,1)S(1)} collective-permute-done((bf16[480,640]{1,0:T(8,128)(2,1)}, bf16[480,640]{1,0:T(8,128)(2,1)S(1)}, u32[]{:S(2)}, u32[]{:S(2)}) %collective-permute-start.3) | collective-permute-done | bytes 614432 | tf_op jit(solution)/shard_map/cond/branch_0_fun/ppermute | solution.py:22
  69.6 1.7 %multiply.27 = bf16[480,256]{1,0:T(8,128)(2,1)S(1)} custom-call(s32[1]{0:T(128)} %slice.40.order, s32[1]{0:T(128)} %slice.41.block_number, bf16[480,640]{1,0:T(8,128)(2,1)S(1)} %collective-permute-done.3.refs_3_.refs_0_, bf16[2560,256]{1,0:T(8,128)(2,1)S(1)} %bitcast.102, f32[480,256]{1,0:T(8,128)S(1)} %multiply.26.refs_2_), custom_call_target="tpu_custom_call" | custom-call | flops 157286400 | bytes 2000000 | tf_op jit(solution)/shard_map/cond/branch_0_fun/multiply/pallas_call | solution.py:203
  71.3 13.5 %collective-permute-start.4 = (bf16[480,256]{1,0:T(8,128)(2,1)S(1)}, bf16[480,256]{1,0:T(8,128)(2,1)S(1)}, u32[]{:S(2)}, u32[]{:S(2)}) collective-permute-start(bf16[480,256]{1,0:T(8,128)(2,1)S(1)} %multiply.27), channel_id=1, source_target_pairs={{0,4},{1,5},{2,6},{3,7},{4,0},{5,1},{6,2},{7,3},{8,12},{9,13},{10,... | collective-permute-start | bytes 737288 | tf_op jit(solution)/shard_map/cond/branch_0_fun/ppermute | solution.py:22
  84.8 0.2 convert_reduce_fusion.1
  85.0 0.0 copy-done.31
  85.0 0.0 copy-start.77
  85.0 2.1 %multiply.25.own_new.own = f32[480,256]{1,0:T(8,128)S(1)} custom-call(s32[4]{0:T(128)S(1)} %get-tuple-element.517.order, s32[4]{0:T(128)S(1)} %get-tuple-element.516.block_number, bf16[480,640]{1,0:T(8,128)(2,1)S(1)} %copy-done.9, bf16[480,640]{1,0:T(8,128)(2,1)S(1)} %copy-done.31, bf16[480,640]{1,0:T(8,128)(2,1)S(1)} %copy-done.34, ...), custom_call_target="tpu_custom_call" | custom-call | flops 629145600 | bytes 2000000 | tf_op jit(solution)/shard_map/cond/branch_0_fun/multiply/pallas_call | solution.py:203
  87.1 19.8 %collective-permute-done.4.got_new.got = bf16[480,256]{1,0:T(8,128)(2,1)S(1)} collective-permute-done((bf16[480,256]{1,0:T(8,128)(2,1)S(1)}, bf16[480,256]{1,0:T(8,128)(2,1)S(1)}, u32[]{:S(2)}, u32[]{:S(2)}) %collective-permute-start.4) | collective-permute-done | bytes 245792 | tf_op jit(solution)/shard_map/cond/branch_0_fun/ppermute | solution.py:22
  107.0 2.0 %prompt_attention.5 = bf16[128,1024]{1,0:T(8,128)(2,1)S(1)} custom-call(f32[480,256]{1,0:T(8,128)S(1)} %multiply.25.own_new.own, bf16[480,256]{1,0:T(8,128)(2,1)S(1)} %collective-permute-done.4.got_new.got, f32[1,128]{1,0:T(1,128)S(1)} %bitcast.127, s32[1,336]{1,0:T(1,128)S(1)} %reshape.815.owners, bf16[128,1024]{1,0:T(8,128)(2,1)S(1)} %reshape.816.query), custom_call_target="tpu_custom_call" | custom-call | flops 1000000000 | bytes 2000000 | tf_op jit(solution)/shard_map/cond/branch_0_fun/prompt_attention/pallas_call | solution.py:120
  108.9 0.0 copy-start.46
  109.0 0.0 copy-start.61
  109.0 0.0 copy-start.72
  109.0 2.1 %collective-permute-start.5 = (bf16[128,1024]{1,0:T(8,128)(2,1)S(1)}, bf16[128,1024]{1,0:T(8,128)(2,1)S(1)}, u32[]{:S(2)}, u32[]{:S(2)}) collective-permute-start(bf16[128,1024]{1,0:T(8,128)(2,1)S(1)} %prompt_attention.5), channel_id=1, source_target_pairs={{0,256},{256,0},{1,257},{257,1},{2,258},{258,2},{3,259},{259,3},{4... | collective-permute-start | bytes 786440 | tf_op jit(solution)/shard_map/cond/branch_0_fun/ppermute | solution.py:22
  111.1 0.1 iota_add_fusion
  111.1 0.1 add.323
  111.2 21.2 %collective-permute-done.5 = bf16[128,1024]{1,0:T(8,128)(2,1)S(1)} collective-permute-done((bf16[128,1024]{1,0:T(8,128)(2,1)S(1)}, bf16[128,1024]{1,0:T(8,128)(2,1)S(1)}, u32[]{:S(2)}, u32[]{:S(2)}) %collective-permute-start.5) | collective-permute-done | bytes 262176 | tf_op jit(solution)/shard_map/cond/branch_0_fun/ppermute | solution.py:22
  132.5 1.1 fusion
  133.5 13.7 %all-to-all-start.1 = ((bf16[32,8,1024]{2,1,0:T(8,128)(2,1)}), bf16[32,8,1024]{2,1,0:T(8,128)(2,1)S(1)}, u32[]{:S(2)}, u32[]{:S(2)}) async-start(bf16[32,8,1024]{2,1,0:T(8,128)(2,1)} %fusion), calls=%async_computation.1 | async-start | bytes 1048576 | tf_op jit(solution)/shard_map/cond/branch_0_fun/all_to_all | solution.py:354
  147.3 0.1 select_bitcast_fusion
  147.3 0.7 cached_attention.5
  148.0 0.6 reshape.814
  148.7 10.2 %all-to-all-done.1 = bf16[32,8,1024]{2,1,0:T(8,128)(2,1)S(1)} async-done(((bf16[32,8,1024]{2,1,0:T(8,128)(2,1)}), bf16[32,8,1024]{2,1,0:T(8,128)(2,1)S(1)}, u32[]{:S(2)}, u32[]{:S(2)}) %all-to-all-start.1) | async-done | bytes 524320 | tf_op jit(solution)/shard_map/cond/branch_0_fun/all_to_all | solution.py:354
  158.8 1.0 reshape.817
  (29 shorter events, 0.1 us)
Async XLA Ops:
  8.9 0.8 copy-start.8
  9.8 11.2 %collective-permute-start = (bf16[80,256]{1,0:T(8,128)(2,1)}, bf16[80,256]{1,0:T(8,128)(2,1)S(1)}, u32[]{:S(2)}, u32[]{:S(2)}) collective-permute-start(bf16[80,256]{1,0:T(8,128)(2,1)} %pass_on.15), channel_id=1, source_target_pairs={{0,4},{1,5},{2,6},{3,7},{4,0},{5,1},{6,2},{7,3},{8,12},{9,13},{10,... | collective-permute-start | bytes 122888 | tf_op jit(solution)/shard_map/cond/branch_0_fun/ppermute | solution.py:22
  21.0 0.6 copy-start.56
  21.6 23.0 %collective-permute-start.1 = (bf16[480,640]{1,0:T(8,128)(2,1)}, bf16[480,640]{1,0:T(8,128)(2,1)S(1)}, u32[]{:S(2)}, u32[]{:S(2)}) collective-permute-start(bf16[480,640]{1,0:T(8,128)(2,1)} %pass_on.16.refs_0_), channel_id=1, source_target_pairs={{0,1},{1,0},{2,3},{3,2},{4,5},{5,4},{6,7},{7,6},{8,9},{9,8},{10,11... | collective-permute-start | bytes 1843208 | tf_op jit(solution)/shard_map/cond/branch_0_fun/ppermute | solution.py:22
  25.2 22.5 %collective-permute-start.2 = (bf16[480,640]{1,0:T(8,128)(2,1)}, bf16[480,640]{1,0:T(8,128)(2,1)S(1)}, u32[]{:S(2)}, u32[]{:S(2)}) collective-permute-start(bf16[480,640]{1,0:T(8,128)(2,1)} %pass_on.16.refs_0_), channel_id=1, source_target_pairs={{0,2},{1,3},{2,0},{3,1},{4,6},{5,7},{6,4},{7,5},{8,10},{9,11},{10,... | collective-permute-start | bytes 1843208 | tf_op jit(solution)/shard_map/cond/branch_0_fun/ppermute | solution.py:22
  33.2 28.1 %all-to-all-start = ((bf16[32,80,256]{2,1,0:T(8,128)(2,1)}), bf16[32,80,256]{2,1,0:T(8,128)(2,1)S(1)}, u32[]{:S(2)}, u32[]{:S(2)}) async-start(bf16[32,80,256]{2,1,0:T(8,128)(2,1)} %broadcast_in_dim.89), calls=%async_computation | async-start | bytes 2621440 | tf_op jit(solution)/shard_map/cond/branch_0_fun/all_to_all | solution.py:174
  41.5 18.8 %copy-start.43 = (bf16[32,4,1024]{2,1,0:T(4,128)(2,1)S(1)}, bf16[32,4,1024]{2,1,0:T(4,128)(2,1)}, u32[]{:S(2)}) copy-start(bf16[32,4,1024]{2,1,0:T(4,128)(2,1)} %get-tuple-element.314) | copy-start | bytes 786436 | tf_op jit(solution)/shard_map/cond
  41.5 18.9 %copy-start.51 = (s32[64,32,1]{0,2,1:T(1,128)S(1)}, s32[64,32,1]{0,2,1:T(1,128)}, u32[]{:S(2)}) copy-start(s32[64,32,1]{0,2,1:T(1,128)} %get-tuple-element.460) | copy-start | bytes 24580 | tf_op jit(solution)/shard_map/cond
  41.5 19.8 %copy-start.9 = (bf16[480,640]{1,0:T(8,128)(2,1)S(1)}, bf16[480,640]{1,0:T(8,128)(2,1)}, u32[]{:S(2)}) copy-start(bf16[480,640]{1,0:T(8,128)(2,1)} %pass_on.16.refs_0_) | copy-start | bytes 1843204 | tf_op jit(solution)/shard_map/cond
  44.7 3.0 %copy-start.29 = (bf16[480,640]{1,0:T(8,128)(2,1)}, bf16[480,640]{1,0:T(8,128)(2,1)S(1)}, u32[]{:S(2)}) copy-start(bf16[480,640]{1,0:T(8,128)(2,1)S(1)} %collective-permute-done.1.awaited_ref.refs_1_) | copy-start | bytes 1843204 | tf_op jit(solution)/shard_map/cond
  47.7 0.8 copy-start.32
  48.5 21.1 %collective-permute-start.3 = (bf16[480,640]{1,0:T(8,128)(2,1)}, bf16[480,640]{1,0:T(8,128)(2,1)S(1)}, u32[]{:S(2)}, u32[]{:S(2)}) collective-permute-start(bf16[480,640]{1,0:T(8,128)(2,1)} %pass_on.17.refs_2_), channel_id=1, source_target_pairs={{0,1},{1,0},{2,3},{3,2},{4,5},{5,4},{6,7},{7,6},{8,9},{9,8},{10,11... | collective-permute-start | bytes 1843208 | tf_op jit(solution)/shard_map/cond/branch_0_fun/ppermute | solution.py:22
  61.3 1.1 copy-start.30
  62.4 1.1 copy-start.33
  63.4 21.5 %copy-start.39 = (bf16[5120,128]{1,0:T(8,128)(2,1)S(1)}, bf16[5120,128]{1,0:T(8,128)(2,1)}, u32[]{:S(2)}) copy-start(bf16[5120,128]{1,0:T(8,128)(2,1)} %get-tuple-element.284.refs_5_) | copy-start | bytes 3932164 | tf_op jit(solution)/shard_map/cond
  65.2 19.8 %copy-start.31 = (bf16[480,640]{1,0:T(8,128)(2,1)S(1)}, bf16[480,640]{1,0:T(8,128)(2,1)}, u32[]{:S(2)}) copy-start(bf16[480,640]{1,0:T(8,128)(2,1)} %copy-done.29) | copy-start | bytes 1843204 | tf_op jit(solution)/shard_map/cond
  65.2 19.8 %copy-start.34 = (bf16[480,640]{1,0:T(8,128)(2,1)S(1)}, bf16[480,640]{1,0:T(8,128)(2,1)}, u32[]{:S(2)}) copy-start(bf16[480,640]{1,0:T(8,128)(2,1)} %pass_on.17.refs_2_) | copy-start | bytes 1843204 | tf_op jit(solution)/shard_map/cond
  65.2 19.8 %copy-start.35 = (bf16[5120,128]{1,0:T(8,128)(2,1)S(1)}, bf16[5120,128]{1,0:T(8,128)(2,1)}, u32[]{:S(2)}) copy-start(bf16[5120,128]{1,0:T(8,128)(2,1)} %get-tuple-element.279.refs_4_) | copy-start | bytes 3932164 | tf_op jit(solution)/shard_map/cond
  71.3 35.7 %collective-permute-start.4 = (bf16[480,256]{1,0:T(8,128)(2,1)S(1)}, bf16[480,256]{1,0:T(8,128)(2,1)S(1)}, u32[]{:S(2)}, u32[]{:S(2)}) collective-permute-start(bf16[480,256]{1,0:T(8,128)(2,1)S(1)} %multiply.27), channel_id=1, source_target_pairs={{0,4},{1,5},{2,6},{3,7},{4,0},{5,1},{6,2},{7,3},{8,12},{9,13},{10,... | collective-permute-start | bytes 737288 | tf_op jit(solution)/shard_map/cond/branch_0_fun/ppermute | solution.py:22
  85.0 22.0 %copy-start.77 = (f32[128]{0:T(128)S(1)}, f32[128]{0:T(128)}, u32[]{:S(2)}) copy-start(f32[128]{0:T(128)} %get-tuple-element.289) | copy-start | bytes 1540 | tf_op jit(solution)/shard_map/cond
  108.9 38.3 %copy-start.46 = (bf16[4,4,1024]{2,1,0:T(4,128)(2,1)S(1)}, bf16[4,4,1024]{2,1,0:T(4,128)(2,1)}, u32[]{:S(2)}) copy-start(bf16[4,4,1024]{2,1,0:T(4,128)(2,1)} %get-tuple-element.299) | copy-start | bytes 98308 | tf_op jit(solution)/shard_map/cond
  109.0 38.3 %copy-start.61 = (s32[4]{0:T(128)S(1)}, s32[4]{0:T(128)}, u32[]{:S(2)}) copy-start(s32[4]{0:T(128)} %get-tuple-element.294) | copy-start | bytes 52 | tf_op jit(solution)/shard_map/cond
  109.0 38.4 %copy-start.72 = (bf16[4,2,256,128]{3,2,1,0:T(8,128)(2,1)S(1)}, bf16[4,2,256,128]{3,2,1,0:T(8,128)(2,1)}, u32[]{:S(2)}) copy-start(bf16[4,2,256,128]{3,2,1,0:T(8,128)(2,1)} %get-tuple-element.304.cache) | copy-start | bytes 1572868 | tf_op jit(solution)/shard_map/cond
  109.0 23.5 %collective-permute-start.5 = (bf16[128,1024]{1,0:T(8,128)(2,1)S(1)}, bf16[128,1024]{1,0:T(8,128)(2,1)S(1)}, u32[]{:S(2)}, u32[]{:S(2)}) collective-permute-start(bf16[128,1024]{1,0:T(8,128)(2,1)S(1)} %prompt_attention.5), channel_id=1, source_target_pairs={{0,256},{256,0},{1,257},{257,1},{2,258},{258,2},{3,259},{259,3},{4... | collective-permute-start | bytes 786440 | tf_op jit(solution)/shard_map/cond/branch_0_fun/ppermute | solution.py:22
  133.5 25.3 %all-to-all-start.1 = ((bf16[32,8,1024]{2,1,0:T(8,128)(2,1)}), bf16[32,8,1024]{2,1,0:T(8,128)(2,1)S(1)}, u32[]{:S(2)}, u32[]{:S(2)}) async-start(bf16[32,8,1024]{2,1,0:T(8,128)(2,1)} %fusion), calls=%async_computation.1 | async-start | bytes 1048576 | tf_op jit(solution)/shard_map/cond/branch_0_fun/all_to_all | solution.py:354

commit v4 on v3

--- a/solution.py
+++ b/solution.py
@@ -73,18 +73,19 @@
 def pack_kernel(place, states, nexts, sequences, packed):
     next_rows = nexts[...].reshape(-1, packed.shape[1])
     sequence_rows = sequences[...].reshape(-1, packed.shape[1])
-    kept = packed.shape[0] - next_rows.shape[0] - sequence_rows.shape[0]
-    row = lax.broadcasted_iota(jnp.int32, (kept, place.shape[1]), 0)
+    fresh = next_rows.shape[0] + sequence_rows.shape[0]
+    row = lax.broadcasted_iota(jnp.int32, (states.shape[0], place.shape[1]), 0)
     chooser = (row == place[...]).astype(jnp.float32).astype(jnp.bfloat16)
     live = jnp.dot(chooser, states[...], preferred_element_type=jnp.float32)
-    packed[:kept, :] = live.astype(jnp.bfloat16)
-    packed[kept : kept + next_rows.shape[0], :] = next_rows
-    packed[kept + next_rows.shape[0] :, :] = sequence_rows
-
-
-def pack(place, states, nexts, sequences, kept):
+    packed[: next_rows.shape[0], :] = next_rows
+    packed[next_rows.shape[0] : fresh, :] = sequence_rows
+    packed[fresh:, :] = live.astype(jnp.bfloat16)
+
+
+def pack(place, states, nexts, sequences):
     whole = pl.BlockSpec(memory_space=pltpu.VMEM)
-    rows = kept + nexts.shape[0] * nexts.shape[1] + sequences.shape[0] * sequences.shape[1]
+    fresh = nexts.shape[0] * nexts.shape[1] + sequences.shape[0] * sequences.shape[1]
+    rows = fresh + states.shape[0]
     return pl.pallas_call(
         pack_kernel,
         in_specs=[whole] * 4,
@@ -96,11 +97,10 @@
 
 
 def prompt_kernel(steps, own, got, gain, owners, query, out):
-    kept = owners.shape[1]
+    fresh = own.shape[0] - owners.shape[1]
     count = query.shape[0]
-    keys, values = finish(own[: kept + count], got[: kept + count], gain[...])
-    old_keys, old_values = keys[:kept], values[:kept]
-    new_keys, new_values = keys[kept:], values[kept:]
+    old_keys, old_values = finish(own[fresh:], got[fresh:], gain[...])
+    new_keys, new_values = finish(own[:count], got[:count], gain[...])
     rows = GROUP * steps
     for first in range(0, count, rows):
         attend(
@@ -146,10 +146,9 @@
     )
 
 
-def cached_attention(own, got, gain, owners, query, cache, steps):
+def cached_attention(own, got, gain, owners, query, cache, steps, first):
     rows = query.shape[0]
-    last = own.shape[0] // rows - 1
-    fresh = pl.BlockSpec((rows, 2 * HD), lambda g: (last, 0))
+    fresh = pl.BlockSpec((rows, 2 * HD), lambda g: (first // rows, 0))
     return pl.pallas_call(
         functools.partial(cached_kernel, steps),
         grid=(1,),
@@ -245,8 +244,121 @@
     return jnp.sum(same_target & earlier, axis=1)
 
 
+def prepare(
+    prompt_states, prompt_lengths, prompt_query, prompt_next, key_weight, value_weight, seq_next
+):
+    groups = lax.axis_size("grp")
+    group_index = lax.axis_index("grp")
+    lane = lax.axis_index("tp")
+    prompts = prompt_query.shape[0]
+    prompt_len = prompt_states.shape[0] // prompts
+    width = prompt_next.shape[2]
+
+    share = QUAD * width // groups
+    start = ((lane ^ 4) // QUAD * QUAD) * width + group_index * share
+    weight_share = jnp.concatenate(
+        [
+            lax.dynamic_slice_in_dim(key_weight, start, share, 0),
+            lax.dynamic_slice_in_dim(value_weight, start, share, 0),
+        ],
+        axis=1,
+    )
+    instance = lax.axis_index("pool") * groups + group_index
+    lengths = lax.dynamic_index_in_dim(prompt_lengths, instance, 0, keepdims=False)
+    ends = jnp.cumsum(lengths)
+    position = jnp.arange(prompt_len)[None, :]
+    place = jnp.where(position < lengths[:, None], (ends - lengths)[:, None] + position, -1)
+    place = place.reshape(1, prompts * prompt_len).astype(jnp.int32)
+    packed = pack(place, prompt_states, prompt_next, seq_next)
+    received_share = exchange(pass_on(weight_share, packed), "tp", 4)
+    return received_share, ends, packed
+
+
 def run(
     kept,
+    received_share,
+    ends,
+    packed,
+    prompt_target,
+    prompt_query,
+    key_weight,
+    value_weight,
+    key_gain,
+    seq_query,
+    cache_kv,
+    context_lengths,
+):
+    groups = lax.axis_size("grp")
+    pool_index = lax.axis_index("pool")
+    group_index = lax.axis_index("grp")
+    lane = lax.axis_index("tp")
+    prompts = prompt_query.shape[0]
+    seq_count, steps, query_width = seq_query.shape
+    quad = QUAD
+    gain = key_gain.reshape(1, HD)
+    prompt_owners = jnp.sum(ends[:, None] <= jnp.arange(kept)[None, :], axis=0, dtype=jnp.int32)
+    prompt_owners = prompt_owners.reshape(1, kept)
+    context = cache_kv.shape[2]
+    seq_owners = jnp.where(
+        jnp.arange(context)[None, :] < context_lengths[:, None],
+        jnp.arange(seq_count, dtype=jnp.int32)[:, None],
+        seq_count,
+    ).reshape(1, seq_count * context)
+
+    query_rows = prompt_query.reshape(prompts * steps, query_width)
+    mine = packed[: (prompts + seq_count) * steps + kept]
+    partner_weight = spread(received_share)
+
+    order = jnp.asarray([0, 1, 2, 3], jnp.int32) ^ (lane % quad)
+    block_number = lane // quad * quad + order
+    second = exchange(mine, "tp", 2)
+    first = exchange(mine, "tp", 1)
+    second = pass_on(second, first, 8000000000)
+    third = exchange(second, "tp", 1)
+    blank = jnp.zeros((1, 2 * HD), jnp.float32)
+    near = (mine, first, second)
+    begun = multiply(
+        blank, near, order[:3], block_number[:3], [partner_weight], False, jnp.float32
+    )
+    sent = multiply(
+        begun, [third], order[3:], block_number[3:], [partner_weight], False, jnp.bfloat16
+    )
+    got = exchange(sent, "tp", 4)
+    own = multiply(
+        blank,
+        near + (third,),
+        order,
+        block_number,
+        [key_weight, value_weight],
+        True,
+        jnp.float32,
+    )
+    result = prompt_attention(own, got, gain, prompt_owners, query_rows, steps)
+    crossed = exchange(result, "pool", 1)
+    seq_output = cached_attention(
+        own,
+        got,
+        gain,
+        seq_owners,
+        seq_query.reshape(seq_count * steps, query_width),
+        cache_kv,
+        steps,
+        prompts * steps,
+    ).reshape(seq_count, steps, query_width)
+
+    source = (pool_index ^ 1) * groups + group_index
+    targets = lax.dynamic_index_in_dim(prompt_target[:, :, 0], source, 0, keepdims=False)
+    places = targets * MOST + rank_within(targets)
+    place_rows = (places[:, None] * steps + jnp.arange(steps)[None, :]).reshape(-1)
+    chooser = (jnp.arange(groups * MOST * steps)[:, None] == place_rows[None, :]).astype(
+        jnp.bfloat16
+    )
+    outgoing = jnp.dot(chooser, crossed, preferred_element_type=jnp.float32).astype(jnp.bfloat16)
+    arrived = lax.all_to_all(outgoing, "grp", split_axis=0, concat_axis=0, tiled=True)
+    return seq_output, arrived.reshape(1, groups * MOST, steps, query_width)
+
+
+def on_device(
     prompt_states,
     prompt_lengths,
     prompt_target,
@@ -260,107 +372,26 @@
     cache_kv,
     context_lengths,
 ):
-    groups = lax.axis_size("grp")
-    pool_index = lax.axis_index("pool")
-    group_index = lax.axis_index("grp")
-    lane = lax.axis_index("tp")
-    prompts = prompt_query.shape[0]
-    prompt_len = prompt_states.shape[0] // prompts
-    seq_count, steps, query_width = seq_query.shape
-    width = prompt_next.shape[2]
-    quad = QUAD
-
-    share = quad * width // groups
-    start = ((lane ^ 4) // quad * quad) * width + group_index * share
-    weight_share = jnp.concatenate(
-        [
-            lax.dynamic_slice_in_dim(key_weight, start, share, 0),
-            lax.dynamic_slice_in_dim(value_weight, start, share, 0),
-        ],
-        axis=1,
-    )
-    gain = key_gain.reshape(1, HD)
-    instance = pool_index * groups + group_index
-    lengths = lax.dynamic_index_in_dim(prompt_lengths, instance, 0, keepdims=False)
-    ends = jnp.cumsum(lengths)
-    position = jnp.arange(prompt_len)[None, :]
-    place = jnp.where(position < lengths[:, None], (ends - lengths)[:, None] + position, -1)
-    place = place.reshape(1, prompts * prompt_len).astype(jnp.int32)
-    prompt_owners = jnp.sum(ends[:, None] <= jnp.arange(kept)[None, :], axis=0, dtype=jnp.int32)
-    prompt_owners = prompt_owners.reshape(1, kept)
-    context = cache_kv.shape[2]
-    seq_owners = jnp.where(
-        jnp.arange(context)[None, :] < context_lengths[:, None],
-        jnp.arange(seq_count, dtype=jnp.int32)[:, None],
-        seq_count,
-    ).reshape(1, seq_count * context)
-
-    query_rows = prompt_query.reshape(prompts * steps, query_width)
-    mine = pack(
-        place,
-        prompt_states,
-        prompt_next,
-        seq_next,
-        kept,
-    )
-    received_share = exchange(pass_on(weight_share, mine), "tp", 4)
-    partner_weight = spread(received_share)
-
-    order = jnp.asarray([0, 1, 2, 3], jnp.int32) ^ (lane % quad)
-    block_number = lane // quad * quad + order
-    mine = pass_on(mine, received_share)
-    second = exchange(mine, "tp", 2)
-    first = exchange(mine, "tp", 1)
-    second = pass_on(second, first, 8000000000)
-    third = exchange(second, "tp", 1)
-    blank = jnp.zeros((1, 2 * HD), jnp.float32)
-    near = (mine, first, second)
-    begun = multiply(
-        blank, near, order[:3], block_number[:3], [partner_weight], False, jnp.float32
-    )
-    sent = multiply(
-        begun, [third], order[3:], block_number[3:], [partner_weight], False, jnp.bfloat16
-    )
-    got = exchange(sent, "tp", 4)
-    own = multiply(
-        blank,
-        near + (third,),
-        order,
-        block_number,
-        [key_weight, value_weight],
-        True,
-        jnp.float32,
-    )
-    result = prompt_attention(own, got, gain, prompt_owners, query_rows, steps)
-    crossed = exchange(result, "pool", 1)
-    seq_output = cached_attention(
-        own,
-        got,
-        gain,
-        seq_owners,
-        seq_query.reshape(seq_count * steps, query_width),
-        cache_kv,
-        steps,
-    ).reshape(seq_count, steps, query_width)
-
-    source = (pool_index ^ 1) * groups + group_index
-    targets = lax.dynamic_index_in_dim(prompt_target[:, :, 0], source, 0, keepdims=False)
-    places = targets * MOST + rank_within(targets)
-    place_rows = (places[:, None] * steps + jnp.arange(steps)[None, :]).reshape(-1)
-    chooser = (jnp.arange(groups * MOST * steps)[:, None] == place_rows[None, :]).astype(
-        jnp.bfloat16
-    )
-    outgoing = jnp.dot(chooser, crossed, preferred_element_type=jnp.float32).astype(jnp.bfloat16)
-    arrived = lax.all_to_all(outgoing, "grp", split_axis=0, concat_axis=0, tiled=True)
-    return seq_output, arrived.reshape(1, groups * MOST, steps, query_width)
-
-
-def on_device(*arrays):
-    rows = arrays[0].shape[0]
-    most = jnp.max(jnp.sum(arrays[1], axis=1))
+    rows = prompt_states.shape[0]
+    most = jnp.max(jnp.sum(prompt_lengths, axis=1))
     sizes = [size for size in BUCKETS if size < rows] + [rows]
     choice = sum((most > size).astype(jnp.int32) for size in sizes[:-1])
-    return lax.switch(choice, [functools.partial(run, size) for size in sizes], *arrays)
+    prepared = prepare(
+        prompt_states, prompt_lengths, prompt_query, prompt_next, key_weight, value_weight, seq_next
+    )
+    return lax.switch(
+        choice,
+        [functools.partial(run, size) for size in sizes],
+        *prepared,
+        prompt_target,
+        prompt_query,
+        key_weight,
+        value_weight,
+        key_gain,
+        seq_query,
+        cache_kv,
+        context_lengths,
+    )
 
 
 def solution(mesh):

time: 161 us -> 155 us (0.963)
  waiting for transfers between devices: 64.1 us -> 56.8 us
    ppermute x6, starting transfers between devices: 45.3 us -> 40.5 us  [exchange(): return lax.ppermute(block, axis, [(i, i ^ apart) for i in range(size)])]
    ppermute x6, waiting for transfers between devices: 53.2 us -> 48.5 us  [exchange(): return lax.ppermute(block, axis, [(i, i ^ apart) for i in range(size)])]
    all_to_all x1, starting transfers between devices: 13.7 us -> 17.7 us  [run(): lax.all_to_all(outgoing, 'grp', split_axis=0, concat_axis=0, tiled=True)]
    unnamed x0 -> x12, local copies, waits for them, and re-layouts: none -> 2.74 us
    all_to_all x1, waiting for transfers between devices: 10.2 us -> 8.11 us  [run(): lax.all_to_all(outgoing, 'grp', split_axis=0, concat_axis=0, tiled=True)]
    cond x35 -> x19, local copies, waits for them, and re-layouts: 4.48 us -> 3.02 us
  transfers between devices with their start and end apart: 8 -> 8, of which waited for: 8 -> 7; matrix products, arithmetic and copies ran while one was open for 3% -> 4% of each run, Pallas kernels for 3% -> 3%
where the time goes in v4:
time: 155 us; the launch traced here: 153 us
  starting transfers between devices  66.7 us (43%)
  waiting for transfers between devices  56.8 us (37%)
  local copies, waits for them, and re-layouts  12.5 us (8%)
  Pallas kernels  10 us (6%)
  between operations  3.34 us (2%)
  other arithmetic  2.61 us (2%)
    ppermute x6, waiting for transfers between devices, exchange(): return lax.ppermute(block, axis, [(i, i ^ apart) for i in range(size)])  48.5 us
    ppermute x6, starting transfers between devices, exchange(): return lax.ppermute(block, axis, [(i, i ^ apart) for i in range(size)])  40.5 us
    all_to_all x1, starting transfers between devices, run(): lax.all_to_all(outgoing, 'grp', split_axis=0, concat_axis=0, tiled=True)  17.7 us
    all_to_all x1, starting transfers between devices, spread(): lax.all_to_all(copies, 'grp', split_axis=0, concat_axis=0, tiled=True)  8.61 us
    all_to_all x1, waiting for transfers between devices, run(): lax.all_to_all(outgoing, 'grp', split_axis=0, concat_axis=0, tiled=True)  8.11 us
    pallas_call x3, Pallas kernels, multiply(): pl.pallas_call(functools.partial(multiply_kernel, len(features)), grid_sp...  5.47 us
  transfers between devices with their start and end apart: 8, of which 7 were waited for; matrix products, arithmetic and copies ran while one was open for 4% of the time, Pallas kernels for 3%

profile of v4, /device:TPU:1, one launch (start us, length us, event | category | flops | bytes accessed | tf_op | source)
XLA Modules:
  0.0 153.3 jit_solution(17913722286414114342)
XLA Ops:
  0.7 0.9 dynamic-slice_reduce_fusion
  1.6 0.1 reduce-window.7
  1.6 0.1 reduce.1
  1.7 0.1 add_select_fusion
  1.8 0.1 select_n.147.place
  1.9 0.8 constant_dynamic-slice_fusion
  2.7 0.6 pad_maximum_fusion.block_ref
  3.3 1.1 copy-done.32
  4.4 0.9 copy-done.33
  5.3 0.7 copy-done.34
  6.0 0.6 pack.1.awaited_ref
  6.6 9.6 %collective-permute-start.25 = (bf16[80,256]{1,0:T(8,128)(2,1)}, bf16[80,256]{1,0:T(8,128)(2,1)S(1)}, u32[]{:S(2)}, u32[]{:S(2)}) collective-permute-start(bf16[80,256]{1,0:T(8,128)(2,1)} %pass_on.11), channel_id=1, source_target_pairs={{0,4},{1,5},{2,6},{3,7},{4,0},{5,1},{6,2},{7,3},{8,12},{9,13},{10,... | collective-permute-start | bytes 122888 | tf_op jit(solution)/shard_map/ppermute | solution.py:22
  16.3 0.0 copy-done.57
  16.3 0.6 reduce_max.9
  19.5 0.0 collective-permute-done.25
  19.6 0.0 copy-done.47
  19.6 0.0 copy-done.56
  19.6 133.8 %conditional.1 = (bf16[4,4,1024]{2,1,0:T(4,128)(2,1)}, bf16[1,64,4,1024]{3,2,1,0:T(4,128)(2,1)}) conditional(s32[]{:T(128)} %clamp.3, (s32[4]{0:T(128)S(1)}, bf16[656,640]{1,0:T(8,128)(2,1)S(1)}, bf16[5120,128]{1,0:T(8,128)(2,1)}, bf16[5120,128]{1,0:T(8,128)(2,1)}, bf16[80,256]{1,0:T(8,128)(2,1)S(1)}, ...), branch_computations={%region_3.6_spmd, %region_6.9_spmd, %region_9.12_spmd, %region_12.... | conditional | flops 11787123712 | bytes 91152752 | solution.py:382
  19.6 0.1 slice.48.refs_0_
  19.7 3.5 %collective-permute-start = (bf16[480,640]{1,0:T(8,128)(2,1)S(1)}, bf16[480,640]{1,0:T(8,128)(2,1)S(1)}, u32[]{:S(2)}, u32[]{:S(2)}) collective-permute-start(bf16[480,640]{1,0:T(8,128)(2,1)S(1)} %slice.48.refs_0_), channel_id=1, source_target_pairs={{0,1},{1,0},{2,3},{3,2},{4,5},{5,4},{6,7},{7,6},{8,9},{9,8},{10,11... | collective-permute-start | bytes 1843208 | tf_op jit(solution)/shard_map/cond/branch_0_fun/ppermute | solution.py:22
  23.2 4.9 %collective-permute-start.1 = (bf16[480,640]{1,0:T(8,128)(2,1)S(1)}, bf16[480,640]{1,0:T(8,128)(2,1)S(1)}, u32[]{:S(2)}, u32[]{:S(2)}) collective-permute-start(bf16[480,640]{1,0:T(8,128)(2,1)S(1)} %slice.48.refs_0_), channel_id=1, source_target_pairs={{0,2},{1,3},{2,0},{3,1},{4,6},{5,7},{6,4},{7,5},{8,10},{9,11},{10,... | collective-permute-start | bytes 1843208 | tf_op jit(solution)/shard_map/cond/branch_0_fun/ppermute | solution.py:22
  28.1 1.1 broadcast_in_dim.58
  29.3 8.6 %all-to-all-start = ((bf16[32,80,256]{2,1,0:T(8,128)(2,1)}), bf16[32,80,256]{2,1,0:T(8,128)(2,1)S(1)}, u32[]{:S(2)}, u32[]{:S(2)}) async-start(bf16[32,80,256]{2,1,0:T(8,128)(2,1)} %broadcast_in_dim.58), calls=%async_computation | async-start | bytes 2621440 | tf_op jit(solution)/shard_map/cond/branch_0_fun/all_to_all | solution.py:173
  37.9 6.1 %collective-permute-done.awaited_ref.refs_1_ = bf16[480,640]{1,0:T(8,128)(2,1)S(1)} collective-permute-done((bf16[480,640]{1,0:T(8,128)(2,1)S(1)}, bf16[480,640]{1,0:T(8,128)(2,1)S(1)}, u32[]{:S(2)}, u32[]{:S(2)}) %collective-permute-start) | collective-permute-done | bytes 614432 | tf_op jit(solution)/shard_map/cond/branch_0_fun/ppermute | solution.py:22
  44.0 3.2 %collective-permute-done.1.block_ref = bf16[480,640]{1,0:T(8,128)(2,1)S(1)} collective-permute-done((bf16[480,640]{1,0:T(8,128)(2,1)S(1)}, bf16[480,640]{1,0:T(8,128)(2,1)S(1)}, u32[]{:S(2)}, u32[]{:S(2)}) %collective-permute-start.1) | collective-permute-done | bytes 614432 | tf_op jit(solution)/shard_map/cond/branch_0_fun/ppermute | solution.py:22
  47.1 0.0 copy-done.24
  47.1 0.8 copy-done.27
  48.0 8.1 %collective-permute-start.2 = (bf16[480,640]{1,0:T(8,128)(2,1)}, bf16[480,640]{1,0:T(8,128)(2,1)S(1)}, u32[]{:S(2)}, u32[]{:S(2)}) collective-permute-start(bf16[480,640]{1,0:T(8,128)(2,1)} %pass_on.6.refs_2_), channel_id=1, source_target_pairs={{0,1},{1,0},{2,3},{3,2},{4,5},{5,4},{6,7},{7,6},{8,9},{9,8},{10,11... | collective-permute-start | bytes 1843208 | tf_op jit(solution)/shard_map/cond/branch_0_fun/ppermute | solution.py:22
  56.1 0.6 slice.49.order
  56.7 0.6 slice.50.block_number
  57.3 0.1 reshape.518.query
  57.4 0.1 convert_reduce_fusion
  57.5 0.1 copy.83
  57.5 0.1 all-to-all-done
  57.7 1.1 copy-done.25
  58.8 1.1 copy-done.28
  59.8 1.7 %multiply.18.refs_2_ = f32[480,256]{1,0:T(8,128)S(1)} custom-call(s32[3]{0:T(128)S(1)} %bitcast.89, s32[3]{0:T(128)S(1)} %bitcast.88, bf16[480,640]{1,0:T(8,128)(2,1)S(1)} %slice.48.refs_0_, bf16[480,640]{1,0:T(8,128)(2,1)S(1)} %copy-done.25, bf16[480,640]{1,0:T(8,128)(2,1)S(1)} %copy-done.28, bf16[2560,256]{1,0:T(8,128)(2,1)S(1)} %bitcast.78, ...), custom_call_target="tpu_custom_call" | custom-call | flops 471859200 | bytes 2000000 | tf_op jit(solution)/shard_map/cond/branch_0_fun/multiply/pallas_call | solution.py:202
  61.5 0.0 copy-start.26
  61.6 0.0 copy-start.29
  61.6 0.0 copy-start.39
  61.6 5.5 %collective-permute-done.2.refs_3_.refs_0_ = bf16[480,640]{1,0:T(8,128)(2,1)S(1)} collective-permute-done((bf16[480,640]{1,0:T(8,128)(2,1)}, bf16[480,640]{1,0:T(8,128)(2,1)S(1)}, u32[]{:S(2)}, u32[]{:S(2)}) %collective-permute-start.2) | collective-permute-done | bytes 614432 | tf_op jit(solution)/shard_map/cond/branch_0_fun/ppermute | solution.py:22
  67.0 1.7 %multiply.19 = bf16[480,256]{1,0:T(8,128)(2,1)S(1)} custom-call(s32[1]{0:T(128)} %slice.49.order, s32[1]{0:T(128)} %slice.50.block_number, bf16[480,640]{1,0:T(8,128)(2,1)S(1)} %collective-permute-done.2.refs_3_.refs_0_, bf16[2560,256]{1,0:T(8,128)(2,1)S(1)} %bitcast.79, f32[480,256]{1,0:T(8,128)S(1)} %multiply.18.refs_2_), custom_call_target="tpu_custom_call" | custom-call | flops 157286400 | bytes 2000000 | tf_op jit(solution)/shard_map/cond/branch_0_fun/multiply/pallas_call | solution.py:202
  68.7 12.2 %collective-permute-start.3 = (bf16[480,256]{1,0:T(8,128)(2,1)S(1)}, bf16[480,256]{1,0:T(8,128)(2,1)S(1)}, u32[]{:S(2)}, u32[]{:S(2)}) collective-permute-start(bf16[480,256]{1,0:T(8,128)(2,1)S(1)} %multiply.19), channel_id=1, source_target_pairs={{0,4},{1,5},{2,6},{3,7},{4,0},{5,1},{6,2},{7,3},{8,12},{9,13},{10,... | collective-permute-start | bytes 737288 | tf_op jit(solution)/shard_map/cond/branch_0_fun/ppermute | solution.py:22
  80.9 0.2 convert_reduce_fusion.1
  81.1 0.0 copy-done.26
  81.1 0.0 copy-done.29
  81.1 0.0 copy-done.39
  81.1 2.1 %multiply.17.own_new.own = f32[480,256]{1,0:T(8,128)S(1)} custom-call(s32[4]{0:T(128)S(1)} %get-tuple-element.435.order, s32[4]{0:T(128)S(1)} %get-tuple-element.434.block_number, bf16[480,640]{1,0:T(8,128)(2,1)S(1)} %slice.48.refs_0_, bf16[480,640]{1,0:T(8,128)(2,1)S(1)} %copy-done.26, bf16[480,640]{1,0:T(8,128)(2,1)S(1)} %copy-done.29, ...), custom_call_target="tpu_custom_call" | custom-call | flops 629145600 | bytes 2000000 | tf_op jit(solution)/shard_map/cond/branch_0_fun/multiply/pallas_call | solution.py:202
  83.2 19.8 %collective-permute-done.3.got_new.got = bf16[480,256]{1,0:T(8,128)(2,1)S(1)} collective-permute-done((bf16[480,256]{1,0:T(8,128)(2,1)S(1)}, bf16[480,256]{1,0:T(8,128)(2,1)S(1)}, u32[]{:S(2)}, u32[]{:S(2)}) %collective-permute-start.3) | collective-permute-done | bytes 245792 | tf_op jit(solution)/shard_map/cond/branch_0_fun/ppermute | solution.py:22
  103.1 2.6 %prompt_attention.5 = bf16[128,1024]{1,0:T(8,128)(2,1)S(1)} custom-call(f32[480,256]{1,0:T(8,128)S(1)} %multiply.17.own_new.own, bf16[480,256]{1,0:T(8,128)(2,1)S(1)} %collective-permute-done.3.got_new.got, f32[1,128]{1,0:T(1,128)} %bitcast.104, s32[1,336]{1,0:T(1,128)S(1)} %reshape.517.owners, bf16[128,1024]{1,0:T(8,128)(2,1)S(1)} %reshape.518.query), custom_call_target="tpu_custom_call" | custom-call | flops 1000000000 | bytes 2000000 | tf_op jit(solution)/shard_map/cond/branch_0_fun/prompt_attention/pallas_call | solution.py:120
  105.7 0.0 copy-start.70
  105.7 2.1 %collective-permute-start.4 = (bf16[128,1024]{1,0:T(8,128)(2,1)S(1)}, bf16[128,1024]{1,0:T(8,128)(2,1)S(1)}, u32[]{:S(2)}, u32[]{:S(2)}) collective-permute-start(bf16[128,1024]{1,0:T(8,128)(2,1)S(1)} %prompt_attention.5), channel_id=1, source_target_pairs={{0,256},{256,0},{1,257},{257,1},{2,258},{258,2},{3,259},{259,3},{4... | collective-permute-start | bytes 786440 | tf_op jit(solution)/shard_map/cond/branch_0_fun/ppermute | solution.py:22
  107.8 0.1 iota_add_fusion
  107.9 0.1 add.209
  108.0 14.0 %collective-permute-done.4 = bf16[128,1024]{1,0:T(8,128)(2,1)S(1)} collective-permute-done((bf16[128,1024]{1,0:T(8,128)(2,1)S(1)}, bf16[128,1024]{1,0:T(8,128)(2,1)S(1)}, u32[]{:S(2)}, u32[]{:S(2)}) %collective-permute-start.4) | collective-permute-done | bytes 262176 | tf_op jit(solution)/shard_map/cond/branch_0_fun/ppermute | solution.py:22
  122.0 1.1 fusion
  123.1 17.7 %all-to-all-start.1 = ((bf16[32,8,1024]{2,1,0:T(8,128)(2,1)}), bf16[32,8,1024]{2,1,0:T(8,128)(2,1)S(1)}, u32[]{:S(2)}, u32[]{:S(2)}) async-start(bf16[32,8,1024]{2,1,0:T(8,128)(2,1)} %fusion), calls=%async_computation.1 | async-start | bytes 1048576 | tf_op jit(solution)/shard_map/cond/branch_0_fun/all_to_all | solution.py:357
  140.7 0.8 reshape.515.query
  141.5 0.7 select_bitcast_fusion
  142.2 0.0 copy-done.70
  142.2 1.3 cached_attention.5
  143.6 0.6 reshape.516
  144.2 8.1 %all-to-all-done.1 = bf16[32,8,1024]{2,1,0:T(8,128)(2,1)S(1)} async-done(((bf16[32,8,1024]{2,1,0:T(8,128)(2,1)}), bf16[32,8,1024]{2,1,0:T(8,128)(2,1)S(1)}, u32[]{:S(2)}, u32[]{:S(2)}) %all-to-all-start.1) | async-done | bytes 524320 | tf_op jit(solution)/shard_map/cond/branch_0_fun/all_to_all | solution.py:357
  152.4 1.0 reshape.519
  (23 shorter events, 0.1 us)
Async XLA Ops:
  3.3 1.1 copy-start.32
  4.4 0.9 copy-start.33
  5.3 0.7 copy-start.34
  6.0 10.2 %copy-start.57 = (s32[64,32]{0,1:T(8,128)S(1)}, s32[64,32]{0,1:T(8,128)}, u32[]{:S(2)}) copy-start(s32[64,32]{0,1:T(8,128)} %param.23) | copy-start | bytes 24580
  6.0 13.5 %copy-start.47 = (bf16[32,4,1024]{2,1,0:T(4,128)(2,1)S(1)}, bf16[32,4,1024]{2,1,0:T(4,128)(2,1)}, u32[]{:S(2)}) copy-start(bf16[32,4,1024]{2,1,0:T(4,128)(2,1)} %param.25) | copy-start | bytes 786436
  6.0 13.5 %copy-start.56 = (s32[64,32,1]{0,2,1:T(1,128)S(1)}, s32[64,32,1]{0,2,1:T(1,128)}, u32[]{:S(2)}) copy-start(s32[64,32,1]{0,2,1:T(1,128)} %param.24) | copy-start | bytes 24580
  6.6 12.9 %collective-permute-start.25 = (bf16[80,256]{1,0:T(8,128)(2,1)}, bf16[80,256]{1,0:T(8,128)(2,1)S(1)}, u32[]{:S(2)}, u32[]{:S(2)}) collective-permute-start(bf16[80,256]{1,0:T(8,128)(2,1)} %pass_on.11), channel_id=1, source_target_pairs={{0,4},{1,5},{2,6},{3,7},{4,0},{5,1},{6,2},{7,3},{8,12},{9,13},{10,... | collective-permute-start | bytes 122888 | tf_op jit(solution)/shard_map/ppermute | solution.py:22
  19.7 24.3 %collective-permute-start = (bf16[480,640]{1,0:T(8,128)(2,1)S(1)}, bf16[480,640]{1,0:T(8,128)(2,1)S(1)}, u32[]{:S(2)}, u32[]{:S(2)}) collective-permute-start(bf16[480,640]{1,0:T(8,128)(2,1)S(1)} %slice.48.refs_0_), channel_id=1, source_target_pairs={{0,1},{1,0},{2,3},{3,2},{4,5},{5,4},{6,7},{7,6},{8,9},{9,8},{10,11... | collective-permute-start | bytes 1843208 | tf_op jit(solution)/shard_map/cond/branch_0_fun/ppermute | solution.py:22
  23.2 23.9 %collective-permute-start.1 = (bf16[480,640]{1,0:T(8,128)(2,1)S(1)}, bf16[480,640]{1,0:T(8,128)(2,1)S(1)}, u32[]{:S(2)}, u32[]{:S(2)}) collective-permute-start(bf16[480,640]{1,0:T(8,128)(2,1)S(1)} %slice.48.refs_0_), channel_id=1, source_target_pairs={{0,2},{1,3},{2,0},{3,1},{4,6},{5,7},{6,4},{7,5},{8,10},{9,11},{10,... | collective-permute-start | bytes 1843208 | tf_op jit(solution)/shard_map/cond/branch_0_fun/ppermute | solution.py:22
  29.3 28.4 %all-to-all-start = ((bf16[32,80,256]{2,1,0:T(8,128)(2,1)}), bf16[32,80,256]{2,1,0:T(8,128)(2,1)S(1)}, u32[]{:S(2)}, u32[]{:S(2)}) async-start(bf16[32,80,256]{2,1,0:T(8,128)(2,1)} %broadcast_in_dim.58), calls=%async_computation | async-start | bytes 2621440 | tf_op jit(solution)/shard_map/cond/branch_0_fun/all_to_all | solution.py:173
  44.0 3.2 %copy-start.24 = (bf16[480,640]{1,0:T(8,128)(2,1)}, bf16[480,640]{1,0:T(8,128)(2,1)S(1)}, u32[]{:S(2)}) copy-start(bf16[480,640]{1,0:T(8,128)(2,1)S(1)} %collective-permute-done.awaited_ref.refs_1_) | copy-start | bytes 1843204 | tf_op jit(solution)/shard_map/cond
  47.1 0.8 copy-start.27
  48.0 19.1 %collective-permute-start.2 = (bf16[480,640]{1,0:T(8,128)(2,1)}, bf16[480,640]{1,0:T(8,128)(2,1)S(1)}, u32[]{:S(2)}, u32[]{:S(2)}) collective-permute-start(bf16[480,640]{1,0:T(8,128)(2,1)} %pass_on.6.refs_2_), channel_id=1, source_target_pairs={{0,1},{1,0},{2,3},{3,2},{4,5},{5,4},{6,7},{7,6},{8,9},{9,8},{10,11... | collective-permute-start | bytes 1843208 | tf_op jit(solution)/shard_map/cond/branch_0_fun/ppermute | solution.py:22
  57.7 1.1 copy-start.25
  58.8 1.1 copy-start.28
  59.8 21.3 %copy-start.43 = (bf16[5120,128]{1,0:T(8,128)(2,1)S(1)}, bf16[5120,128]{1,0:T(8,128)(2,1)}, u32[]{:S(2)}) copy-start(bf16[5120,128]{1,0:T(8,128)(2,1)} %get-tuple-element.123.refs_5_) | copy-start | bytes 3932164 | tf_op jit(solution)/shard_map/cond
  61.5 19.6 %copy-start.26 = (bf16[480,640]{1,0:T(8,128)(2,1)S(1)}, bf16[480,640]{1,0:T(8,128)(2,1)}, u32[]{:S(2)}) copy-start(bf16[480,640]{1,0:T(8,128)(2,1)} %copy-done.24) | copy-start | bytes 1843204 | tf_op jit(solution)/shard_map/cond
  61.6 19.6 %copy-start.29 = (bf16[480,640]{1,0:T(8,128)(2,1)S(1)}, bf16[480,640]{1,0:T(8,128)(2,1)}, u32[]{:S(2)}) copy-start(bf16[480,640]{1,0:T(8,128)(2,1)} %pass_on.6.refs_2_) | copy-start | bytes 1843204 | tf_op jit(solution)/shard_map/cond
  61.6 19.6 %copy-start.39 = (bf16[5120,128]{1,0:T(8,128)(2,1)S(1)}, bf16[5120,128]{1,0:T(8,128)(2,1)}, u32[]{:S(2)}) copy-start(bf16[5120,128]{1,0:T(8,128)(2,1)} %get-tuple-element.122.refs_4_) | copy-start | bytes 3932164 | tf_op jit(solution)/shard_map/cond
  68.7 34.4 %collective-permute-start.3 = (bf16[480,256]{1,0:T(8,128)(2,1)S(1)}, bf16[480,256]{1,0:T(8,128)(2,1)S(1)}, u32[]{:S(2)}, u32[]{:S(2)}) collective-permute-start(bf16[480,256]{1,0:T(8,128)(2,1)S(1)} %multiply.19), channel_id=1, source_target_pairs={{0,4},{1,5},{2,6},{3,7},{4,0},{5,1},{6,2},{7,3},{8,12},{9,13},{10,... | collective-permute-start | bytes 737288 | tf_op jit(solution)/shard_map/cond/branch_0_fun/ppermute | solution.py:22
  105.7 36.5 %copy-start.70 = (bf16[4,2,256,128]{3,2,1,0:T(8,128)(2,1)S(1)}, bf16[4,2,256,128]{3,2,1,0:T(8,128)(2,1)}, u32[]{:S(2)}) copy-start(bf16[4,2,256,128]{3,2,1,0:T(8,128)(2,1)} %get-tuple-element.239.cache) | copy-start | bytes 1572868 | tf_op jit(solution)/shard_map/cond
  105.7 16.2 %collective-permute-start.4 = (bf16[128,1024]{1,0:T(8,128)(2,1)S(1)}, bf16[128,1024]{1,0:T(8,128)(2,1)S(1)}, u32[]{:S(2)}, u32[]{:S(2)}) collective-permute-start(bf16[128,1024]{1,0:T(8,128)(2,1)S(1)} %prompt_attention.5), channel_id=1, source_target_pairs={{0,256},{256,0},{1,257},{257,1},{2,258},{258,2},{3,259},{259,3},{4... | collective-permute-start | bytes 786440 | tf_op jit(solution)/shard_map/cond/branch_0_fun/ppermute | solution.py:22
  123.1 29.3 %all-to-all-start.1 = ((bf16[32,8,1024]{2,1,0:T(8,128)(2,1)}), bf16[32,8,1024]{2,1,0:T(8,128)(2,1)S(1)}, u32[]{:S(2)}, u32[]{:S(2)}) async-start(bf16[32,8,1024]{2,1,0:T(8,128)(2,1)} %fusion), calls=%async_computation.1 | async-start | bytes 1048576 | tf_op jit(solution)/shard_map/cond/branch_0_fun/all_to_all | solution.py:357

commit v5 on v4

--- a/solution.py
+++ b/solution.py
@@ -70,30 +70,46 @@
     return (row >> step_bits) == owners
 
 
-def pack_kernel(place, states, nexts, sequences, packed):
+def pack_kernel(prompt_len, instance, lengths, states, nexts, sequences, packed):
+    here = lax.broadcasted_iota(jnp.int32, lengths.shape, 0) == instance[0]
+    mine = jnp.sum(jnp.where(here, lengths[...], 0), axis=0, keepdims=True)
+    mine = jnp.broadcast_to(mine.astype(jnp.float32), (8, mine.shape[1])).astype(jnp.bfloat16)
+    shape = (lengths.shape[1], states.shape[0])
+    prompt = lax.broadcasted_iota(jnp.int32, shape, 0)
+    source = lax.broadcasted_iota(jnp.int32, shape, 1) // prompt_len
+
+    def total(chosen):
+        chosen = chosen.astype(jnp.float32).astype(jnp.bfloat16)
+        sums = jnp.dot(mine, chosen, preferred_element_type=jnp.float32)
+        return sums[:1].astype(jnp.int32)
+
+    position = lax.broadcasted_iota(jnp.int32, (1, shape[1]), 1) % prompt_len
+    place = jnp.where(
+        position < total(prompt == source), total(prompt < source) + position, -1
+    )
     next_rows = nexts[...].reshape(-1, packed.shape[1])
     sequence_rows = sequences[...].reshape(-1, packed.shape[1])
     fresh = next_rows.shape[0] + sequence_rows.shape[0]
-    row = lax.broadcasted_iota(jnp.int32, (states.shape[0], place.shape[1]), 0)
-    chooser = (row == place[...]).astype(jnp.float32).astype(jnp.bfloat16)
+    row = lax.broadcasted_iota(jnp.int32, (states.shape[0], shape[1]), 0)
+    chooser = (row == place).astype(jnp.float32).astype(jnp.bfloat16)
     live = jnp.dot(chooser, states[...], preferred_element_type=jnp.float32)
     packed[: next_rows.shape[0], :] = next_rows
     packed[next_rows.shape[0] : fresh, :] = sequence_rows
     packed[fresh:, :] = live.astype(jnp.bfloat16)
 
 
-def pack(place, states, nexts, sequences):
+def pack(instance, lengths, states, nexts, sequences):
     whole = pl.BlockSpec(memory_space=pltpu.VMEM)
     fresh = nexts.shape[0] * nexts.shape[1] + sequences.shape[0] * sequences.shape[1]
     rows = fresh + states.shape[0]
     return pl.pallas_call(
-        pack_kernel,
-        in_specs=[whole] * 4,
+        functools.partial(pack_kernel, states.shape[0] // lengths.shape[1]),
+        in_specs=[pl.BlockSpec(memory_space=pltpu.SMEM)] + [whole] * 4,
         out_specs=whole,
         out_shape=jax.ShapeDtypeStruct((rows, states.shape[1]), jnp.bfloat16),
-        compiler_params=pltpu.CompilerParams(vmem_limit_bytes=24 * 2**20),
+        compiler_params=pltpu.CompilerParams(vmem_limit_bytes=60 * 2**20),
         name="pack",
-    )(place, states, nexts, sequences)
+    )(instance.reshape(1), lengths, states, nexts, sequences)
 
 
 def prompt_kernel(steps, own, got, gain, owners, query, out):
@@ -245,13 +261,11 @@
 
 
 def prepare(
-    prompt_states, prompt_lengths, prompt_query, prompt_next, key_weight, value_weight, seq_next
+    prompt_states, prompt_lengths, prompt_next, key_weight, value_weight, seq_next
 ):
     groups = lax.axis_size("grp")
     group_index = lax.axis_index("grp")
     lane = lax.axis_index("tp")
-    prompts = prompt_query.shape[0]
-    prompt_len = prompt_states.shape[0] // prompts
     width = prompt_next.shape[2]
 
     share = QUAD * width // groups
@@ -266,10 +280,7 @@
     instance = lax.axis_index("pool") * groups + group_index
     lengths = lax.dynamic_index_in_dim(prompt_lengths, instance, 0, keepdims=False)
     ends = jnp.cumsum(lengths)
-    position = jnp.arange(prompt_len)[None, :]
-    place = jnp.where(position < lengths[:, None], (ends - lengths)[:, None] + position, -1)
-    place = place.reshape(1, prompts * prompt_len).astype(jnp.int32)
-    packed = pack(place, prompt_states, prompt_next, seq_next)
+    packed = pack(instance, prompt_lengths, prompt_states, prompt_next, seq_next)
     received_share = exchange(pass_on(weight_share, packed), "tp", 4)
     return received_share, ends, packed
 
@@ -377,7 +388,7 @@
     sizes = [size for size in BUCKETS if size < rows] + [rows]
     choice = sum((most > size).astype(jnp.int32) for size in sizes[:-1])
     prepared = prepare(
-        prompt_states, prompt_lengths, prompt_query, prompt_next, key_weight, value_weight, seq_next
+        prompt_states, prompt_lengths, prompt_next, key_weight, value_weight, seq_next
     )
     return lax.switch(
         choice,

time: 155 us -> 160 us (1.032)
  waiting for transfers between devices: 56.8 us -> 73.9 us
  starting transfers between devices: 66.7 us -> 56.6 us
    ppermute x6, waiting for transfers between devices: 48.5 us -> 63.7 us  [exchange(): return lax.ppermute(block, axis, [(i, i ^ apart) for i in range(size)])]
    all_to_all x1, starting transfers between devices: 17.7 us -> 7.7 us  [run(): lax.all_to_all(outgoing, 'grp', split_axis=0, concat_axis=0, tiled=True)]
    all_to_all x1, waiting for transfers between devices: 8.11 us -> 10.2 us  [run(): lax.all_to_all(outgoing, 'grp', split_axis=0, concat_axis=0, tiled=True)]
    cond x19 -> x29, local copies, waits for them, and re-layouts: 3.02 us -> 3.97 us
  transfers between devices with their start and end apart: 8 -> 8, of which waited for: 7 -> 6; matrix products, arithmetic and copies ran while one was open for 4% -> 3% of each run, Pallas kernels for 3% -> 3%
where the time goes in v5:
time: 160 us; the launch traced here: 159 us
  waiting for transfers between devices  73.9 us (46%)
  starting transfers between devices  56.6 us (35%)
  local copies, waits for them, and re-layouts  11.7 us (7%)
  Pallas kernels  10.1 us (6%)
  between operations  3.34 us (2%)
  other arithmetic  1.76 us (1%)
    ppermute x6, waiting for transfers between devices, exchange(): return lax.ppermute(block, axis, [(i, i ^ apart) for i in range(size)])  63.7 us
    ppermute x6, starting transfers between devices, exchange(): return lax.ppermute(block, axis, [(i, i ^ apart) for i in range(size)])  40.3 us
    all_to_all x1, waiting for transfers between devices, run(): lax.all_to_all(outgoing, 'grp', split_axis=0, concat_axis=0, tiled=True)  10.2 us
    all_to_all x1, starting transfers between devices, spread(): lax.all_to_all(copies, 'grp', split_axis=0, concat_axis=0, tiled=True)  8.6 us
    all_to_all x1, starting transfers between devices, run(): lax.all_to_all(outgoing, 'grp', split_axis=0, concat_axis=0, tiled=True)  7.7 us
    pallas_call x3, Pallas kernels, multiply(): pl.pallas_call(functools.partial(multiply_kernel, len(features)), grid_sp...  5.54 us
    cond x29, local copies, waits for them, and re-layouts  3.97 us
  transfers between devices with their start and end apart: 8, of which 6 were waited for; matrix products, arithmetic and copies ran while one was open for 3% of the time, Pallas kernels for 3%

profile of v5, /device:TPU:1, one launch (start us, length us, event | category | flops | bytes accessed | tf_op | source)
XLA Modules:
  0.0 158.8 jit_solution(4933214576232447429)
XLA Ops:
  0.7 1.4 copy.94.lengths
  2.1 0.7 constant_dynamic-slice_fusion
  2.8 0.6 pad_maximum_fusion.block_ref
  3.5 1.9 %pack.1.awaited_ref = bf16[656,640]{1,0:T(8,128)(2,1)S(1)} custom-call(s32[1]{0:T(128)} %bitcast.26.instance, s32[64,32]{1,0:T(8,128)} %copy.94.lengths, bf16[512,640]{1,0:T(8,128)(2,1)} %states.1, bf16[32,4,640]{2,1,0:T(4,128)(2,1)} %nexts.1, bf16[4,4,640]{2,1,0:T(4,128)(2,1)} %sequences.1), custom_call_target="tpu_custom_call" | custom-call | tf_op jit(solution)/shard_map/pack/pallas_call | solution.py:105
  5.4 9.6 %collective-permute-start.25 = (bf16[80,256]{1,0:T(8,128)(2,1)}, bf16[80,256]{1,0:T(8,128)(2,1)S(1)}, u32[]{:S(2)}, u32[]{:S(2)}) collective-permute-start(bf16[80,256]{1,0:T(8,128)(2,1)} %pass_on.11), channel_id=1, source_target_pairs={{0,4},{1,5},{2,6},{3,7},{4,0},{5,1},{6,2},{7,3},{8,12},{9,13},{10,... | collective-permute-start | bytes 122888 | tf_op jit(solution)/shard_map/ppermute | solution.py:22
  15.0 0.0 copy-done.57
  15.0 0.1 dynamic-slice_bitcast_fusion.5
  15.1 0.1 reduce-window.9
  15.2 0.6 reduce_max.9
  18.4 0.0 collective-permute-done.25
  18.4 0.0 copy-done.44
  18.4 0.0 copy-done.53
  18.5 0.0 copy-done.58
  18.5 140.3 %conditional.1 = (bf16[4,4,1024]{2,1,0:T(4,128)(2,1)}, bf16[1,64,4,1024]{3,2,1,0:T(4,128)(2,1)}) conditional(s32[]{:T(128)} %clamp.3, (s32[4]{0:T(128)S(1)}, bf16[656,640]{1,0:T(8,128)(2,1)S(1)}, bf16[5120,128]{1,0:T(8,128)(2,1)}, bf16[5120,128]{1,0:T(8,128)(2,1)}, bf16[80,256]{1,0:T(8,128)(2,1)S(1)}, ...), branch_computations={%region_3.6_spmd, %region_6.9_spmd, %region_9.12_spmd, %region_12.... | conditional | flops 11787123712 | bytes 91217600 | solution.py:393
  18.5 0.0 copy-start.32
  18.5 0.9 copy-done.32
  19.4 1.1 slice.53.refs_0_
  20.6 3.5 %collective-permute-start.5 = (bf16[496,640]{1,0:T(8,128)(2,1)S(1)}, bf16[496,640]{1,0:T(8,128)(2,1)S(1)}, u32[]{:S(2)}, u32[]{:S(2)}) collective-permute-start(bf16[496,640]{1,0:T(8,128)(2,1)S(1)} %slice.53.refs_0_), channel_id=1, source_target_pairs={{0,1},{1,0},{2,3},{3,2},{4,5},{5,4},{6,7},{7,6},{8,9},{9,8},{10,11... | collective-permute-start | bytes 1904648 | tf_op jit(solution)/shard_map/cond/branch_1_fun/ppermute | solution.py:22
  24.1 4.9 %collective-permute-start.6 = (bf16[496,640]{1,0:T(8,128)(2,1)S(1)}, bf16[496,640]{1,0:T(8,128)(2,1)S(1)}, u32[]{:S(2)}, u32[]{:S(2)}) collective-permute-start(bf16[496,640]{1,0:T(8,128)(2,1)S(1)} %slice.53.refs_0_), channel_id=1, source_target_pairs={{0,2},{1,3},{2,0},{3,1},{4,6},{5,7},{6,4},{7,5},{8,10},{9,11},{10,... | collective-permute-start | bytes 1904648 | tf_op jit(solution)/shard_map/cond/branch_1_fun/ppermute | solution.py:22
  29.0 1.2 broadcast_in_dim.74
  30.2 8.6 %all-to-all-start.2 = ((bf16[32,80,256]{2,1,0:T(8,128)(2,1)}), bf16[32,80,256]{2,1,0:T(8,128)(2,1)S(1)}, u32[]{:S(2)}, u32[]{:S(2)}) async-start(bf16[32,80,256]{2,1,0:T(8,128)(2,1)} %broadcast_in_dim.74), calls=%async_computation.2 | async-start | bytes 2621440 | tf_op jit(solution)/shard_map/cond/branch_1_fun/all_to_all | solution.py:189
  38.8 0.0 copy-start.66
  38.8 7.1 %collective-permute-done.5.awaited_ref.refs_1_ = bf16[496,640]{1,0:T(8,128)(2,1)S(1)} collective-permute-done((bf16[496,640]{1,0:T(8,128)(2,1)S(1)}, bf16[496,640]{1,0:T(8,128)(2,1)S(1)}, u32[]{:S(2)}, u32[]{:S(2)}) %collective-permute-start.5) | collective-permute-done | bytes 634912 | tf_op jit(solution)/shard_map/cond/branch_1_fun/ppermute | solution.py:22
  45.9 3.2 %collective-permute-done.6.block_ref = bf16[496,640]{1,0:T(8,128)(2,1)S(1)} collective-permute-done((bf16[496,640]{1,0:T(8,128)(2,1)S(1)}, bf16[496,640]{1,0:T(8,128)(2,1)S(1)}, u32[]{:S(2)}, u32[]{:S(2)}) %collective-permute-start.6) | collective-permute-done | bytes 634912 | tf_op jit(solution)/shard_map/cond/branch_1_fun/ppermute | solution.py:22
  49.0 0.0 copy-done.18
  49.0 0.8 copy-done.21
  49.9 8.1 %collective-permute-start.7 = (bf16[496,640]{1,0:T(8,128)(2,1)}, bf16[496,640]{1,0:T(8,128)(2,1)S(1)}, u32[]{:S(2)}, u32[]{:S(2)}) collective-permute-start(bf16[496,640]{1,0:T(8,128)(2,1)} %pass_on.7.refs_2_), channel_id=1, source_target_pairs={{0,1},{1,0},{2,3},{3,2},{4,5},{5,4},{6,7},{7,6},{8,9},{9,8},{10,11... | collective-permute-start | bytes 1904648 | tf_op jit(solution)/shard_map/cond/branch_1_fun/ppermute | solution.py:22
  58.0 0.0 copy-done.66
  58.0 0.6 slice.54.order
  58.6 0.6 slice.55.block_number
  59.2 0.1 reshape.478.query
  59.3 0.1 copy.99
  59.3 0.1 convert_reduce_fusion.2
  59.5 0.1 copy.98
  59.5 0.0 all-to-all-done.2
  59.6 1.1 copy-done.19
  60.6 1.1 copy-done.22
  61.7 1.7 %multiply.21.refs_2_ = f32[496,256]{1,0:T(8,128)S(1)} custom-call(s32[3]{0:T(128)S(1)} %bitcast.97, s32[3]{0:T(128)S(1)} %bitcast.96, bf16[496,640]{1,0:T(8,128)(2,1)S(1)} %slice.53.refs_0_, bf16[496,640]{1,0:T(8,128)(2,1)S(1)} %copy-done.19, bf16[496,640]{1,0:T(8,128)(2,1)S(1)} %copy-done.22, bf16[2560,256]{1,0:T(8,128)(2,1)S(1)} %bitcast.90, ...), custom_call_target="tpu_custom_call" | custom-call | flops 487587840 | bytes 2000000 | tf_op jit(solution)/shard_map/cond/branch_1_fun/multiply/pallas_call | solution.py:218
  63.5 0.0 copy-start.37
  63.5 6.0 %collective-permute-done.7.refs_3_.refs_0_ = bf16[496,640]{1,0:T(8,128)(2,1)S(1)} collective-permute-done((bf16[496,640]{1,0:T(8,128)(2,1)}, bf16[496,640]{1,0:T(8,128)(2,1)S(1)}, u32[]{:S(2)}, u32[]{:S(2)}) %collective-permute-start.7) | collective-permute-done | bytes 634912 | tf_op jit(solution)/shard_map/cond/branch_1_fun/ppermute | solution.py:22
  69.5 1.7 %multiply.22 = bf16[496,256]{1,0:T(8,128)(2,1)S(1)} custom-call(s32[1]{0:T(128)} %slice.54.order, s32[1]{0:T(128)} %slice.55.block_number, bf16[496,640]{1,0:T(8,128)(2,1)S(1)} %collective-permute-done.7.refs_3_.refs_0_, bf16[2560,256]{1,0:T(8,128)(2,1)S(1)} %bitcast.91, f32[496,256]{1,0:T(8,128)S(1)} %multiply.21.refs_2_), custom_call_target="tpu_custom_call" | custom-call | flops 162529280 | bytes 2000000 | tf_op jit(solution)/shard_map/cond/branch_1_fun/multiply/pallas_call | solution.py:218
  71.1 12.0 %collective-permute-start.8 = (bf16[496,256]{1,0:T(8,128)(2,1)S(1)}, bf16[496,256]{1,0:T(8,128)(2,1)S(1)}, u32[]{:S(2)}, u32[]{:S(2)}) collective-permute-start(bf16[496,256]{1,0:T(8,128)(2,1)S(1)} %multiply.22), channel_id=1, source_target_pairs={{0,4},{1,5},{2,6},{3,7},{4,0},{5,1},{6,2},{7,3},{8,12},{9,13},{10,... | collective-permute-start | bytes 761864 | tf_op jit(solution)/shard_map/cond/branch_1_fun/ppermute | solution.py:22
  83.2 0.2 convert_reduce_fusion.3
  83.4 0.0 copy-done.20
  83.4 0.0 copy-done.23
  83.4 0.0 copy-done.37
  83.4 0.0 copy-start.75
  83.4 2.1 %multiply.20.own_new.own = f32[496,256]{1,0:T(8,128)S(1)} custom-call(s32[4]{0:T(128)S(1)} %get-tuple-element.442.order, s32[4]{0:T(128)S(1)} %get-tuple-element.441.block_number, bf16[496,640]{1,0:T(8,128)(2,1)S(1)} %slice.53.refs_0_, bf16[496,640]{1,0:T(8,128)(2,1)S(1)} %copy-done.20, bf16[496,640]{1,0:T(8,128)(2,1)S(1)} %copy-done.23, ...), custom_call_target="tpu_custom_call" | custom-call | flops 650117120 | bytes 2000000 | tf_op jit(solution)/shard_map/cond/branch_1_fun/multiply/pallas_call | solution.py:218
  85.6 25.9 %collective-permute-done.8.got_new.got = bf16[496,256]{1,0:T(8,128)(2,1)S(1)} collective-permute-done((bf16[496,256]{1,0:T(8,128)(2,1)S(1)}, bf16[496,256]{1,0:T(8,128)(2,1)S(1)}, u32[]{:S(2)}, u32[]{:S(2)}) %collective-permute-start.8) | collective-permute-done | bytes 253984 | tf_op jit(solution)/shard_map/cond/branch_1_fun/ppermute | solution.py:22
  111.5 2.0 %prompt_attention.6 = bf16[128,1024]{1,0:T(8,128)(2,1)S(1)} custom-call(f32[496,256]{1,0:T(8,128)S(1)} %multiply.20.own_new.own, bf16[496,256]{1,0:T(8,128)(2,1)S(1)} %collective-permute-done.8.got_new.got, f32[1,128]{1,0:T(1,128)S(1)} %bitcast.117, s32[1,352]{1,0:T(1,128)S(1)} %reshape.477.owners, bf16[128,1024]{1,0:T(8,128)(2,1)S(1)} %reshape.478.query), custom_call_target="tpu_custom_call" | custom-call | flops 1000000000 | bytes 2000000 | tf_op jit(solution)/shard_map/cond/branch_1_fun/prompt_attention/pallas_call | solution.py:136
  113.5 0.0 copy-start.49
  113.5 0.0 copy-start.71
  113.5 2.1 %collective-permute-start.9 = (bf16[128,1024]{1,0:T(8,128)(2,1)S(1)}, bf16[128,1024]{1,0:T(8,128)(2,1)S(1)}, u32[]{:S(2)}, u32[]{:S(2)}) collective-permute-start(bf16[128,1024]{1,0:T(8,128)(2,1)S(1)} %prompt_attention.6), channel_id=1, source_target_pairs={{0,256},{256,0},{1,257},{257,1},{2,258},{258,2},{3,259},{259,3},{4... | collective-permute-start | bytes 786440 | tf_op jit(solution)/shard_map/cond/branch_1_fun/ppermute | solution.py:22
  115.6 0.1 iota_add_fusion.1
  115.7 0.1 add.202
  115.8 21.6 %collective-permute-done.9 = bf16[128,1024]{1,0:T(8,128)(2,1)S(1)} collective-permute-done((bf16[128,1024]{1,0:T(8,128)(2,1)S(1)}, bf16[128,1024]{1,0:T(8,128)(2,1)S(1)}, u32[]{:S(2)}, u32[]{:S(2)}) %collective-permute-start.9) | collective-permute-done | bytes 262176 | tf_op jit(solution)/shard_map/cond/branch_1_fun/ppermute | solution.py:22
  137.4 1.1 fusion.3
  138.5 7.7 %all-to-all-start.3 = ((bf16[32,8,1024]{2,1,0:T(8,128)(2,1)}), bf16[32,8,1024]{2,1,0:T(8,128)(2,1)S(1)}, u32[]{:S(2)}, u32[]{:S(2)}) async-start(bf16[32,8,1024]{2,1,0:T(8,128)(2,1)} %fusion.3), calls=%async_computation.3 | async-start | bytes 1048576 | tf_op jit(solution)/shard_map/cond/branch_1_fun/all_to_all | solution.py:368
  146.2 0.0 copy-done.49
  146.2 0.1 select_bitcast_fusion.1
  146.3 0.7 cached_attention.6
  147.0 0.6 reshape.476
  147.6 10.2 %all-to-all-done.3 = bf16[32,8,1024]{2,1,0:T(8,128)(2,1)S(1)} async-done(((bf16[32,8,1024]{2,1,0:T(8,128)(2,1)}), bf16[32,8,1024]{2,1,0:T(8,128)(2,1)S(1)}, u32[]{:S(2)}, u32[]{:S(2)}) %all-to-all-start.3) | async-done | bytes 524320 | tf_op jit(solution)/shard_map/cond/branch_1_fun/all_to_all | solution.py:368
  157.8 1.0 reshape.479
  (27 shorter events, 0.1 us)
Async XLA Ops:
  3.5 11.6 %copy-start.57 = (s32[64,32]{0,1:T(8,128)S(1)}, s32[64,32]{0,1:T(8,128)}, u32[]{:S(2)}) copy-start(s32[64,32]{0,1:T(8,128)} %param.23) | copy-start | bytes 24580
  3.5 15.0 %copy-start.44 = (bf16[32,4,1024]{2,1,0:T(4,128)(2,1)S(1)}, bf16[32,4,1024]{2,1,0:T(4,128)(2,1)}, u32[]{:S(2)}) copy-start(bf16[32,4,1024]{2,1,0:T(4,128)(2,1)} %param.25) | copy-start | bytes 786436
  3.5 15.0 %copy-start.53 = (s32[64,32,1]{0,2,1:T(1,128)S(1)}, s32[64,32,1]{0,2,1:T(1,128)}, u32[]{:S(2)}) copy-start(s32[64,32,1]{0,2,1:T(1,128)} %param.24) | copy-start | bytes 24580
  3.5 15.0 %copy-start.58 = (s32[4]{0:T(128)S(1)}, s32[4]{0:T(128)}, u32[]{:S(2)}) copy-start(s32[4]{0:T(128)} %param.33) | copy-start | bytes 52
  5.4 13.1 %collective-permute-start.25 = (bf16[80,256]{1,0:T(8,128)(2,1)}, bf16[80,256]{1,0:T(8,128)(2,1)S(1)}, u32[]{:S(2)}, u32[]{:S(2)}) collective-permute-start(bf16[80,256]{1,0:T(8,128)(2,1)} %pass_on.11), channel_id=1, source_target_pairs={{0,4},{1,5},{2,6},{3,7},{4,0},{5,1},{6,2},{7,3},{8,12},{9,13},{10,... | collective-permute-start | bytes 122888 | tf_op jit(solution)/shard_map/ppermute | solution.py:22
  18.5 0.9 copy-start.32
  19.4 1.1 copy-start.65
  20.6 25.3 %collective-permute-start.5 = (bf16[496,640]{1,0:T(8,128)(2,1)S(1)}, bf16[496,640]{1,0:T(8,128)(2,1)S(1)}, u32[]{:S(2)}, u32[]{:S(2)}) collective-permute-start(bf16[496,640]{1,0:T(8,128)(2,1)S(1)} %slice.53.refs_0_), channel_id=1, source_target_pairs={{0,1},{1,0},{2,3},{3,2},{4,5},{5,4},{6,7},{7,6},{8,9},{9,8},{10,11... | collective-permute-start | bytes 1904648 | tf_op jit(solution)/shard_map/cond/branch_1_fun/ppermute | solution.py:22
  24.1 24.9 %collective-permute-start.6 = (bf16[496,640]{1,0:T(8,128)(2,1)S(1)}, bf16[496,640]{1,0:T(8,128)(2,1)S(1)}, u32[]{:S(2)}, u32[]{:S(2)}) collective-permute-start(bf16[496,640]{1,0:T(8,128)(2,1)S(1)} %slice.53.refs_0_), channel_id=1, source_target_pairs={{0,2},{1,3},{2,0},{3,1},{4,6},{5,7},{6,4},{7,5},{8,10},{9,11},{10,... | collective-permute-start | bytes 1904648 | tf_op jit(solution)/shard_map/cond/branch_1_fun/ppermute | solution.py:22
  30.2 29.4 %all-to-all-start.2 = ((bf16[32,80,256]{2,1,0:T(8,128)(2,1)}), bf16[32,80,256]{2,1,0:T(8,128)(2,1)S(1)}, u32[]{:S(2)}, u32[]{:S(2)}) async-start(bf16[32,80,256]{2,1,0:T(8,128)(2,1)} %broadcast_in_dim.74), calls=%async_computation.2 | async-start | bytes 2621440 | tf_op jit(solution)/shard_map/cond/branch_1_fun/all_to_all | solution.py:189
  38.8 19.2 %copy-start.66 = (s32[4]{0:T(128)S(1)}, s32[4]{0:T(128)}, u32[]{:S(2)}) copy-start(s32[4]{0:T(128)} %copy-done.65) | copy-start | bytes 52 | tf_op jit(solution)/shard_map/cond
  45.9 3.2 %copy-start.18 = (bf16[496,640]{1,0:T(8,128)(2,1)}, bf16[496,640]{1,0:T(8,128)(2,1)S(1)}, u32[]{:S(2)}) copy-start(bf16[496,640]{1,0:T(8,128)(2,1)S(1)} %collective-permute-done.5.awaited_ref.refs_1_) | copy-start | bytes 1904644 | tf_op jit(solution)/shard_map/cond
  49.0 0.8 copy-start.21
  49.9 19.6 %collective-permute-start.7 = (bf16[496,640]{1,0:T(8,128)(2,1)}, bf16[496,640]{1,0:T(8,128)(2,1)S(1)}, u32[]{:S(2)}, u32[]{:S(2)}) collective-permute-start(bf16[496,640]{1,0:T(8,128)(2,1)} %pass_on.7.refs_2_), channel_id=1, source_target_pairs={{0,1},{1,0},{2,3},{3,2},{4,5},{5,4},{6,7},{7,6},{8,9},{9,8},{10,11... | collective-permute-start | bytes 1904648 | tf_op jit(solution)/shard_map/cond/branch_1_fun/ppermute | solution.py:22
  59.6 1.1 copy-start.19
  60.6 1.1 copy-start.22
  61.7 21.7 %copy-start.41 = (bf16[5120,128]{1,0:T(8,128)(2,1)S(1)}, bf16[5120,128]{1,0:T(8,128)(2,1)}, u32[]{:S(2)}) copy-start(bf16[5120,128]{1,0:T(8,128)(2,1)} %get-tuple-element.135.refs_5_) | copy-start | bytes 3932164 | tf_op jit(solution)/shard_map/cond
  63.5 19.9 %copy-start.20 = (bf16[496,640]{1,0:T(8,128)(2,1)S(1)}, bf16[496,640]{1,0:T(8,128)(2,1)}, u32[]{:S(2)}) copy-start(bf16[496,640]{1,0:T(8,128)(2,1)} %copy-done.18) | copy-start | bytes 1904644 | tf_op jit(solution)/shard_map/cond
  63.5 19.9 %copy-start.23 = (bf16[496,640]{1,0:T(8,128)(2,1)S(1)}, bf16[496,640]{1,0:T(8,128)(2,1)}, u32[]{:S(2)}) copy-start(bf16[496,640]{1,0:T(8,128)(2,1)} %pass_on.7.refs_2_) | copy-start | bytes 1904644 | tf_op jit(solution)/shard_map/cond
  63.5 19.9 %copy-start.37 = (bf16[5120,128]{1,0:T(8,128)(2,1)S(1)}, bf16[5120,128]{1,0:T(8,128)(2,1)}, u32[]{:S(2)}) copy-start(bf16[5120,128]{1,0:T(8,128)(2,1)} %get-tuple-element.134.refs_4_) | copy-start | bytes 3932164 | tf_op jit(solution)/shard_map/cond
  71.1 40.4 %collective-permute-start.8 = (bf16[496,256]{1,0:T(8,128)(2,1)S(1)}, bf16[496,256]{1,0:T(8,128)(2,1)S(1)}, u32[]{:S(2)}, u32[]{:S(2)}) collective-permute-start(bf16[496,256]{1,0:T(8,128)(2,1)S(1)} %multiply.22), channel_id=1, source_target_pairs={{0,4},{1,5},{2,6},{3,7},{4,0},{5,1},{6,2},{7,3},{8,12},{9,13},{10,... | collective-permute-start | bytes 761864 | tf_op jit(solution)/shard_map/cond/branch_1_fun/ppermute | solution.py:22
  83.4 28.1 %copy-start.75 = (f32[128]{0:T(128)S(1)}, f32[128]{0:T(128)}, u32[]{:S(2)}) copy-start(f32[128]{0:T(128)} %get-tuple-element.230) | copy-start | bytes 1540 | tf_op jit(solution)/shard_map/cond
  113.5 32.7 %copy-start.49 = (bf16[4,4,1024]{2,1,0:T(4,128)(2,1)S(1)}, bf16[4,4,1024]{2,1,0:T(4,128)(2,1)}, u32[]{:S(2)}) copy-start(bf16[4,4,1024]{2,1,0:T(4,128)(2,1)} %get-tuple-element.240) | copy-start | bytes 98308 | tf_op jit(solution)/shard_map/cond
  113.5 32.8 %copy-start.71 = (bf16[4,2,256,128]{3,2,1,0:T(8,128)(2,1)S(1)}, bf16[4,2,256,128]{3,2,1,0:T(8,128)(2,1)}, u32[]{:S(2)}) copy-start(bf16[4,2,256,128]{3,2,1,0:T(8,128)(2,1)} %get-tuple-element.245.cache) | copy-start | bytes 1572868 | tf_op jit(solution)/shard_map/cond
  113.5 23.9 %collective-permute-start.9 = (bf16[128,1024]{1,0:T(8,128)(2,1)S(1)}, bf16[128,1024]{1,0:T(8,128)(2,1)S(1)}, u32[]{:S(2)}, u32[]{:S(2)}) collective-permute-start(bf16[128,1024]{1,0:T(8,128)(2,1)S(1)} %prompt_attention.6), channel_id=1, source_target_pairs={{0,256},{256,0},{1,257},{257,1},{2,258},{258,2},{3,259},{259,3},{4... | collective-permute-start | bytes 786440 | tf_op jit(solution)/shard_map/cond/branch_1_fun/ppermute | solution.py:22
  138.5 19.3 %all-to-all-start.3 = ((bf16[32,8,1024]{2,1,0:T(8,128)(2,1)}), bf16[32,8,1024]{2,1,0:T(8,128)(2,1)S(1)}, u32[]{:S(2)}, u32[]{:S(2)}) async-start(bf16[32,8,1024]{2,1,0:T(8,128)(2,1)} %fusion.3), calls=%async_computation.3 | async-start | bytes 1048576 | tf_op jit(solution)/shard_map/cond/branch_1_fun/all_to_all | solution.py:368
